TPU v7x, 32 devices: a whole 2x2x4 slice. The times are simulated.
32 devices in a mesh: grp: 2 (over y), row: 16 (over z, x, core).
Axes of the slice: x: 2, y: 2, z: 4, core: 2. Of those that a mesh axis runs over, the one named last changes fastest.
Arguments:
- sensing: float32 [3072, 16384], P('row')
- measured: float32 [1536], P(('grp', 'row')), parts along dimension 0, may hold values from -6 to 6
- thresholds: float32 [12], P('grp'), parts along dimension 0, may hold values from 3 to 4
Outputs:
- estimate: float32 [131072], P(('grp', 'row')), parts along dimension 0
- residual: float32 [1536], P(('grp', 'row')), parts along dimension 0
There are 2 independent parts, one for each index of `grp`. A program takes and returns all parts, laid end to end along the dimension named above; an argument that names none is the same for every part. Nothing has to cross between parts.
All inputs are finite; a program needn't handle non-finite values.
Results may differ from a plain program's by a relative error of at most 0.0003.
Values sent between devices are 32-bit elements; how exact they have to be, the bound alone decides.
No kernel may reach another device: no remote copies, remote signals or barrier semaphores. Data moves between devices by JAX's collectives and lax.ppermute only.
A program may use at most 64 MiB of HBM per device.

v0:
```python
import jax
import jax.numpy as jnp
from jax import lax
from jax.sharding import PartitionSpec as P

COLS = 4
ITERS = 6


SOFTNESS = 0.25


def swapped(value, axis, distance):
    mask = 2**distance
    pairs = [(source, source ^ mask) for source in range(lax.axis_size(axis))]
    return lax.ppermute(value, axis, pairs)


def shrink(values, level):
    return SOFTNESS * (
        jax.nn.softplus((values - level) / SOFTNESS) - jax.nn.softplus((-values - level) / SOFTNESS)
    )


def slopes(values, level):
    return jax.nn.sigmoid((values - level) / SOFTNESS) + jax.nn.sigmoid(
        (-values - level) / SOFTNESS
    )


def gather_measured(piece, index, first_bit, count_bits):
    for offset in range(count_bits):
        position = first_bit + offset
        partner = swapped(piece, "row", position)
        upper = index >> position & 1 == 1
        piece = jnp.where(
            upper, jnp.concatenate([partner, piece]), jnp.concatenate([piece, partner])
        )
    return piece


def double_columns(vector, count_bits):
    for position in range(count_bits):
        vector = vector + swapped(vector, "row", position)
    return vector


def block_product(sensing, full_estimate, first_bit, count_bits):
    product = jnp.dot(
        sensing, full_estimate, precision=lax.Precision.HIGHEST, preferred_element_type=jnp.float32
    )
    for offset in range(count_bits):
        product = product + swapped(product, "row", first_bit + offset)
    return product


def total_slope(local_slope):
    return lax.psum(local_slope, "row")


def on_device(sensing, measured, thresholds):
    width = sensing.shape[1]
    local_rows = measured.shape[0]
    devices = lax.axis_size("row")
    groups = devices // COLS
    all_rows = local_rows * devices
    low_bits = groups.bit_length() - 1
    high_bits = COLS.bit_length() - 1
    index = lax.axis_index("row")
    group_pos = index % groups
    column_pos = index // groups
    share = width // groups
    measured_rows = gather_measured(measured, index, low_bits, high_bits)
    block_residual = measured_rows
    full_estimate = jnp.zeros((width,), jnp.float32)
    for step in range(ITERS):
        partial_sums = jnp.dot(
            block_residual,
            sensing,
            precision=lax.Precision.HIGHEST,
            preferred_element_type=jnp.float32,
        )
        pseudo = full_estimate + double_columns(partial_sums, low_bits)
        own_part = lax.dynamic_slice_in_dim(pseudo, group_pos * share, share)
        local_slope = jnp.sum(slopes(own_part, thresholds[step]))
        full_estimate = shrink(pseudo, thresholds[step])
        product = block_product(sensing, full_estimate, low_bits, high_bits)
        onsager = total_slope(local_slope) / all_rows
        block_residual = measured_rows - product + onsager * block_residual
    estimate = lax.dynamic_slice_in_dim(full_estimate, group_pos * share, share)
    residual = lax.dynamic_slice_in_dim(block_residual, column_pos * local_rows, local_rows)
    return (estimate, residual)


def solution(mesh):
    in_specs = (P("row", None), P(("grp", "row")), P("grp"))
    out_specs = (P(("grp", "row")), P(("grp", "row")))
    return jax.shard_map(
        on_device, mesh=mesh, in_specs=in_specs, out_specs=out_specs, check_vma=False
    )
```

profile of v0, /device:TPU:0, one launch (start us, length us, event | category | flops | bytes accessed | tf_op | source)
XLA Modules:
  0.0 398.7 jit_solution(8642005301162302000)
XLA Ops:
  0.6 3.1 collective-permute-start
  3.7 1.7 collective-permute-done
  6.2 3.0 collective-permute-start.1
  9.2 1.5 collective-permute-done.1
  10.8 8.9 %fusion.13 = f32[1,16384]{1,0:T(1,128)S(1)} fusion(f32[192,1]{0,1:T(1,128)S(1)} %bitcast.72, f32[192,16384]{1,0:T(8,128)} %param.3), kind=kOutput, calls=%fused_computation.44 | convolution fusion | flops 37748736 | bytes 12649216 | tf_op jit(solution)/shard_map/dot_general | solution.py:77
  19.8 1.2 collective-permute-done.2
  21.0 1.9 collective-permute-start.3
  23.6 1.8 collective-permute-done.3
  26.1 12.7 %fusion.14 = f32[1,192]{1,0:T(1,128)S(1)} fusion(f32[16384,1]{0,1:T(1,128)S(1)} %bitcast.58, f32[192,16384]{1,0:T(8,128)} %param.3), kind=kOutput, calls=%fused_computation.45 | convolution fusion | flops 37748736 | bytes 12649216 | tf_op jit(solution)/shard_map/dot_general | solution.py:49
  38.8 1.9 collective-permute-start.4
  40.8 1.7 collective-permute-done.4
  42.4 2.9 collective-permute-start.5
  45.4 1.3 add_reduce_fusion.5
  46.7 30.3 %psum.42 = f32[]{:T(128)} all-reduce(f32[]{:T(128)} %add_reduce_fusion.5), channel_id=1, replica_groups=mesh['grp'=2,'row'=16] {'row'}, use_global_device_ids=true, to_apply=%region_1.2 | all-reduce | flops 1 | bytes 8 | tf_op jit(solution)/shard_map/psum | solution.py:58
  77.6 8.9 %fusion.15 = f32[1,16384]{1,0:T(1,128)S(1)} fusion(f32[192,1]{0,1:T(1,128)S(1)} %bitcast.77, f32[192,16384]{1,0:T(8,128)} %param.3), kind=kOutput, calls=%fused_computation.46 | convolution fusion | flops 37748736 | bytes 12649216 | tf_op jit(solution)/shard_map/dot_general | solution.py:77
  86.6 1.2 collective-permute-done.6
  87.9 4.3 %collective-permute-done.7 = f32[16384]{0:T(1024)S(1)} collective-permute-done((f32[16384]{0:T(1024)S(1)}, f32[16384]{0:T(1024)S(1)}, u32[]{:S(2)}, u32[]{:S(2)}) %collective-permute-start.7) | collective-permute-done | bytes 65568 | tf_op jit(solution)/shard_map/ppermute | solution.py:16
  92.9 12.7 %fusion.16 = f32[1,192]{1,0:T(1,128)S(1)} fusion(f32[16384,1]{0,1:T(1,128)S(1)} %bitcast.55, f32[192,16384]{1,0:T(8,128)} %param.3), kind=kOutput, calls=%fused_computation.47 | convolution fusion | flops 37748736 | bytes 12649216 | tf_op jit(solution)/shard_map/dot_general | solution.py:49
  105.6 3.6 collective-permute-done.8
  110.4 30.4 %psum.43 = f32[]{:T(128)} all-reduce(f32[]{:T(128)} %add_reduce_fusion.4), channel_id=1, replica_groups=mesh['grp'=2,'row'=16] {'row'}, use_global_device_ids=true, to_apply=%region_3.4 | all-reduce | flops 1 | bytes 8 | tf_op jit(solution)/shard_map/psum | solution.py:58
  141.5 8.9 %fusion.17 = f32[1,16384]{1,0:T(1,128)S(1)} fusion(f32[192,1]{0,1:T(1,128)S(1)} %bitcast.74, f32[192,16384]{1,0:T(8,128)} %param.3), kind=kOutput, calls=%fused_computation.48 | convolution fusion | flops 37748736 | bytes 12649216 | tf_op jit(solution)/shard_map/dot_general | solution.py:77
  150.4 1.2 collective-permute-done.10
  151.8 4.3 %collective-permute-done.11 = f32[16384]{0:T(1024)S(1)} collective-permute-done((f32[16384]{0:T(1024)S(1)}, f32[16384]{0:T(1024)S(1)}, u32[]{:S(2)}, u32[]{:S(2)}) %collective-permute-start.11) | collective-permute-done | bytes 65568 | tf_op jit(solution)/shard_map/ppermute | solution.py:16
  156.8 12.7 %fusion.18 = f32[1,192]{1,0:T(1,128)S(1)} fusion(f32[16384,1]{0,1:T(1,128)S(1)} %bitcast.56, f32[192,16384]{1,0:T(8,128)} %param.3), kind=kOutput, calls=%fused_computation.49 | convolution fusion | flops 37748736 | bytes 12649216 | tf_op jit(solution)/shard_map/dot_general | solution.py:49
  169.6 3.6 collective-permute-done.12
  173.1 1.3 add_reduce_fusion.3
  174.4 30.6 %psum.44 = f32[]{:T(128)} all-reduce(f32[]{:T(128)} %add_reduce_fusion.3), channel_id=1, replica_groups=mesh['grp'=2,'row'=16] {'row'}, use_global_device_ids=true, to_apply=%region_5.6 | all-reduce | flops 1 | bytes 8 | tf_op jit(solution)/shard_map/psum | solution.py:58
  205.8 8.9 %fusion.19 = f32[1,16384]{1,0:T(1,128)S(1)} fusion(f32[192,1]{0,1:T(1,128)S(1)} %bitcast.75, f32[192,16384]{1,0:T(8,128)} %param.3), kind=kOutput, calls=%fused_computation.50 | convolution fusion | flops 37748736 | bytes 12649216 | tf_op jit(solution)/shard_map/dot_general | solution.py:77
  214.7 1.2 collective-permute-done.14
  216.0 4.3 %collective-permute-done.15 = f32[16384]{0:T(1024)S(1)} collective-permute-done((f32[16384]{0:T(1024)S(1)}, f32[16384]{0:T(1024)S(1)}, u32[]{:S(2)}, u32[]{:S(2)}) %collective-permute-start.15) | collective-permute-done | bytes 65568 | tf_op jit(solution)/shard_map/ppermute | solution.py:16
  221.1 12.7 %fusion.20 = f32[1,192]{1,0:T(1,128)S(1)} fusion(f32[16384,1]{0,1:T(1,128)S(1)} %bitcast.57, f32[192,16384]{1,0:T(8,128)} %param.3), kind=kOutput, calls=%fused_computation.51 | convolution fusion | flops 37748736 | bytes 12649216 | tf_op jit(solution)/shard_map/dot_general | solution.py:49
  233.8 3.6 collective-permute-done.16
  237.4 1.3 add_reduce_fusion.2
  238.7 30.3 %psum.45 = f32[]{:T(128)} all-reduce(f32[]{:T(128)} %add_reduce_fusion.2), channel_id=1, replica_groups=mesh['grp'=2,'row'=16] {'row'}, use_global_device_ids=true, to_apply=%region_7.8 | all-reduce | flops 1 | bytes 8 | tf_op jit(solution)/shard_map/psum | solution.py:58
  269.7 8.9 %fusion.21 = f32[1,16384]{1,0:T(1,128)S(1)} fusion(f32[192,1]{0,1:T(1,128)S(1)} %bitcast.76, f32[192,16384]{1,0:T(8,128)} %param.3), kind=kOutput, calls=%fused_computation.52 | convolution fusion | flops 37748736 | bytes 12649216 | tf_op jit(solution)/shard_map/dot_general | solution.py:77
  278.6 1.2 collective-permute-done.18
  280.0 4.3 %collective-permute-done.19 = f32[16384]{0:T(1024)S(1)} collective-permute-done((f32[16384]{0:T(1024)S(1)}, f32[16384]{0:T(1024)S(1)}, u32[]{:S(2)}, u32[]{:S(2)}) %collective-permute-start.19) | collective-permute-done | bytes 65568 | tf_op jit(solution)/shard_map/ppermute | solution.py:16
  284.9 12.7 %fusion.22 = f32[1,192]{1,0:T(1,128)S(1)} fusion(f32[16384,1]{0,1:T(1,128)S(1)} %bitcast.54, f32[192,16384]{1,0:T(8,128)} %param.3), kind=kOutput, calls=%fused_computation.53 | convolution fusion | flops 37748736 | bytes 12649216 | tf_op jit(solution)/shard_map/dot_general | solution.py:49
  297.7 3.6 collective-permute-done.20
  301.3 1.3 add_reduce_fusion.1
  302.5 30.4 %psum.46 = f32[]{:T(128)} all-reduce(f32[]{:T(128)} %add_reduce_fusion.1), channel_id=1, replica_groups=mesh['grp'=2,'row'=16] {'row'}, use_global_device_ids=true, to_apply=%region_9.10 | all-reduce | flops 1 | bytes 8 | tf_op jit(solution)/shard_map/psum | solution.py:58
  333.6 8.9 %fusion.23 = f32[1,16384]{1,0:T(1,128)S(1)} fusion(f32[192,1]{0,1:T(1,128)S(1)} %bitcast.73, f32[192,16384]{1,0:T(8,128)} %param.3), kind=kOutput, calls=%fused_computation.54 | convolution fusion | flops 37748736 | bytes 12649216 | tf_op jit(solution)/shard_map/dot_general | solution.py:77
  342.6 1.2 collective-permute-done.22
  343.9 4.3 %collective-permute-done.23 = f32[16384]{0:T(1024)S(1)} collective-permute-done((f32[16384]{0:T(1024)S(1)}, f32[16384]{0:T(1024)S(1)}, u32[]{:S(2)}, u32[]{:S(2)}) %collective-permute-start.23) | collective-permute-done | bytes 65568 | tf_op jit(solution)/shard_map/ppermute | solution.py:16
  348.9 12.7 %fusion.24 = f32[1,192]{1,0:T(1,128)S(1)} fusion(f32[16384,1]{0,1:T(1,128)S(1)} %bitcast.59, f32[192,16384]{1,0:T(8,128)} %param.3), kind=kOutput, calls=%fused_computation.55 | convolution fusion | flops 37748736 | bytes 12649216 | tf_op jit(solution)/shard_map/dot_general | solution.py:49
  361.7 3.5 collective-permute-done.24
  365.2 1.3 add_reduce_fusion
  366.5 30.2 %psum.47 = f32[]{:T(128)} all-reduce(f32[]{:T(128)} %add_reduce_fusion), channel_id=1, replica_groups=mesh['grp'=2,'row'=16] {'row'}, use_global_device_ids=true, to_apply=%region_11.12 | all-reduce | flops 1 | bytes 8 | tf_op jit(solution)/shard_map/psum | solution.py:58
  (59 shorter events, 9.4 us)
Async XLA Ops:
  0.6 22.3 %copy-start = (f32[6]{0:T(128)S(1)}, f32[6]{0:T(128)}, u32[]{:S(2)}) copy-start(f32[6]{0:T(128)} %param.5) | copy-start | bytes 76
  0.6 4.7 %collective-permute-start = (f32[48]{0:T(128)}, f32[48]{0:T(128)S(1)}, u32[]{:S(2)}, u32[]{:S(2)}) collective-permute-start(f32[48]{0:T(128)} %param.4), channel_id=1, source_target_pairs={{0,4},{1,5},{2,6},{3,7},{4,0},{5,1},{6,2},{7,3},{8,12},{9,13},{10,... | collective-permute-start | bytes 584 | tf_op jit(solution)/shard_map/ppermute | solution.py:16
  6.2 4.6 %collective-permute-start.1 = (f32[96]{0:T(128)S(1)}, f32[96]{0:T(128)S(1)}, u32[]{:S(2)}, u32[]{:S(2)}) collective-permute-start(f32[96]{0:T(128)S(1)} %broadcast_select_fusion), channel_id=1, source_target_pairs={{0,8},{1,9},{2,10},{3,11},{4,12},{5,13},{6,14},{7,15},{8,0},{9,1},... | collective-permute-start | bytes 1160 | tf_op jit(solution)/shard_map/ppermute | solution.py:16
  19.7 1.3 collective-permute-start.2
  21.0 4.3 %collective-permute-start.3 = (f32[16384]{0:T(1024)S(1)}, f32[16384]{0:T(1024)S(1)}, u32[]{:S(2)}, u32[]{:S(2)}) collective-permute-start(f32[16384]{0:T(1024)S(1)} %add.225), channel_id=1, source_target_pairs={{0,2},{1,3},{2,0},{3,1},{4,6},{5,7},{6,4},{7,5},{8,10},{9,11},{10,... | collective-permute-start | bytes 196616 | tf_op jit(solution)/shard_map/ppermute | solution.py:16
  38.8 3.6 collective-permute-start.4
  42.4 35.2 %collective-permute-start.5 = (f32[192]{0:T(256)S(1)}, f32[192]{0:T(256)S(1)}, u32[]{:S(2)}, u32[]{:S(2)}) collective-permute-start(f32[192]{0:T(256)S(1)} %add.229), channel_id=1, source_target_pairs={{0,8},{1,9},{2,10},{3,11},{4,12},{5,13},{6,14},{7,15},{8,0},{9,1},... | collective-permute-start | bytes 2312 | tf_op jit(solution)/shard_map/ppermute | solution.py:16
  86.5 1.3 collective-permute-start.6
  87.9 4.3 %collective-permute-start.7 = (f32[16384]{0:T(1024)S(1)}, f32[16384]{0:T(1024)S(1)}, u32[]{:S(2)}, u32[]{:S(2)}) collective-permute-start(f32[16384]{0:T(1024)S(1)} %add.237), channel_id=1, source_target_pairs={{0,2},{1,3},{2,0},{3,1},{4,6},{5,7},{6,4},{7,5},{8,10},{9,11},{10,... | collective-permute-start | bytes 196616 | tf_op jit(solution)/shard_map/ppermute | solution.py:16
  105.6 3.6 collective-permute-start.8
  109.2 32.3 %collective-permute-start.9 = (f32[192]{0:T(256)S(1)}, f32[192]{0:T(256)S(1)}, u32[]{:S(2)}, u32[]{:S(2)}) collective-permute-start(f32[192]{0:T(256)S(1)} %add.242), channel_id=1, source_target_pairs={{0,8},{1,9},{2,10},{3,11},{4,12},{5,13},{6,14},{7,15},{8,0},{9,1},... | collective-permute-start | bytes 2312 | tf_op jit(solution)/shard_map/ppermute | solution.py:16
  150.4 1.3 collective-permute-start.10
  151.7 4.3 %collective-permute-start.11 = (f32[16384]{0:T(1024)S(1)}, f32[16384]{0:T(1024)S(1)}, u32[]{:S(2)}, u32[]{:S(2)}) collective-permute-start(f32[16384]{0:T(1024)S(1)} %add.248), channel_id=1, source_target_pairs={{0,2},{1,3},{2,0},{3,1},{4,6},{5,7},{6,4},{7,5},{8,10},{9,11},{10,... | collective-permute-start | bytes 196616 | tf_op jit(solution)/shard_map/ppermute | solution.py:16
  169.5 3.6 collective-permute-start.12
  173.1 32.6 %collective-permute-start.13 = (f32[192]{0:T(256)S(1)}, f32[192]{0:T(256)S(1)}, u32[]{:S(2)}, u32[]{:S(2)}) collective-permute-start(f32[192]{0:T(256)S(1)} %add.253), channel_id=1, source_target_pairs={{0,8},{1,9},{2,10},{3,11},{4,12},{5,13},{6,14},{7,15},{8,0},{9,1},... | collective-permute-start | bytes 2312 | tf_op jit(solution)/shard_map/ppermute | solution.py:16
  214.7 1.3 collective-permute-start.14
  216.0 4.3 %collective-permute-start.15 = (f32[16384]{0:T(1024)S(1)}, f32[16384]{0:T(1024)S(1)}, u32[]{:S(2)}, u32[]{:S(2)}) collective-permute-start(f32[16384]{0:T(1024)S(1)} %add.259), channel_id=1, source_target_pairs={{0,2},{1,3},{2,0},{3,1},{4,6},{5,7},{6,4},{7,5},{8,10},{9,11},{10,... | collective-permute-start | bytes 196616 | tf_op jit(solution)/shard_map/ppermute | solution.py:16
  233.8 3.6 collective-permute-start.16
  237.4 32.3 %collective-permute-start.17 = (f32[192]{0:T(256)S(1)}, f32[192]{0:T(256)S(1)}, u32[]{:S(2)}, u32[]{:S(2)}) collective-permute-start(f32[192]{0:T(256)S(1)} %add.264), channel_id=1, source_target_pairs={{0,8},{1,9},{2,10},{3,11},{4,12},{5,13},{6,14},{7,15},{8,0},{9,1},... | collective-permute-start | bytes 2312 | tf_op jit(solution)/shard_map/ppermute | solution.py:16
  278.6 1.3 collective-permute-start.18
  279.9 4.3 %collective-permute-start.19 = (f32[16384]{0:T(1024)S(1)}, f32[16384]{0:T(1024)S(1)}, u32[]{:S(2)}, u32[]{:S(2)}) collective-permute-start(f32[16384]{0:T(1024)S(1)} %add.270), channel_id=1, source_target_pairs={{0,2},{1,3},{2,0},{3,1},{4,6},{5,7},{6,4},{7,5},{8,10},{9,11},{10,... | collective-permute-start | bytes 196616 | tf_op jit(solution)/shard_map/ppermute | solution.py:16
  297.7 3.6 collective-permute-start.20
  301.3 32.3 %collective-permute-start.21 = (f32[192]{0:T(256)S(1)}, f32[192]{0:T(256)S(1)}, u32[]{:S(2)}, u32[]{:S(2)}) collective-permute-start(f32[192]{0:T(256)S(1)} %add.275), channel_id=1, source_target_pairs={{0,8},{1,9},{2,10},{3,11},{4,12},{5,13},{6,14},{7,15},{8,0},{9,1},... | collective-permute-start | bytes 2312 | tf_op jit(solution)/shard_map/ppermute | solution.py:16
  342.5 1.3 collective-permute-start.22
  343.8 4.3 %collective-permute-start.23 = (f32[16384]{0:T(1024)S(1)}, f32[16384]{0:T(1024)S(1)}, u32[]{:S(2)}, u32[]{:S(2)}) collective-permute-start(f32[16384]{0:T(1024)S(1)} %add.281), channel_id=1, source_target_pairs={{0,2},{1,3},{2,0},{3,1},{4,6},{5,7},{6,4},{7,5},{8,10},{9,11},{10,... | collective-permute-start | bytes 196616 | tf_op jit(solution)/shard_map/ppermute | solution.py:16
  361.6 3.6 collective-permute-start.24
  365.2 32.7 %collective-permute-start.25 = (f32[192]{0:T(256)S(1)}, f32[192]{0:T(256)S(1)}, u32[]{:S(2)}, u32[]{:S(2)}) collective-permute-start(f32[192]{0:T(256)S(1)} %add.286), channel_id=1, source_target_pairs={{0,8},{1,9},{2,10},{3,11},{4,12},{5,13},{6,14},{7,15},{8,0},{9,1},... | collective-permute-start | bytes 2312 | tf_op jit(solution)/shard_map/ppermute | solution.py:16
where the time goes:
time: 406 us; the launch traced here: 399 us
  blocking collectives  182 us (45%)
  matrix products  130 us (32%)
  waiting for transfers between devices  53.1 us (13%)
  starting transfers between devices  13.8 us (3%)
  other arithmetic  13 us (3%)
  between operations  5.09 us (1%)
    psum x6, blocking collectives, total_slope(): return lax.psum(local_slope, 'row')  182 us
    dot_general x6, matrix products, block_product(): jnp.dot(sensing, full_estimate, precision=lax.Precision.HIGHEST, preferre...  76.3 us
    dot_general x6, matrix products, on_device(): jnp.dot(block_residual, sensing, precision=lax.Precision.HIGHEST, preferr...  53.4 us
    ppermute x26, waiting for transfers between devices, swapped(): return lax.ppermute(value, axis, pairs)  53.1 us
    ppermute x26, starting transfers between devices, swapped(): return lax.ppermute(value, axis, pairs)  13.8 us
  transfers between devices with their start and end apart: 26, of which 20 were waited for; matrix products, arithmetic and copies ran while one was open for 2% of the time, Pallas kernels for 0%

commit v1 on v0

v1 whole, which is shorter than its diff:
```python
import functools

import jax
import jax.numpy as jnp
from jax import lax
from jax.experimental import pallas as pl
from jax.experimental.pallas import tpu as pltpu
from jax.sharding import PartitionSpec as P

COLS = 4
ITERS = 6
SOFTNESS = 0.25
LANES = 128
UNROLL = 16
VMEM = pltpu.VMEM
LIMIT = 40 * 2**20
ATANH = (
    0.999999999783453,
    0.3333334145023831,
    0.1999927837517024,
    0.14311218617609153,
    0.10693692054721207,
    0.1220053340626646,
)


def swapped(value, mask):
    pairs = [(source, source ^ mask) for source in range(lax.axis_size("row"))]
    return lax.ppermute(value, "row", pairs)


def shrink_and_slope(values, level):
    scaled = jnp.abs(values) * (1.0 / SOFTNESS)
    scaled_level = level * (1.0 / SOFTNESS)
    gap = scaled - scaled_level
    upper = jnp.exp(-jnp.abs(gap))
    lower = jnp.exp(-(scaled + scaled_level))
    one, two = 1.0 + upper, 2.0 + upper
    inverse = 1.0 / (one * two)
    ratio = upper * (one * inverse)
    square = ratio * ratio
    series = ATANH[-1]
    for coefficient in ATANH[-2::-1]:
        series = series * square + coefficient
    upper_log = (ratio + ratio) * series
    lower_log = lower * (1.0 - lower * (0.5 - lower * (1.0 / 3.0)))
    size = SOFTNESS * (jnp.maximum(gap, 0.0) + (upper_log - lower_log))
    estimate = jnp.where(values < 0.0, -size, jnp.where(values > 0.0, size, 0.0))
    slope = jnp.where(gap >= 0.0, 1.0, upper) * (two * inverse) + lower * (1.0 - lower * (1.0 - lower))
    return estimate, slope


def load_kernel(source, target, semaphore):
    copy = pltpu.make_async_copy(source, target, semaphore)
    copy.start()
    copy.wait()


def back_kernel(first, rows, all_rows, *refs):
    if first:
        *parts, sensing, out, residual_out = refs
    else:
        *parts, measured, old, sensing, out, residual_out = refs
    total = parts[0][...]
    for part in parts[1:]:
        total = total + part[...]
    if first:
        residual = total
    else:
        onsager = total[:, rows : rows + 1] / all_rows
        residual = measured[...] - total + onsager * old[...]
    residual_out[...] = residual
    columns = jnp.broadcast_to(residual, (LANES, residual.shape[1])).T

    def step(group, carry):
        start = pl.multiple_of(group * UNROLL * LANES, UNROLL * LANES)
        sums = [jnp.zeros((8, LANES), jnp.float32)] * UNROLL
        for at in range(0, rows, 8):
            block = sensing[pl.ds(at, 8), pl.ds(start, UNROLL * LANES)]
            for tile in range(UNROLL):
                sums[tile] += block[:, tile * LANES : (tile + 1) * LANES] * columns[at : at + 8]
        out[pl.ds(pl.multiple_of(group * UNROLL, UNROLL), UNROLL), :] = jnp.concatenate(
            [jnp.sum(total, axis=0, keepdims=True) for total in sums]
        )
        return carry

    lax.fori_loop(0, out.shape[0] // UNROLL, step, 0)


def forward_kernel(first, rows, step_at, *refs):
    if first:
        thresholds, partial, other, sensing, estimate_out, out = refs
        pseudo = partial[...] + other[...]
    else:
        thresholds, partial, other, old, sensing, estimate_out, out = refs
        pseudo = old[...] + (partial[...] + other[...])
    estimate, slopes = shrink_and_slope(pseudo, thresholds[step_at])
    estimate_out[...] = estimate
    slope = jnp.sum(slopes, keepdims=True)

    def step(group, totals):
        start = pl.multiple_of(group * UNROLL * LANES, UNROLL * LANES)
        values = estimate_out[pl.ds(pl.multiple_of(group * UNROLL, UNROLL), UNROLL), :]
        spread = [jnp.broadcast_to(values[tile : tile + 1], (8, LANES)) for tile in range(UNROLL)]
        totals = list(totals)
        for at in range(0, rows, 8):
            block = sensing[pl.ds(at, 8), pl.ds(start, UNROLL * LANES)]
            for tile in range(UNROLL):
                totals[at // 8] += block[:, tile * LANES : (tile + 1) * LANES] * spread[tile]
        return tuple(totals)

    nothing = tuple(jnp.zeros((8, LANES), jnp.float32) for _ in range(rows // 8))
    totals = lax.fori_loop(0, estimate_out.shape[0] // UNROLL, step, nothing)
    total = jnp.concatenate(totals)
    padded = out.shape[1]
    total = jnp.concatenate([total, jnp.zeros((padded - rows, LANES), jnp.float32)])
    product = jnp.sum(total.T, axis=0, keepdims=True)
    place = lax.broadcasted_iota(jnp.int32, product.shape, 1)
    out[...] = jnp.where(place == rows, slope, product)


def on_device(sensing, measured, thresholds):
    rows, width = sensing.shape
    local_rows = measured.shape[0]
    devices = lax.axis_size("row")
    groups = devices // COLS
    all_rows = local_rows * devices
    low_bits = groups.bit_length() - 1
    index = lax.axis_index("row")
    group_pos = index % groups
    column_pos = index // groups
    share = width // groups
    padded = (rows + LANES) // LANES * LANES
    tiles = width // LANES
    params = pltpu.CompilerParams(vmem_limit_bytes=LIMIT)
    in_vmem = pl.BlockSpec(memory_space=VMEM)
    in_smem = pl.BlockSpec(memory_space=pltpu.SMEM)
    matrix = pl.pallas_call(
        load_kernel,
        out_shape=VMEM(sensing.shape, sensing.dtype),
        in_specs=[pl.BlockSpec(memory_space=pl.ANY)],
        out_specs=in_vmem,
        scratch_shapes=[pltpu.SemaphoreType.DMA(())],
        compiler_params=params,
        cost_estimate=pl.CostEstimate(
            flops=0, bytes_accessed=2 * sensing.size * 4, transcendentals=0
        ),
        name="load",
    )(sensing)
    matrix = pltpu.with_memory_space_constraint(matrix, VMEM)
    row = jax.ShapeDtypeStruct((1, padded), jnp.float32)
    signal = jax.ShapeDtypeStruct((tiles, LANES), jnp.float32)

    def back(first, parts, *others):
        return pl.pallas_call(
            functools.partial(back_kernel, first, rows, all_rows),
            out_shape=(signal, row),
            in_specs=[in_vmem] * (len(parts) + len(others) + 1),
            out_specs=(in_vmem, in_vmem),
            compiler_params=params,
            name="back",
        )(*parts, *others, matrix)

    def forward(first, step, *others):
        return pl.pallas_call(
            functools.partial(forward_kernel, first, rows, step),
            out_shape=(signal, row),
            in_specs=[in_smem] + [in_vmem] * (len(others) + 1),
            out_specs=(in_vmem, in_vmem),
            compiler_params=params,
            name="forward",
        )(thresholds, *others, matrix)

    def all_columns(piece):
        flat = piece.reshape(padded)
        return [piece] + [
            swapped(flat, groups * mask).reshape(1, padded) for mask in range(1, COLS)
        ]

    own = lax.dynamic_update_slice(
        jnp.zeros((padded,), jnp.float32), measured, (column_pos * local_rows,)
    ).reshape(1, padded)
    parts = all_columns(own)
    others = ()
    estimate = ()
    for step in range(ITERS):
        partial, residual = back(step == 0, parts, *others)
        if step == 0:
            measured_row = residual
        others = (measured_row, residual)
        flat = partial.reshape(width)
        for position in range(low_bits - 1):
            flat = flat + swapped(flat, 2**position)
        other = swapped(flat, 2 ** (low_bits - 1))
        shaped = (tiles, LANES)
        new_estimate, product = forward(
            step == 0, step, flat.reshape(shaped), other.reshape(shaped), *estimate
        )
        estimate = (new_estimate,)
        parts = all_columns(product)
    total = sum(parts[1:], parts[0])[0]
    onsager = total[rows] / all_rows
    final = measured_row[0] - total + onsager * others[1][0]
    estimate = lax.dynamic_slice_in_dim(estimate[0].reshape(width), group_pos * share, share)
    residual = lax.dynamic_slice_in_dim(final, column_pos * local_rows, local_rows)
    return (estimate, residual)


def solution(mesh):
    in_specs = (P("row", None), P(("grp", "row")), P("grp"))
    out_specs = (P(("grp", "row")), P(("grp", "row")))
    return jax.shard_map(
        on_device, mesh=mesh, in_specs=in_specs, out_specs=out_specs, check_vma=False
    )
```

time: 406 us -> 107 us (0.26); the launches traced: 399 us -> 106 us
  blocking collectives: 182 us -> 0 us
  matrix products: 130 us -> 0 us
  starting transfers between devices: 13.8 us -> 42.3 us
  Pallas kernels: 0 us -> 22.8 us
  waiting for transfers between devices: 53.1 us -> 37.1 us
  other arithmetic: 13 us -> 0.66 us
    psum x6 -> x0, blocking collectives: 182 us -> none  [total_slope(): return lax.psum(local_slope, 'row')]
    dot_general x12 -> x0, matrix products: 130 us -> none  [the longest x6 76.3 us: block_product(): jnp.dot(sensing, full_estimate, precision=lax.Precision.HIGHEST, preferre...]
    ppermute x26 -> x33, starting transfers between devices: 13.8 us -> 42.3 us  [swapped(): return lax.ppermute(value, 'row', pairs)]
    pallas_call x0 -> x13, Pallas kernels: none -> 22.8 us  [the longest x6 11.2 us: forward(): pl.pallas_call(functools.partial(forward_kernel, first, rows, step), out_...]
    ppermute x26 -> x33, waiting for transfers between devices: 53.1 us -> 37.1 us  [swapped(): return lax.ppermute(value, 'row', pairs)]
    reduce_sum x6 -> x0, other arithmetic: 7.58 us -> none  [on_device(): local_slope = jnp.sum(slopes(own_part, thresholds[step]))]
    mul x6 -> x0, other arithmetic: 4.39 us -> none  [shrink(): SOFTNESS * (jax.nn.softplus((values - level) / SOFTNESS) - jax.nn.softplu...]
  transfers between devices with their start and end apart: 26 -> 33, of which waited for: 20 -> 24; matrix products, arithmetic and copies ran while one was open for 2% -> 1% of each run, Pallas kernels for 0% -> 4%
where the time goes in v1:
time: 107 us; the launch traced here: 106 us
  starting transfers between devices  42.3 us (40%)
  waiting for transfers between devices  37.1 us (35%)
  Pallas kernels  22.8 us (21%)
  local copies, waits for them, and re-layouts  2.06 us (2%)
  between operations  1.5 us (1%)
    ppermute x33, starting transfers between devices, swapped(): return lax.ppermute(value, 'row', pairs)  42.3 us
    ppermute x33, waiting for transfers between devices, swapped(): return lax.ppermute(value, 'row', pairs)  37.1 us
    pallas_call x6, Pallas kernels, forward(): pl.pallas_call(functools.partial(forward_kernel, first, rows, step), out_...  11.2 us
    pallas_call x6, Pallas kernels, back(): pl.pallas_call(functools.partial(back_kernel, first, rows, all_rows), out...  7.04 us
    pallas_call x1, Pallas kernels, on_device(): pl.pallas_call(load_kernel, out_shape=VMEM(sensing.shape, sensing.dtype),...  4.58 us
  transfers between devices with their start and end apart: 33, of which 24 were waited for; matrix products, arithmetic and copies ran while one was open for 1% of the time, Pallas kernels for 4%

profile of v1, /device:TPU:0, one launch (start us, length us, event | category | flops | bytes accessed | tf_op | source)
XLA Modules:
  0.0 106.5 jit_solution(11411035359435194092)
XLA Ops:
  1.5 5.1 %collective-permute-start.2 = (f32[256]{0:T(256)S(1)}, f32[256]{0:T(256)S(1)}, u32[]{:S(2)}, u32[]{:S(2)}) collective-permute-start(f32[256]{0:T(256)S(1)} %dynamic_update_slice.3), channel_id=1, source_target_pairs={{0,12},{1,13},{2,14},{3,15},{4,8},{5,9},{6,10},{7,11},{8,4},{9,5},... | collective-permute-start | bytes 3080 | tf_op jit(solution)/shard_map/ppermute | solution.py:29
  7.2 4.6 %load.1.refs_4_.refs_3_.refs_6_ = f32[192,16384]{1,0:T(8,128)S(1)} custom-call(f32[192,16384]{1,0:T(8,128)} %source.1), custom_call_target="tpu_custom_call" | custom-call | bytes 25165824 | tf_op jit(solution)/shard_map/load/pallas_call | solution.py:138
  11.9 1.1 back.6
  13.0 1.2 %collective-permute-done.3 = f32[16384]{0:T(1024)S(1)} collective-permute-done((f32[16384]{0:T(1024)S(1)}, f32[16384]{0:T(1024)S(1)}, u32[]{:S(2)}, u32[]{:S(2)}) %collective-permute-start.3) | collective-permute-done | bytes 65568 | tf_op jit(solution)/shard_map/ppermute | solution.py:29
  14.3 1.7 %collective-permute-start.4 = (f32[16384]{0:T(1024)S(1)}, f32[16384]{0:T(1024)S(1)}, u32[]{:S(2)}, u32[]{:S(2)}) collective-permute-start(f32[16384]{0:T(1024)S(1)} %bitcast_add_fusion.5), channel_id=1, source_target_pairs={{0,2},{1,3},{2,0},{3,1},{4,6},{5,7},{6,4},{7,5},{8,10},{9,11},{10,... | collective-permute-start | bytes 196616 | tf_op jit(solution)/shard_map/ppermute | solution.py:29
  16.0 2.6 %collective-permute-done.4 = f32[16384]{0:T(1024)S(1)} collective-permute-done((f32[16384]{0:T(1024)S(1)}, f32[16384]{0:T(1024)S(1)}, u32[]{:S(2)}, u32[]{:S(2)}) %collective-permute-start.4) | collective-permute-done | bytes 65568 | tf_op jit(solution)/shard_map/ppermute | solution.py:29
  18.6 1.8 %forward.6 = (f32[128,128]{1,0:T(8,128)S(1)}, f32[1,256]{1,0:T(1,128)S(1)}) custom-call(f32[6]{0:T(128)S(1)} %copy-done, f32[128,128]{1,0:T(8,128)S(1)} %bitcast.61, f32[128,128]{1,0:T(8,128)S(1)} %bitcast.67, f32[192,16384]{1,0:T(8,128)S(1)} %load.1.refs_4_.refs_3_.refs_6_), custom_call_target="tpu_custom_call" | custom-call | tf_op jit(solution)/shard_map/forward/pallas_call | solution.py:165
  20.4 3.8 %collective-permute-start.7 = (f32[256]{0:T(256)S(1)}, f32[256]{0:T(256)S(1)}, u32[]{:S(2)}, u32[]{:S(2)}) collective-permute-start(f32[256]{0:T(256)S(1)} %bitcast.87), channel_id=1, source_target_pairs={{0,12},{1,13},{2,14},{3,15},{4,8},{5,9},{6,10},{7,11},{8,4},{9,5},... | collective-permute-start | bytes 3080 | tf_op jit(solution)/shard_map/ppermute | solution.py:29
  24.9 1.0 collective-permute-done.7
  25.9 2.8 %collective-permute-done.6 = f32[256]{0:T(256)S(1)} collective-permute-done((f32[256]{0:T(256)S(1)}, f32[256]{0:T(256)S(1)}, u32[]{:S(2)}, u32[]{:S(2)}) %collective-permute-start.6) | collective-permute-done | bytes 1056 | tf_op jit(solution)/shard_map/ppermute | solution.py:29
  28.7 1.2 %back.7 = (f32[128,128]{1,0:T(8,128)S(1)}, f32[1,256]{1,0:T(1,128)S(1)}) custom-call(f32[1,256]{1,0:T(1,128)S(1)} %get-tuple-element.27.refs_0_, f32[1,256]{1,0:T(1,128)S(1)} %bitcast.107, f32[1,256]{1,0:T(1,128)S(1)} %bitcast.101, f32[1,256]{1,0:T(1,128)S(1)} %bitcast.95, f32[1,256]{1,0:T(1,128)S(1)} %get-tuple-element.28.refs_4_.refs_5_, ...), custom_call_target="tpu_custom_call" | custom-call | tf_op jit(solution)/shard_map/back/pallas_call | solution.py:155
  30.0 1.2 %collective-permute-done.8 = f32[16384]{0:T(1024)S(1)} collective-permute-done((f32[16384]{0:T(1024)S(1)}, f32[16384]{0:T(1024)S(1)}, u32[]{:S(2)}, u32[]{:S(2)}) %collective-permute-start.8) | collective-permute-done | bytes 65568 | tf_op jit(solution)/shard_map/ppermute | solution.py:29
  31.3 1.6 %collective-permute-start.9 = (f32[16384]{0:T(1024)S(1)}, f32[16384]{0:T(1024)S(1)}, u32[]{:S(2)}, u32[]{:S(2)}) collective-permute-start(f32[16384]{0:T(1024)S(1)} %bitcast_add_fusion.4), channel_id=1, source_target_pairs={{0,2},{1,3},{2,0},{3,1},{4,6},{5,7},{6,4},{7,5},{8,10},{9,11},{10,... | collective-permute-start | bytes 196616 | tf_op jit(solution)/shard_map/ppermute | solution.py:29
  32.8 2.8 %collective-permute-done.9 = f32[16384]{0:T(1024)S(1)} collective-permute-done((f32[16384]{0:T(1024)S(1)}, f32[16384]{0:T(1024)S(1)}, u32[]{:S(2)}, u32[]{:S(2)}) %collective-permute-start.9) | collective-permute-done | bytes 65568 | tf_op jit(solution)/shard_map/ppermute | solution.py:29
  35.6 1.9 %forward.7 = (f32[128,128]{1,0:T(8,128)S(1)}, f32[1,256]{1,0:T(1,128)S(1)}) custom-call(f32[6]{0:T(128)S(1)} %copy-done, f32[128,128]{1,0:T(8,128)S(1)} %bitcast.57, f32[128,128]{1,0:T(8,128)S(1)} %bitcast.63, f32[128,128]{1,0:T(8,128)S(1)} %get-tuple-element.30.refs_3_, f32[192,16384]{1,0:T(8,128)S(1)} %load.1.refs_4_.refs_3_.refs_6_), custom_call_target="tpu_custom_call" | custom-call | tf_op jit(solution)/shard_map/forward/pallas_call | solution.py:165
  37.5 1.5 %collective-permute-start.12 = (f32[256]{0:T(256)S(1)}, f32[256]{0:T(256)S(1)}, u32[]{:S(2)}, u32[]{:S(2)}) collective-permute-start(f32[256]{0:T(256)S(1)} %bitcast.75), channel_id=1, source_target_pairs={{0,12},{1,13},{2,14},{3,15},{4,8},{5,9},{6,10},{7,11},{8,4},{9,5},... | collective-permute-start | bytes 3080 | tf_op jit(solution)/shard_map/ppermute | solution.py:29
  39.6 2.3 %collective-permute-start.10 = (f32[256]{0:T(256)S(1)}, f32[256]{0:T(256)S(1)}, u32[]{:S(2)}, u32[]{:S(2)}) collective-permute-start(f32[256]{0:T(256)S(1)} %bitcast.77), channel_id=1, source_target_pairs={{0,4},{1,5},{2,6},{3,7},{4,0},{5,1},{6,2},{7,3},{8,12},{9,13},{10,... | collective-permute-start | bytes 3080 | tf_op jit(solution)/shard_map/ppermute | solution.py:29
  41.9 1.0 collective-permute-done.12
  43.5 1.2 %back.8 = (f32[128,128]{1,0:T(8,128)S(1)}, f32[1,256]{1,0:T(1,128)S(1)}) custom-call(f32[1,256]{1,0:T(1,128)S(1)} %get-tuple-element.31.refs_0_, f32[1,256]{1,0:T(1,128)S(1)} %bitcast.102, f32[1,256]{1,0:T(1,128)S(1)} %bitcast.96, f32[1,256]{1,0:T(1,128)S(1)} %bitcast.90, f32[1,256]{1,0:T(1,128)S(1)} %get-tuple-element.28.refs_4_.refs_5_, ...), custom_call_target="tpu_custom_call" | custom-call | tf_op jit(solution)/shard_map/back/pallas_call | solution.py:155
  44.7 1.2 %collective-permute-done.13 = f32[16384]{0:T(1024)S(1)} collective-permute-done((f32[16384]{0:T(1024)S(1)}, f32[16384]{0:T(1024)S(1)}, u32[]{:S(2)}, u32[]{:S(2)}) %collective-permute-start.13) | collective-permute-done | bytes 65568 | tf_op jit(solution)/shard_map/ppermute | solution.py:29
  46.0 1.6 %collective-permute-start.14 = (f32[16384]{0:T(1024)S(1)}, f32[16384]{0:T(1024)S(1)}, u32[]{:S(2)}, u32[]{:S(2)}) collective-permute-start(f32[16384]{0:T(1024)S(1)} %bitcast_add_fusion.3), channel_id=1, source_target_pairs={{0,2},{1,3},{2,0},{3,1},{4,6},{5,7},{6,4},{7,5},{8,10},{9,11},{10,... | collective-permute-start | bytes 196616 | tf_op jit(solution)/shard_map/ppermute | solution.py:29
  47.6 2.8 %collective-permute-done.14 = f32[16384]{0:T(1024)S(1)} collective-permute-done((f32[16384]{0:T(1024)S(1)}, f32[16384]{0:T(1024)S(1)}, u32[]{:S(2)}, u32[]{:S(2)}) %collective-permute-start.14) | collective-permute-done | bytes 65568 | tf_op jit(solution)/shard_map/ppermute | solution.py:29
  50.3 1.9 %forward.8 = (f32[128,128]{1,0:T(8,128)S(1)}, f32[1,256]{1,0:T(1,128)S(1)}) custom-call(f32[6]{0:T(128)S(1)} %copy-done, f32[128,128]{1,0:T(8,128)S(1)} %bitcast.58, f32[128,128]{1,0:T(8,128)S(1)} %bitcast.64, f32[128,128]{1,0:T(8,128)S(1)} %get-tuple-element.34.refs_3_, f32[192,16384]{1,0:T(8,128)S(1)} %load.1.refs_4_.refs_3_.refs_6_), custom_call_target="tpu_custom_call" | custom-call | tf_op jit(solution)/shard_map/forward/pallas_call | solution.py:165
  52.2 2.6 %collective-permute-start.17 = (f32[256]{0:T(256)S(1)}, f32[256]{0:T(256)S(1)}, u32[]{:S(2)}, u32[]{:S(2)}) collective-permute-start(f32[256]{0:T(256)S(1)} %bitcast.78), channel_id=1, source_target_pairs={{0,12},{1,13},{2,14},{3,15},{4,8},{5,9},{6,10},{7,11},{8,4},{9,5},... | collective-permute-start | bytes 3080 | tf_op jit(solution)/shard_map/ppermute | solution.py:29
  56.6 1.0 collective-permute-done.17
  57.6 1.7 %collective-permute-done.16 = f32[256]{0:T(256)S(1)} collective-permute-done((f32[256]{0:T(256)S(1)}, f32[256]{0:T(256)S(1)}, u32[]{:S(2)}, u32[]{:S(2)}) %collective-permute-start.16) | collective-permute-done | bytes 1056 | tf_op jit(solution)/shard_map/ppermute | solution.py:29
  59.3 1.2 %back.9 = (f32[128,128]{1,0:T(8,128)S(1)}, f32[1,256]{1,0:T(1,128)S(1)}) custom-call(f32[1,256]{1,0:T(1,128)S(1)} %get-tuple-element.35.refs_0_, f32[1,256]{1,0:T(1,128)S(1)} %bitcast.103, f32[1,256]{1,0:T(1,128)S(1)} %bitcast.97, f32[1,256]{1,0:T(1,128)S(1)} %bitcast.91, f32[1,256]{1,0:T(1,128)S(1)} %get-tuple-element.28.refs_4_.refs_5_, ...), custom_call_target="tpu_custom_call" | custom-call | tf_op jit(solution)/shard_map/back/pallas_call | solution.py:155
  60.6 1.2 %collective-permute-done.18 = f32[16384]{0:T(1024)S(1)} collective-permute-done((f32[16384]{0:T(1024)S(1)}, f32[16384]{0:T(1024)S(1)}, u32[]{:S(2)}, u32[]{:S(2)}) %collective-permute-start.18) | collective-permute-done | bytes 65568 | tf_op jit(solution)/shard_map/ppermute | solution.py:29
  61.8 1.6 %collective-permute-start.19 = (f32[16384]{0:T(1024)S(1)}, f32[16384]{0:T(1024)S(1)}, u32[]{:S(2)}, u32[]{:S(2)}) collective-permute-start(f32[16384]{0:T(1024)S(1)} %bitcast_add_fusion.2), channel_id=1, source_target_pairs={{0,2},{1,3},{2,0},{3,1},{4,6},{5,7},{6,4},{7,5},{8,10},{9,11},{10,... | collective-permute-start | bytes 196616 | tf_op jit(solution)/shard_map/ppermute | solution.py:29
  63.4 2.8 %collective-permute-done.19 = f32[16384]{0:T(1024)S(1)} collective-permute-done((f32[16384]{0:T(1024)S(1)}, f32[16384]{0:T(1024)S(1)}, u32[]{:S(2)}, u32[]{:S(2)}) %collective-permute-start.19) | collective-permute-done | bytes 65568 | tf_op jit(solution)/shard_map/ppermute | solution.py:29
  66.2 1.9 %forward.9 = (f32[128,128]{1,0:T(8,128)S(1)}, f32[1,256]{1,0:T(1,128)S(1)}) custom-call(f32[6]{0:T(128)S(1)} %copy-done, f32[128,128]{1,0:T(8,128)S(1)} %bitcast.59, f32[128,128]{1,0:T(8,128)S(1)} %bitcast.65, f32[128,128]{1,0:T(8,128)S(1)} %get-tuple-element.38.refs_3_, f32[192,16384]{1,0:T(8,128)S(1)} %load.1.refs_4_.refs_3_.refs_6_), custom_call_target="tpu_custom_call" | custom-call | tf_op jit(solution)/shard_map/forward/pallas_call | solution.py:165
  68.1 1.5 %collective-permute-start.22 = (f32[256]{0:T(256)S(1)}, f32[256]{0:T(256)S(1)}, u32[]{:S(2)}, u32[]{:S(2)}) collective-permute-start(f32[256]{0:T(256)S(1)} %bitcast.81), channel_id=1, source_target_pairs={{0,12},{1,13},{2,14},{3,15},{4,8},{5,9},{6,10},{7,11},{8,4},{9,5},... | collective-permute-start | bytes 3080 | tf_op jit(solution)/shard_map/ppermute | solution.py:29
  70.5 2.0 %collective-permute-start.20 = (f32[256]{0:T(256)S(1)}, f32[256]{0:T(256)S(1)}, u32[]{:S(2)}, u32[]{:S(2)}) collective-permute-start(f32[256]{0:T(256)S(1)} %bitcast.83), channel_id=1, source_target_pairs={{0,4},{1,5},{2,6},{3,7},{4,0},{5,1},{6,2},{7,3},{8,12},{9,13},{10,... | collective-permute-start | bytes 3080 | tf_op jit(solution)/shard_map/ppermute | solution.py:29
  72.5 1.0 collective-permute-done.22
  74.1 1.2 %back.10 = (f32[128,128]{1,0:T(8,128)S(1)}, f32[1,256]{1,0:T(1,128)S(1)}) custom-call(f32[1,256]{1,0:T(1,128)S(1)} %get-tuple-element.39.refs_0_, f32[1,256]{1,0:T(1,128)S(1)} %bitcast.104, f32[1,256]{1,0:T(1,128)S(1)} %bitcast.98, f32[1,256]{1,0:T(1,128)S(1)} %bitcast.92, f32[1,256]{1,0:T(1,128)S(1)} %get-tuple-element.28.refs_4_.refs_5_, ...), custom_call_target="tpu_custom_call" | custom-call | tf_op jit(solution)/shard_map/back/pallas_call | solution.py:155
  75.3 1.2 %collective-permute-done.23 = f32[16384]{0:T(1024)S(1)} collective-permute-done((f32[16384]{0:T(1024)S(1)}, f32[16384]{0:T(1024)S(1)}, u32[]{:S(2)}, u32[]{:S(2)}) %collective-permute-start.23) | collective-permute-done | bytes 65568 | tf_op jit(solution)/shard_map/ppermute | solution.py:29
  76.6 1.6 %collective-permute-start.24 = (f32[16384]{0:T(1024)S(1)}, f32[16384]{0:T(1024)S(1)}, u32[]{:S(2)}, u32[]{:S(2)}) collective-permute-start(f32[16384]{0:T(1024)S(1)} %bitcast_add_fusion.1), channel_id=1, source_target_pairs={{0,2},{1,3},{2,0},{3,1},{4,6},{5,7},{6,4},{7,5},{8,10},{9,11},{10,... | collective-permute-start | bytes 196616 | tf_op jit(solution)/shard_map/ppermute | solution.py:29
  78.1 2.8 %collective-permute-done.24 = f32[16384]{0:T(1024)S(1)} collective-permute-done((f32[16384]{0:T(1024)S(1)}, f32[16384]{0:T(1024)S(1)}, u32[]{:S(2)}, u32[]{:S(2)}) %collective-permute-start.24) | collective-permute-done | bytes 65568 | tf_op jit(solution)/shard_map/ppermute | solution.py:29
  80.9 1.9 %forward.10 = (f32[128,128]{1,0:T(8,128)S(1)}, f32[1,256]{1,0:T(1,128)S(1)}) custom-call(f32[6]{0:T(128)S(1)} %copy-done, f32[128,128]{1,0:T(8,128)S(1)} %bitcast.60, f32[128,128]{1,0:T(8,128)S(1)} %bitcast.66, f32[128,128]{1,0:T(8,128)S(1)} %get-tuple-element.42.refs_3_, f32[192,16384]{1,0:T(8,128)S(1)} %load.1.refs_4_.refs_3_.refs_6_), custom_call_target="tpu_custom_call" | custom-call | tf_op jit(solution)/shard_map/forward/pallas_call | solution.py:165
  82.8 2.6 %collective-permute-start.27 = (f32[256]{0:T(256)S(1)}, f32[256]{0:T(256)S(1)}, u32[]{:S(2)}, u32[]{:S(2)}) collective-permute-start(f32[256]{0:T(256)S(1)} %bitcast.84), channel_id=1, source_target_pairs={{0,12},{1,13},{2,14},{3,15},{4,8},{5,9},{6,10},{7,11},{8,4},{9,5},... | collective-permute-start | bytes 3080 | tf_op jit(solution)/shard_map/ppermute | solution.py:29
  88.2 1.7 %collective-permute-done.26 = f32[256]{0:T(256)S(1)} collective-permute-done((f32[256]{0:T(256)S(1)}, f32[256]{0:T(256)S(1)}, u32[]{:S(2)}, u32[]{:S(2)}) %collective-permute-start.26) | collective-permute-done | bytes 1056 | tf_op jit(solution)/shard_map/ppermute | solution.py:29
  89.9 1.2 %back.11 = (f32[128,128]{1,0:T(8,128)S(1)}, f32[1,256]{1,0:T(1,128)S(1)}) custom-call(f32[1,256]{1,0:T(1,128)S(1)} %get-tuple-element.43.refs_0_, f32[1,256]{1,0:T(1,128)S(1)} %bitcast.105, f32[1,256]{1,0:T(1,128)S(1)} %bitcast.99, f32[1,256]{1,0:T(1,128)S(1)} %bitcast.93, f32[1,256]{1,0:T(1,128)S(1)} %get-tuple-element.28.refs_4_.refs_5_, ...), custom_call_target="tpu_custom_call" | custom-call | tf_op jit(solution)/shard_map/back/pallas_call | solution.py:155
  91.2 1.2 %collective-permute-done.28 = f32[16384]{0:T(1024)S(1)} collective-permute-done((f32[16384]{0:T(1024)S(1)}, f32[16384]{0:T(1024)S(1)}, u32[]{:S(2)}, u32[]{:S(2)}) %collective-permute-start.28) | collective-permute-done | bytes 65568 | tf_op jit(solution)/shard_map/ppermute | solution.py:29
  92.4 1.6 %collective-permute-start.29 = (f32[16384]{0:T(1024)S(1)}, f32[16384]{0:T(1024)S(1)}, u32[]{:S(2)}, u32[]{:S(2)}) collective-permute-start(f32[16384]{0:T(1024)S(1)} %bitcast_add_fusion), channel_id=1, source_target_pairs={{0,2},{1,3},{2,0},{3,1},{4,6},{5,7},{6,4},{7,5},{8,10},{9,11},{10,... | collective-permute-start | bytes 196616 | tf_op jit(solution)/shard_map/ppermute | solution.py:29
  94.0 2.8 %collective-permute-done.29 = f32[16384]{0:T(1024)S(1)} collective-permute-done((f32[16384]{0:T(1024)S(1)}, f32[16384]{0:T(1024)S(1)}, u32[]{:S(2)}, u32[]{:S(2)}) %collective-permute-start.29) | collective-permute-done | bytes 65568 | tf_op jit(solution)/shard_map/ppermute | solution.py:29
  96.8 1.9 %forward.11 = (f32[128,128]{1,0:T(8,128)S(1)}, f32[1,256]{1,0:T(1,128)S(1)}) custom-call(f32[6]{0:T(128)S(1)} %copy-done, f32[128,128]{1,0:T(8,128)S(1)} %bitcast.56, f32[128,128]{1,0:T(8,128)S(1)} %bitcast.62, f32[128,128]{1,0:T(8,128)S(1)} %get-tuple-element.46.refs_3_, f32[192,16384]{1,0:T(8,128)S(1)} %load.1.refs_4_.refs_3_.refs_6_), custom_call_target="tpu_custom_call" | custom-call | tf_op jit(solution)/shard_map/forward/pallas_call | solution.py:165
  98.6 1.5 %collective-permute-start.32 = (f32[256]{0:T(256)S(1)}, f32[256]{0:T(256)S(1)}, u32[]{:S(2)}, u32[]{:S(2)}) collective-permute-start(f32[256]{0:T(256)S(1)} %bitcast.109), channel_id=1, source_target_pairs={{0,12},{1,13},{2,14},{3,15},{4,8},{5,9},{6,10},{7,11},{8,4},{9,5},... | collective-permute-start | bytes 3080 | tf_op jit(solution)/shard_map/ppermute | solution.py:29
  101.1 2.0 %collective-permute-start.30 = (f32[256]{0:T(256)S(1)}, f32[256]{0:T(256)S(1)}, u32[]{:S(2)}, u32[]{:S(2)}) collective-permute-start(f32[256]{0:T(256)S(1)} %bitcast.111), channel_id=1, source_target_pairs={{0,4},{1,5},{2,6},{3,7},{4,0},{5,1},{6,2},{7,3},{8,12},{9,13},{10,... | collective-permute-start | bytes 3080 | tf_op jit(solution)/shard_map/ppermute | solution.py:29
  (45 shorter events, 13.6 us)
Async XLA Ops:
  1.5 10.3 %collective-permute-start.2 = (f32[256]{0:T(256)S(1)}, f32[256]{0:T(256)S(1)}, u32[]{:S(2)}, u32[]{:S(2)}) collective-permute-start(f32[256]{0:T(256)S(1)} %dynamic_update_slice.3), channel_id=1, source_target_pairs={{0,12},{1,13},{2,14},{3,15},{4,8},{5,9},{6,10},{7,11},{8,4},{9,5},... | collective-permute-start | bytes 3080 | tf_op jit(solution)/shard_map/ppermute | solution.py:29
  6.6 5.3 %collective-permute-start.1 = (f32[256]{0:T(256)S(1)}, f32[256]{0:T(256)S(1)}, u32[]{:S(2)}, u32[]{:S(2)}) collective-permute-start(f32[256]{0:T(256)S(1)} %dynamic_update_slice.3), channel_id=1, source_target_pairs={{0,8},{1,9},{2,10},{3,11},{4,12},{5,13},{6,14},{7,15},{8,0},{9,1},... | collective-permute-start | bytes 3080 | tf_op jit(solution)/shard_map/ppermute | solution.py:29
  6.6 5.3 %collective-permute-start = (f32[256]{0:T(256)S(1)}, f32[256]{0:T(256)S(1)}, u32[]{:S(2)}, u32[]{:S(2)}) collective-permute-start(f32[256]{0:T(256)S(1)} %dynamic_update_slice.3), channel_id=1, source_target_pairs={{0,4},{1,5},{2,6},{3,7},{4,0},{5,1},{6,2},{7,3},{8,12},{9,13},{10,... | collective-permute-start | bytes 3080 | tf_op jit(solution)/shard_map/ppermute | solution.py:29
  11.8 6.8 %copy-start = (f32[6]{0:T(128)S(1)}, f32[6]{0:T(128)}, u32[]{:S(2)}) copy-start(f32[6]{0:T(128)} %refs_0_.11) | copy-start | bytes 76
  12.9 1.3 %collective-permute-start.3 = (f32[16384]{0:T(1024)S(1)}, f32[16384]{0:T(1024)S(1)}, u32[]{:S(2)}, u32[]{:S(2)}) collective-permute-start(f32[16384]{0:T(1024)S(1)} %bitcast.72), channel_id=1, source_target_pairs={{0,1},{1,0},{2,3},{3,2},{4,5},{5,4},{6,7},{7,6},{8,9},{9,8},{10,11... | collective-permute-start | bytes 196616 | tf_op jit(solution)/shard_map/ppermute | solution.py:29
  14.3 4.3 %collective-permute-start.4 = (f32[16384]{0:T(1024)S(1)}, f32[16384]{0:T(1024)S(1)}, u32[]{:S(2)}, u32[]{:S(2)}) collective-permute-start(f32[16384]{0:T(1024)S(1)} %bitcast_add_fusion.5), channel_id=1, source_target_pairs={{0,2},{1,3},{2,0},{3,1},{4,6},{5,7},{6,4},{7,5},{8,10},{9,11},{10,... | collective-permute-start | bytes 196616 | tf_op jit(solution)/shard_map/ppermute | solution.py:29
  20.4 5.4 %collective-permute-start.7 = (f32[256]{0:T(256)S(1)}, f32[256]{0:T(256)S(1)}, u32[]{:S(2)}, u32[]{:S(2)}) collective-permute-start(f32[256]{0:T(256)S(1)} %bitcast.87), channel_id=1, source_target_pairs={{0,12},{1,13},{2,14},{3,15},{4,8},{5,9},{6,10},{7,11},{8,4},{9,5},... | collective-permute-start | bytes 3080 | tf_op jit(solution)/shard_map/ppermute | solution.py:29
  24.3 4.5 %collective-permute-start.6 = (f32[256]{0:T(256)S(1)}, f32[256]{0:T(256)S(1)}, u32[]{:S(2)}, u32[]{:S(2)}) collective-permute-start(f32[256]{0:T(256)S(1)} %bitcast.88), channel_id=1, source_target_pairs={{0,8},{1,9},{2,10},{3,11},{4,12},{5,13},{6,14},{7,15},{8,0},{9,1},... | collective-permute-start | bytes 3080 | tf_op jit(solution)/shard_map/ppermute | solution.py:29
  24.3 4.5 %collective-permute-start.5 = (f32[256]{0:T(256)S(1)}, f32[256]{0:T(256)S(1)}, u32[]{:S(2)}, u32[]{:S(2)}) collective-permute-start(f32[256]{0:T(256)S(1)} %bitcast.89), channel_id=1, source_target_pairs={{0,4},{1,5},{2,6},{3,7},{4,0},{5,1},{6,2},{7,3},{8,12},{9,13},{10,... | collective-permute-start | bytes 3080 | tf_op jit(solution)/shard_map/ppermute | solution.py:29
  29.9 1.3 %collective-permute-start.8 = (f32[16384]{0:T(1024)S(1)}, f32[16384]{0:T(1024)S(1)}, u32[]{:S(2)}, u32[]{:S(2)}) collective-permute-start(f32[16384]{0:T(1024)S(1)} %bitcast.73), channel_id=1, source_target_pairs={{0,1},{1,0},{2,3},{3,2},{4,5},{5,4},{6,7},{7,6},{8,9},{9,8},{10,11... | collective-permute-start | bytes 196616 | tf_op jit(solution)/shard_map/ppermute | solution.py:29
  31.3 4.3 %collective-permute-start.9 = (f32[16384]{0:T(1024)S(1)}, f32[16384]{0:T(1024)S(1)}, u32[]{:S(2)}, u32[]{:S(2)}) collective-permute-start(f32[16384]{0:T(1024)S(1)} %bitcast_add_fusion.4), channel_id=1, source_target_pairs={{0,2},{1,3},{2,0},{3,1},{4,6},{5,7},{6,4},{7,5},{8,10},{9,11},{10,... | collective-permute-start | bytes 196616 | tf_op jit(solution)/shard_map/ppermute | solution.py:29
  37.5 5.4 %collective-permute-start.12 = (f32[256]{0:T(256)S(1)}, f32[256]{0:T(256)S(1)}, u32[]{:S(2)}, u32[]{:S(2)}) collective-permute-start(f32[256]{0:T(256)S(1)} %bitcast.75), channel_id=1, source_target_pairs={{0,12},{1,13},{2,14},{3,15},{4,8},{5,9},{6,10},{7,11},{8,4},{9,5},... | collective-permute-start | bytes 3080 | tf_op jit(solution)/shard_map/ppermute | solution.py:29
  39.0 4.5 %collective-permute-start.11 = (f32[256]{0:T(256)S(1)}, f32[256]{0:T(256)S(1)}, u32[]{:S(2)}, u32[]{:S(2)}) collective-permute-start(f32[256]{0:T(256)S(1)} %bitcast.76), channel_id=1, source_target_pairs={{0,8},{1,9},{2,10},{3,11},{4,12},{5,13},{6,14},{7,15},{8,0},{9,1},... | collective-permute-start | bytes 3080 | tf_op jit(solution)/shard_map/ppermute | solution.py:29
  39.6 3.8 %collective-permute-start.10 = (f32[256]{0:T(256)S(1)}, f32[256]{0:T(256)S(1)}, u32[]{:S(2)}, u32[]{:S(2)}) collective-permute-start(f32[256]{0:T(256)S(1)} %bitcast.77), channel_id=1, source_target_pairs={{0,4},{1,5},{2,6},{3,7},{4,0},{5,1},{6,2},{7,3},{8,12},{9,13},{10,... | collective-permute-start | bytes 3080 | tf_op jit(solution)/shard_map/ppermute | solution.py:29
  44.7 1.3 %collective-permute-start.13 = (f32[16384]{0:T(1024)S(1)}, f32[16384]{0:T(1024)S(1)}, u32[]{:S(2)}, u32[]{:S(2)}) collective-permute-start(f32[16384]{0:T(1024)S(1)} %bitcast.68), channel_id=1, source_target_pairs={{0,1},{1,0},{2,3},{3,2},{4,5},{5,4},{6,7},{7,6},{8,9},{9,8},{10,11... | collective-permute-start | bytes 196616 | tf_op jit(solution)/shard_map/ppermute | solution.py:29
  46.0 4.3 %collective-permute-start.14 = (f32[16384]{0:T(1024)S(1)}, f32[16384]{0:T(1024)S(1)}, u32[]{:S(2)}, u32[]{:S(2)}) collective-permute-start(f32[16384]{0:T(1024)S(1)} %bitcast_add_fusion.3), channel_id=1, source_target_pairs={{0,2},{1,3},{2,0},{3,1},{4,6},{5,7},{6,4},{7,5},{8,10},{9,11},{10,... | collective-permute-start | bytes 196616 | tf_op jit(solution)/shard_map/ppermute | solution.py:29
  52.2 5.4 %collective-permute-start.17 = (f32[256]{0:T(256)S(1)}, f32[256]{0:T(256)S(1)}, u32[]{:S(2)}, u32[]{:S(2)}) collective-permute-start(f32[256]{0:T(256)S(1)} %bitcast.78), channel_id=1, source_target_pairs={{0,12},{1,13},{2,14},{3,15},{4,8},{5,9},{6,10},{7,11},{8,4},{9,5},... | collective-permute-start | bytes 3080 | tf_op jit(solution)/shard_map/ppermute | solution.py:29
  54.8 4.5 %collective-permute-start.16 = (f32[256]{0:T(256)S(1)}, f32[256]{0:T(256)S(1)}, u32[]{:S(2)}, u32[]{:S(2)}) collective-permute-start(f32[256]{0:T(256)S(1)} %bitcast.79), channel_id=1, source_target_pairs={{0,8},{1,9},{2,10},{3,11},{4,12},{5,13},{6,14},{7,15},{8,0},{9,1},... | collective-permute-start | bytes 3080 | tf_op jit(solution)/shard_map/ppermute | solution.py:29
  55.7 3.6 %collective-permute-start.15 = (f32[256]{0:T(256)S(1)}, f32[256]{0:T(256)S(1)}, u32[]{:S(2)}, u32[]{:S(2)}) collective-permute-start(f32[256]{0:T(256)S(1)} %bitcast.80), channel_id=1, source_target_pairs={{0,4},{1,5},{2,6},{3,7},{4,0},{5,1},{6,2},{7,3},{8,12},{9,13},{10,... | collective-permute-start | bytes 3080 | tf_op jit(solution)/shard_map/ppermute | solution.py:29
  60.5 1.3 %collective-permute-start.18 = (f32[16384]{0:T(1024)S(1)}, f32[16384]{0:T(1024)S(1)}, u32[]{:S(2)}, u32[]{:S(2)}) collective-permute-start(f32[16384]{0:T(1024)S(1)} %bitcast.69), channel_id=1, source_target_pairs={{0,1},{1,0},{2,3},{3,2},{4,5},{5,4},{6,7},{7,6},{8,9},{9,8},{10,11... | collective-permute-start | bytes 196616 | tf_op jit(solution)/shard_map/ppermute | solution.py:29
  61.8 4.3 %collective-permute-start.19 = (f32[16384]{0:T(1024)S(1)}, f32[16384]{0:T(1024)S(1)}, u32[]{:S(2)}, u32[]{:S(2)}) collective-permute-start(f32[16384]{0:T(1024)S(1)} %bitcast_add_fusion.2), channel_id=1, source_target_pairs={{0,2},{1,3},{2,0},{3,1},{4,6},{5,7},{6,4},{7,5},{8,10},{9,11},{10,... | collective-permute-start | bytes 196616 | tf_op jit(solution)/shard_map/ppermute | solution.py:29
  68.1 5.4 %collective-permute-start.22 = (f32[256]{0:T(256)S(1)}, f32[256]{0:T(256)S(1)}, u32[]{:S(2)}, u32[]{:S(2)}) collective-permute-start(f32[256]{0:T(256)S(1)} %bitcast.81), channel_id=1, source_target_pairs={{0,12},{1,13},{2,14},{3,15},{4,8},{5,9},{6,10},{7,11},{8,4},{9,5},... | collective-permute-start | bytes 3080 | tf_op jit(solution)/shard_map/ppermute | solution.py:29
  69.6 4.5 %collective-permute-start.21 = (f32[256]{0:T(256)S(1)}, f32[256]{0:T(256)S(1)}, u32[]{:S(2)}, u32[]{:S(2)}) collective-permute-start(f32[256]{0:T(256)S(1)} %bitcast.82), channel_id=1, source_target_pairs={{0,8},{1,9},{2,10},{3,11},{4,12},{5,13},{6,14},{7,15},{8,0},{9,1},... | collective-permute-start | bytes 3080 | tf_op jit(solution)/shard_map/ppermute | solution.py:29
  70.5 3.6 %collective-permute-start.20 = (f32[256]{0:T(256)S(1)}, f32[256]{0:T(256)S(1)}, u32[]{:S(2)}, u32[]{:S(2)}) collective-permute-start(f32[256]{0:T(256)S(1)} %bitcast.83), channel_id=1, source_target_pairs={{0,4},{1,5},{2,6},{3,7},{4,0},{5,1},{6,2},{7,3},{8,12},{9,13},{10,... | collective-permute-start | bytes 3080 | tf_op jit(solution)/shard_map/ppermute | solution.py:29
  75.3 1.3 %collective-permute-start.23 = (f32[16384]{0:T(1024)S(1)}, f32[16384]{0:T(1024)S(1)}, u32[]{:S(2)}, u32[]{:S(2)}) collective-permute-start(f32[16384]{0:T(1024)S(1)} %bitcast.70), channel_id=1, source_target_pairs={{0,1},{1,0},{2,3},{3,2},{4,5},{5,4},{6,7},{7,6},{8,9},{9,8},{10,11... | collective-permute-start | bytes 196616 | tf_op jit(solution)/shard_map/ppermute | solution.py:29
  76.6 4.3 %collective-permute-start.24 = (f32[16384]{0:T(1024)S(1)}, f32[16384]{0:T(1024)S(1)}, u32[]{:S(2)}, u32[]{:S(2)}) collective-permute-start(f32[16384]{0:T(1024)S(1)} %bitcast_add_fusion.1), channel_id=1, source_target_pairs={{0,2},{1,3},{2,0},{3,1},{4,6},{5,7},{6,4},{7,5},{8,10},{9,11},{10,... | collective-permute-start | bytes 196616 | tf_op jit(solution)/shard_map/ppermute | solution.py:29
  82.8 5.4 %collective-permute-start.27 = (f32[256]{0:T(256)S(1)}, f32[256]{0:T(256)S(1)}, u32[]{:S(2)}, u32[]{:S(2)}) collective-permute-start(f32[256]{0:T(256)S(1)} %bitcast.84), channel_id=1, source_target_pairs={{0,12},{1,13},{2,14},{3,15},{4,8},{5,9},{6,10},{7,11},{8,4},{9,5},... | collective-permute-start | bytes 3080 | tf_op jit(solution)/shard_map/ppermute | solution.py:29
  85.4 4.5 %collective-permute-start.26 = (f32[256]{0:T(256)S(1)}, f32[256]{0:T(256)S(1)}, u32[]{:S(2)}, u32[]{:S(2)}) collective-permute-start(f32[256]{0:T(256)S(1)} %bitcast.85), channel_id=1, source_target_pairs={{0,8},{1,9},{2,10},{3,11},{4,12},{5,13},{6,14},{7,15},{8,0},{9,1},... | collective-permute-start | bytes 3080 | tf_op jit(solution)/shard_map/ppermute | solution.py:29
  86.3 3.6 %collective-permute-start.25 = (f32[256]{0:T(256)S(1)}, f32[256]{0:T(256)S(1)}, u32[]{:S(2)}, u32[]{:S(2)}) collective-permute-start(f32[256]{0:T(256)S(1)} %bitcast.86), channel_id=1, source_target_pairs={{0,4},{1,5},{2,6},{3,7},{4,0},{5,1},{6,2},{7,3},{8,12},{9,13},{10,... | collective-permute-start | bytes 3080 | tf_op jit(solution)/shard_map/ppermute | solution.py:29
  91.1 1.3 %collective-permute-start.28 = (f32[16384]{0:T(1024)S(1)}, f32[16384]{0:T(1024)S(1)}, u32[]{:S(2)}, u32[]{:S(2)}) collective-permute-start(f32[16384]{0:T(1024)S(1)} %bitcast.71), channel_id=1, source_target_pairs={{0,1},{1,0},{2,3},{3,2},{4,5},{5,4},{6,7},{7,6},{8,9},{9,8},{10,11... | collective-permute-start | bytes 196616 | tf_op jit(solution)/shard_map/ppermute | solution.py:29
  92.4 4.3 %collective-permute-start.29 = (f32[16384]{0:T(1024)S(1)}, f32[16384]{0:T(1024)S(1)}, u32[]{:S(2)}, u32[]{:S(2)}) collective-permute-start(f32[16384]{0:T(1024)S(1)} %bitcast_add_fusion), channel_id=1, source_target_pairs={{0,2},{1,3},{2,0},{3,1},{4,6},{5,7},{6,4},{7,5},{8,10},{9,11},{10,... | collective-permute-start | bytes 196616 | tf_op jit(solution)/shard_map/ppermute | solution.py:29
  98.6 5.4 %collective-permute-start.32 = (f32[256]{0:T(256)S(1)}, f32[256]{0:T(256)S(1)}, u32[]{:S(2)}, u32[]{:S(2)}) collective-permute-start(f32[256]{0:T(256)S(1)} %bitcast.109), channel_id=1, source_target_pairs={{0,12},{1,13},{2,14},{3,15},{4,8},{5,9},{6,10},{7,11},{8,4},{9,5},... | collective-permute-start | bytes 3080 | tf_op jit(solution)/shard_map/ppermute | solution.py:29
  100.2 4.5 %collective-permute-start.31 = (f32[256]{0:T(256)S(1)}, f32[256]{0:T(256)S(1)}, u32[]{:S(2)}, u32[]{:S(2)}) collective-permute-start(f32[256]{0:T(256)S(1)} %bitcast.110), channel_id=1, source_target_pairs={{0,8},{1,9},{2,10},{3,11},{4,12},{5,13},{6,14},{7,15},{8,0},{9,1},... | collective-permute-start | bytes 3080 | tf_op jit(solution)/shard_map/ppermute | solution.py:29
  101.1 3.6 %collective-permute-start.30 = (f32[256]{0:T(256)S(1)}, f32[256]{0:T(256)S(1)}, u32[]{:S(2)}, u32[]{:S(2)}) collective-permute-start(f32[256]{0:T(256)S(1)} %bitcast.111), channel_id=1, source_target_pairs={{0,4},{1,5},{2,6},{3,7},{4,0},{5,1},{6,2},{7,3},{8,12},{9,13},{10,... | collective-permute-start | bytes 3080 | tf_op jit(solution)/shard_map/ppermute | solution.py:29

commit v2 on v1

--- a/solution.py
+++ b/solution.py
@@ -50,6 +50,12 @@
     return estimate, slope
 
 
+def column_total(parts):
+    while len(parts) > 1:
+        parts = [parts[at] + parts[at + 1] for at in range(0, len(parts), 2)]
+    return parts[0]
+
+
 def load_kernel(source, target, semaphore):
     copy = pltpu.make_async_copy(source, target, semaphore)
     copy.start()
@@ -61,9 +67,7 @@
         *parts, sensing, out, residual_out = refs
     else:
         *parts, measured, old, sensing, out, residual_out = refs
-    total = parts[0][...]
-    for part in parts[1:]:
-        total = total + part[...]
+    total = column_total([part[...] for part in parts])
     if first:
         residual = total
     else:
@@ -94,9 +98,9 @@
     else:
         thresholds, partial, other, old, sensing, estimate_out, out = refs
         pseudo = old[...] + (partial[...] + other[...])
-    estimate, slopes = shrink_and_slope(pseudo, thresholds[step_at])
+    estimate, slopes = shrink_and_slope(pseudo, thresholds[:, step_at : step_at + 1])
     estimate_out[...] = estimate
-    slope = jnp.sum(slopes, keepdims=True)
+    slope = jnp.sum(slopes, axis=0, keepdims=True)
 
     def step(group, totals):
         start = pl.multiple_of(group * UNROLL * LANES, UNROLL * LANES)
@@ -111,12 +115,9 @@
 
     nothing = tuple(jnp.zeros((8, LANES), jnp.float32) for _ in range(rows // 8))
     totals = lax.fori_loop(0, estimate_out.shape[0] // UNROLL, step, nothing)
-    total = jnp.concatenate(totals)
-    padded = out.shape[1]
-    total = jnp.concatenate([total, jnp.zeros((padded - rows, LANES), jnp.float32)])
-    product = jnp.sum(total.T, axis=0, keepdims=True)
-    place = lax.broadcasted_iota(jnp.int32, product.shape, 1)
-    out[...] = jnp.where(place == rows, slope, product)
+    padding = jnp.zeros((out.shape[1] - rows - 8, LANES), jnp.float32)
+    total = jnp.concatenate([*totals, jnp.broadcast_to(slope, (8, LANES)), padding])
+    out[...] = jnp.sum(total.T, axis=0, keepdims=True)
 
 
 def on_device(sensing, measured, thresholds):
@@ -130,11 +131,10 @@
     group_pos = index % groups
     column_pos = index // groups
     share = width // groups
-    padded = (rows + LANES) // LANES * LANES
+    padded = (rows + 8 + LANES - 1) // LANES * LANES
     tiles = width // LANES
     params = pltpu.CompilerParams(vmem_limit_bytes=LIMIT)
     in_vmem = pl.BlockSpec(memory_space=VMEM)
-    in_smem = pl.BlockSpec(memory_space=pltpu.SMEM)
     matrix = pl.pallas_call(
         load_kernel,
         out_shape=VMEM(sensing.shape, sensing.dtype),
@@ -165,11 +165,11 @@
         return pl.pallas_call(
             functools.partial(forward_kernel, first, rows, step),
             out_shape=(signal, row),
-            in_specs=[in_smem] + [in_vmem] * (len(others) + 1),
+            in_specs=[in_vmem] * (len(others) + 2),
             out_specs=(in_vmem, in_vmem),
             compiler_params=params,
             name="forward",
-        )(thresholds, *others, matrix)
+        )(thresholds.reshape(1, -1), *others, matrix)
 
     def all_columns(piece):
         flat = piece.reshape(padded)
@@ -198,7 +198,7 @@
         )
         estimate = (new_estimate,)
         parts = all_columns(product)
-    total = sum(parts[1:], parts[0])[0]
+    total = column_total(parts)[0]
     onsager = total[rows] / all_rows
     final = measured_row[0] - total + onsager * others[1][0]
     estimate = lax.dynamic_slice_in_dim(estimate[0].reshape(width), group_pos * share, share)

time: 107 us -> 103 us (0.963)
  Pallas kernels: 22.8 us -> 19.2 us
    pallas_call x6, Pallas kernels: 11.2 us -> 7.59 us  [forward(): pl.pallas_call(functools.partial(forward_kernel, first, rows, step), out_...]
where the time goes in v2:
time: 103 us
  starting transfers between devices  42.3 us (41%)
  waiting for transfers between devices  37.1 us (36%)
  Pallas kernels  19.2 us (19%)
  local copies, waits for them, and re-layouts  2.06 us (2%)
  between operations  1.54 us (1%)
    ppermute x33, starting transfers between devices, swapped(): return lax.ppermute(value, 'row', pairs)  42.3 us
    ppermute x33, waiting for transfers between devices, swapped(): return lax.ppermute(value, 'row', pairs)  37.1 us
    pallas_call x6, Pallas kernels, forward(): pl.pallas_call(functools.partial(forward_kernel, first, rows, step), out_...  7.59 us
    pallas_call x6, Pallas kernels, back(): pl.pallas_call(functools.partial(back_kernel, first, rows, all_rows), out...  7.04 us
    pallas_call x1, Pallas kernels, on_device(): pl.pallas_call(load_kernel, out_shape=VMEM(sensing.shape, sensing.dtype),...  4.58 us
  transfers between devices with their start and end apart: 33, of which 24 were waited for; matrix products, arithmetic and copies ran while one was open for 1% of the time, Pallas kernels for 4%

profile of v2, /device:TPU:0, one launch (start us, length us, event | category | flops | bytes accessed | tf_op | source)
XLA Modules:
  0.0 102.9 jit_solution(16679854763601617276)
XLA Ops:
  1.5 5.1 %collective-permute-start.2 = (f32[256]{0:T(256)S(1)}, f32[256]{0:T(256)S(1)}, u32[]{:S(2)}, u32[]{:S(2)}) collective-permute-start(f32[256]{0:T(256)S(1)} %dynamic_update_slice.3), channel_id=1, source_target_pairs={{0,12},{1,13},{2,14},{3,15},{4,8},{5,9},{6,10},{7,11},{8,4},{9,5},... | collective-permute-start | bytes 3080 | tf_op jit(solution)/shard_map/ppermute | solution.py:29
  7.2 4.6 %load.1.refs_4_.refs_3_.refs_6_ = f32[192,16384]{1,0:T(8,128)S(1)} custom-call(f32[192,16384]{1,0:T(8,128)} %source.1), custom_call_target="tpu_custom_call" | custom-call | bytes 25165824 | tf_op jit(solution)/shard_map/load/pallas_call | solution.py:138
  11.9 1.1 %back.6 = (f32[128,128]{1,0:T(8,128)S(1)}, f32[1,256]{1,0:T(1,128)S(1)}) custom-call(f32[1,256]{1,0:T(1,128)S(1)} %bitcast.114, f32[1,256]{1,0:T(1,128)S(1)} %bitcast.112, f32[1,256]{1,0:T(1,128)S(1)} %bitcast.106, f32[1,256]{1,0:T(1,128)S(1)} %bitcast.100, f32[192,16384]{1,0:T(8,128)S(1)} %load.1.refs_4_.refs_3_.refs_6_), custom_call_target="tpu_custom_call" | custom-call | tf_op jit(solution)/shard_map/back/pallas_call | solution.py:155
  13.0 1.2 %collective-permute-done.3 = f32[16384]{0:T(1024)S(1)} collective-permute-done((f32[16384]{0:T(1024)S(1)}, f32[16384]{0:T(1024)S(1)}, u32[]{:S(2)}, u32[]{:S(2)}) %collective-permute-start.3) | collective-permute-done | bytes 65568 | tf_op jit(solution)/shard_map/ppermute | solution.py:29
  14.3 1.7 %collective-permute-start.4 = (f32[16384]{0:T(1024)S(1)}, f32[16384]{0:T(1024)S(1)}, u32[]{:S(2)}, u32[]{:S(2)}) collective-permute-start(f32[16384]{0:T(1024)S(1)} %bitcast_add_fusion.5), channel_id=1, source_target_pairs={{0,2},{1,3},{2,0},{3,1},{4,6},{5,7},{6,4},{7,5},{8,10},{9,11},{10,... | collective-permute-start | bytes 196616 | tf_op jit(solution)/shard_map/ppermute | solution.py:29
  16.0 2.6 %collective-permute-done.4 = f32[16384]{0:T(1024)S(1)} collective-permute-done((f32[16384]{0:T(1024)S(1)}, f32[16384]{0:T(1024)S(1)}, u32[]{:S(2)}, u32[]{:S(2)}) %collective-permute-start.4) | collective-permute-done | bytes 65568 | tf_op jit(solution)/shard_map/ppermute | solution.py:29
  18.6 1.3 %forward.6 = (f32[128,128]{1,0:T(8,128)S(1)}, f32[1,256]{1,0:T(1,128)S(1)}) custom-call(f32[1,6]{1,0:T(1,128)S(1)} %bitcast.74, f32[128,128]{1,0:T(8,128)S(1)} %bitcast.61, f32[128,128]{1,0:T(8,128)S(1)} %bitcast.67, f32[192,16384]{1,0:T(8,128)S(1)} %load.1.refs_4_.refs_3_.refs_6_), custom_call_target="tpu_custom_call" | custom-call | tf_op jit(solution)/shard_map/forward/pallas_call | solution.py:165
  19.9 3.8 %collective-permute-start.7 = (f32[256]{0:T(256)S(1)}, f32[256]{0:T(256)S(1)}, u32[]{:S(2)}, u32[]{:S(2)}) collective-permute-start(f32[256]{0:T(256)S(1)} %bitcast.93), channel_id=1, source_target_pairs={{0,12},{1,13},{2,14},{3,15},{4,8},{5,9},{6,10},{7,11},{8,4},{9,5},... | collective-permute-start | bytes 3080 | tf_op jit(solution)/shard_map/ppermute | solution.py:29
  24.3 1.0 collective-permute-done.7
  25.3 2.8 %collective-permute-done.6 = f32[256]{0:T(256)S(1)} collective-permute-done((f32[256]{0:T(256)S(1)}, f32[256]{0:T(256)S(1)}, u32[]{:S(2)}, u32[]{:S(2)}) %collective-permute-start.6) | collective-permute-done | bytes 1056 | tf_op jit(solution)/shard_map/ppermute | solution.py:29
  28.1 1.2 %back.7 = (f32[128,128]{1,0:T(8,128)S(1)}, f32[1,256]{1,0:T(1,128)S(1)}) custom-call(f32[1,256]{1,0:T(1,128)S(1)} %get-tuple-element.27.refs_0_, f32[1,256]{1,0:T(1,128)S(1)} %bitcast.113, f32[1,256]{1,0:T(1,128)S(1)} %bitcast.107, f32[1,256]{1,0:T(1,128)S(1)} %bitcast.101, f32[1,256]{1,0:T(1,128)S(1)} %get-tuple-element.28.refs_4_.refs_5_, ...), custom_call_target="tpu_custom_call" | custom-call | tf_op jit(solution)/shard_map/back/pallas_call | solution.py:155
  29.4 1.2 %collective-permute-done.8 = f32[16384]{0:T(1024)S(1)} collective-permute-done((f32[16384]{0:T(1024)S(1)}, f32[16384]{0:T(1024)S(1)}, u32[]{:S(2)}, u32[]{:S(2)}) %collective-permute-start.8) | collective-permute-done | bytes 65568 | tf_op jit(solution)/shard_map/ppermute | solution.py:29
  30.7 1.6 %collective-permute-start.9 = (f32[16384]{0:T(1024)S(1)}, f32[16384]{0:T(1024)S(1)}, u32[]{:S(2)}, u32[]{:S(2)}) collective-permute-start(f32[16384]{0:T(1024)S(1)} %bitcast_add_fusion.4), channel_id=1, source_target_pairs={{0,2},{1,3},{2,0},{3,1},{4,6},{5,7},{6,4},{7,5},{8,10},{9,11},{10,... | collective-permute-start | bytes 196616 | tf_op jit(solution)/shard_map/ppermute | solution.py:29
  32.2 2.8 %collective-permute-done.9 = f32[16384]{0:T(1024)S(1)} collective-permute-done((f32[16384]{0:T(1024)S(1)}, f32[16384]{0:T(1024)S(1)}, u32[]{:S(2)}, u32[]{:S(2)}) %collective-permute-start.9) | collective-permute-done | bytes 65568 | tf_op jit(solution)/shard_map/ppermute | solution.py:29
  35.0 1.3 %forward.7 = (f32[128,128]{1,0:T(8,128)S(1)}, f32[1,256]{1,0:T(1,128)S(1)}) custom-call(f32[1,6]{1,0:T(1,128)S(1)} %bitcast.75, f32[128,128]{1,0:T(8,128)S(1)} %bitcast.57, f32[128,128]{1,0:T(8,128)S(1)} %bitcast.63, f32[128,128]{1,0:T(8,128)S(1)} %get-tuple-element.30.refs_3_, f32[192,16384]{1,0:T(8,128)S(1)} %load.1.refs_4_.refs_3_.refs_6_), custom_call_target="tpu_custom_call" | custom-call | tf_op jit(solution)/shard_map/forward/pallas_call | solution.py:165
  36.3 1.5 %collective-permute-start.12 = (f32[256]{0:T(256)S(1)}, f32[256]{0:T(256)S(1)}, u32[]{:S(2)}, u32[]{:S(2)}) collective-permute-start(f32[256]{0:T(256)S(1)} %bitcast.81), channel_id=1, source_target_pairs={{0,12},{1,13},{2,14},{3,15},{4,8},{5,9},{6,10},{7,11},{8,4},{9,5},... | collective-permute-start | bytes 3080 | tf_op jit(solution)/shard_map/ppermute | solution.py:29
  38.5 2.3 %collective-permute-start.10 = (f32[256]{0:T(256)S(1)}, f32[256]{0:T(256)S(1)}, u32[]{:S(2)}, u32[]{:S(2)}) collective-permute-start(f32[256]{0:T(256)S(1)} %bitcast.83), channel_id=1, source_target_pairs={{0,4},{1,5},{2,6},{3,7},{4,0},{5,1},{6,2},{7,3},{8,12},{9,13},{10,... | collective-permute-start | bytes 3080 | tf_op jit(solution)/shard_map/ppermute | solution.py:29
  40.7 1.0 collective-permute-done.12
  42.3 1.2 %back.8 = (f32[128,128]{1,0:T(8,128)S(1)}, f32[1,256]{1,0:T(1,128)S(1)}) custom-call(f32[1,256]{1,0:T(1,128)S(1)} %get-tuple-element.31.refs_0_, f32[1,256]{1,0:T(1,128)S(1)} %bitcast.108, f32[1,256]{1,0:T(1,128)S(1)} %bitcast.102, f32[1,256]{1,0:T(1,128)S(1)} %bitcast.96, f32[1,256]{1,0:T(1,128)S(1)} %get-tuple-element.28.refs_4_.refs_5_, ...), custom_call_target="tpu_custom_call" | custom-call | tf_op jit(solution)/shard_map/back/pallas_call | solution.py:155
  43.6 1.2 %collective-permute-done.13 = f32[16384]{0:T(1024)S(1)} collective-permute-done((f32[16384]{0:T(1024)S(1)}, f32[16384]{0:T(1024)S(1)}, u32[]{:S(2)}, u32[]{:S(2)}) %collective-permute-start.13) | collective-permute-done | bytes 65568 | tf_op jit(solution)/shard_map/ppermute | solution.py:29
  44.8 1.6 %collective-permute-start.14 = (f32[16384]{0:T(1024)S(1)}, f32[16384]{0:T(1024)S(1)}, u32[]{:S(2)}, u32[]{:S(2)}) collective-permute-start(f32[16384]{0:T(1024)S(1)} %bitcast_add_fusion.3), channel_id=1, source_target_pairs={{0,2},{1,3},{2,0},{3,1},{4,6},{5,7},{6,4},{7,5},{8,10},{9,11},{10,... | collective-permute-start | bytes 196616 | tf_op jit(solution)/shard_map/ppermute | solution.py:29
  46.4 2.8 %collective-permute-done.14 = f32[16384]{0:T(1024)S(1)} collective-permute-done((f32[16384]{0:T(1024)S(1)}, f32[16384]{0:T(1024)S(1)}, u32[]{:S(2)}, u32[]{:S(2)}) %collective-permute-start.14) | collective-permute-done | bytes 65568 | tf_op jit(solution)/shard_map/ppermute | solution.py:29
  49.2 1.3 %forward.8 = (f32[128,128]{1,0:T(8,128)S(1)}, f32[1,256]{1,0:T(1,128)S(1)}) custom-call(f32[1,6]{1,0:T(1,128)S(1)} %bitcast.76, f32[128,128]{1,0:T(8,128)S(1)} %bitcast.58, f32[128,128]{1,0:T(8,128)S(1)} %bitcast.64, f32[128,128]{1,0:T(8,128)S(1)} %get-tuple-element.34.refs_3_, f32[192,16384]{1,0:T(8,128)S(1)} %load.1.refs_4_.refs_3_.refs_6_), custom_call_target="tpu_custom_call" | custom-call | tf_op jit(solution)/shard_map/forward/pallas_call | solution.py:165
  50.4 2.6 %collective-permute-start.17 = (f32[256]{0:T(256)S(1)}, f32[256]{0:T(256)S(1)}, u32[]{:S(2)}, u32[]{:S(2)}) collective-permute-start(f32[256]{0:T(256)S(1)} %bitcast.84), channel_id=1, source_target_pairs={{0,12},{1,13},{2,14},{3,15},{4,8},{5,9},{6,10},{7,11},{8,4},{9,5},... | collective-permute-start | bytes 3080 | tf_op jit(solution)/shard_map/ppermute | solution.py:29
  55.9 1.7 %collective-permute-done.16 = f32[256]{0:T(256)S(1)} collective-permute-done((f32[256]{0:T(256)S(1)}, f32[256]{0:T(256)S(1)}, u32[]{:S(2)}, u32[]{:S(2)}) %collective-permute-start.16) | collective-permute-done | bytes 1056 | tf_op jit(solution)/shard_map/ppermute | solution.py:29
  57.5 1.2 %back.9 = (f32[128,128]{1,0:T(8,128)S(1)}, f32[1,256]{1,0:T(1,128)S(1)}) custom-call(f32[1,256]{1,0:T(1,128)S(1)} %get-tuple-element.35.refs_0_, f32[1,256]{1,0:T(1,128)S(1)} %bitcast.109, f32[1,256]{1,0:T(1,128)S(1)} %bitcast.103, f32[1,256]{1,0:T(1,128)S(1)} %bitcast.97, f32[1,256]{1,0:T(1,128)S(1)} %get-tuple-element.28.refs_4_.refs_5_, ...), custom_call_target="tpu_custom_call" | custom-call | tf_op jit(solution)/shard_map/back/pallas_call | solution.py:155
  58.8 1.2 %collective-permute-done.18 = f32[16384]{0:T(1024)S(1)} collective-permute-done((f32[16384]{0:T(1024)S(1)}, f32[16384]{0:T(1024)S(1)}, u32[]{:S(2)}, u32[]{:S(2)}) %collective-permute-start.18) | collective-permute-done | bytes 65568 | tf_op jit(solution)/shard_map/ppermute | solution.py:29
  60.1 1.6 %collective-permute-start.19 = (f32[16384]{0:T(1024)S(1)}, f32[16384]{0:T(1024)S(1)}, u32[]{:S(2)}, u32[]{:S(2)}) collective-permute-start(f32[16384]{0:T(1024)S(1)} %bitcast_add_fusion.2), channel_id=1, source_target_pairs={{0,2},{1,3},{2,0},{3,1},{4,6},{5,7},{6,4},{7,5},{8,10},{9,11},{10,... | collective-permute-start | bytes 196616 | tf_op jit(solution)/shard_map/ppermute | solution.py:29
  61.6 2.8 %collective-permute-done.19 = f32[16384]{0:T(1024)S(1)} collective-permute-done((f32[16384]{0:T(1024)S(1)}, f32[16384]{0:T(1024)S(1)}, u32[]{:S(2)}, u32[]{:S(2)}) %collective-permute-start.19) | collective-permute-done | bytes 65568 | tf_op jit(solution)/shard_map/ppermute | solution.py:29
  64.4 1.3 %forward.9 = (f32[128,128]{1,0:T(8,128)S(1)}, f32[1,256]{1,0:T(1,128)S(1)}) custom-call(f32[1,6]{1,0:T(1,128)S(1)} %bitcast.77, f32[128,128]{1,0:T(8,128)S(1)} %bitcast.59, f32[128,128]{1,0:T(8,128)S(1)} %bitcast.65, f32[128,128]{1,0:T(8,128)S(1)} %get-tuple-element.38.refs_3_, f32[192,16384]{1,0:T(8,128)S(1)} %load.1.refs_4_.refs_3_.refs_6_), custom_call_target="tpu_custom_call" | custom-call | tf_op jit(solution)/shard_map/forward/pallas_call | solution.py:165
  65.7 1.5 %collective-permute-start.22 = (f32[256]{0:T(256)S(1)}, f32[256]{0:T(256)S(1)}, u32[]{:S(2)}, u32[]{:S(2)}) collective-permute-start(f32[256]{0:T(256)S(1)} %bitcast.87), channel_id=1, source_target_pairs={{0,12},{1,13},{2,14},{3,15},{4,8},{5,9},{6,10},{7,11},{8,4},{9,5},... | collective-permute-start | bytes 3080 | tf_op jit(solution)/shard_map/ppermute | solution.py:29
  68.1 2.0 %collective-permute-start.20 = (f32[256]{0:T(256)S(1)}, f32[256]{0:T(256)S(1)}, u32[]{:S(2)}, u32[]{:S(2)}) collective-permute-start(f32[256]{0:T(256)S(1)} %bitcast.89), channel_id=1, source_target_pairs={{0,4},{1,5},{2,6},{3,7},{4,0},{5,1},{6,2},{7,3},{8,12},{9,13},{10,... | collective-permute-start | bytes 3080 | tf_op jit(solution)/shard_map/ppermute | solution.py:29
  70.2 1.0 collective-permute-done.22
  71.7 1.2 %back.10 = (f32[128,128]{1,0:T(8,128)S(1)}, f32[1,256]{1,0:T(1,128)S(1)}) custom-call(f32[1,256]{1,0:T(1,128)S(1)} %get-tuple-element.39.refs_0_, f32[1,256]{1,0:T(1,128)S(1)} %bitcast.110, f32[1,256]{1,0:T(1,128)S(1)} %bitcast.104, f32[1,256]{1,0:T(1,128)S(1)} %bitcast.98, f32[1,256]{1,0:T(1,128)S(1)} %get-tuple-element.28.refs_4_.refs_5_, ...), custom_call_target="tpu_custom_call" | custom-call | tf_op jit(solution)/shard_map/back/pallas_call | solution.py:155
  73.0 1.2 %collective-permute-done.23 = f32[16384]{0:T(1024)S(1)} collective-permute-done((f32[16384]{0:T(1024)S(1)}, f32[16384]{0:T(1024)S(1)}, u32[]{:S(2)}, u32[]{:S(2)}) %collective-permute-start.23) | collective-permute-done | bytes 65568 | tf_op jit(solution)/shard_map/ppermute | solution.py:29
  74.2 1.6 %collective-permute-start.24 = (f32[16384]{0:T(1024)S(1)}, f32[16384]{0:T(1024)S(1)}, u32[]{:S(2)}, u32[]{:S(2)}) collective-permute-start(f32[16384]{0:T(1024)S(1)} %bitcast_add_fusion.1), channel_id=1, source_target_pairs={{0,2},{1,3},{2,0},{3,1},{4,6},{5,7},{6,4},{7,5},{8,10},{9,11},{10,... | collective-permute-start | bytes 196616 | tf_op jit(solution)/shard_map/ppermute | solution.py:29
  75.8 2.8 %collective-permute-done.24 = f32[16384]{0:T(1024)S(1)} collective-permute-done((f32[16384]{0:T(1024)S(1)}, f32[16384]{0:T(1024)S(1)}, u32[]{:S(2)}, u32[]{:S(2)}) %collective-permute-start.24) | collective-permute-done | bytes 65568 | tf_op jit(solution)/shard_map/ppermute | solution.py:29
  78.6 1.3 %forward.10 = (f32[128,128]{1,0:T(8,128)S(1)}, f32[1,256]{1,0:T(1,128)S(1)}) custom-call(f32[1,6]{1,0:T(1,128)S(1)} %bitcast.78, f32[128,128]{1,0:T(8,128)S(1)} %bitcast.60, f32[128,128]{1,0:T(8,128)S(1)} %bitcast.66, f32[128,128]{1,0:T(8,128)S(1)} %get-tuple-element.42.refs_3_, f32[192,16384]{1,0:T(8,128)S(1)} %load.1.refs_4_.refs_3_.refs_6_), custom_call_target="tpu_custom_call" | custom-call | tf_op jit(solution)/shard_map/forward/pallas_call | solution.py:165
  79.8 2.6 %collective-permute-start.27 = (f32[256]{0:T(256)S(1)}, f32[256]{0:T(256)S(1)}, u32[]{:S(2)}, u32[]{:S(2)}) collective-permute-start(f32[256]{0:T(256)S(1)} %bitcast.90), channel_id=1, source_target_pairs={{0,12},{1,13},{2,14},{3,15},{4,8},{5,9},{6,10},{7,11},{8,4},{9,5},... | collective-permute-start | bytes 3080 | tf_op jit(solution)/shard_map/ppermute | solution.py:29
  84.3 1.0 collective-permute-done.27
  85.3 1.7 %collective-permute-done.26 = f32[256]{0:T(256)S(1)} collective-permute-done((f32[256]{0:T(256)S(1)}, f32[256]{0:T(256)S(1)}, u32[]{:S(2)}, u32[]{:S(2)}) %collective-permute-start.26) | collective-permute-done | bytes 1056 | tf_op jit(solution)/shard_map/ppermute | solution.py:29
  87.0 1.2 %back.11 = (f32[128,128]{1,0:T(8,128)S(1)}, f32[1,256]{1,0:T(1,128)S(1)}) custom-call(f32[1,256]{1,0:T(1,128)S(1)} %get-tuple-element.43.refs_0_, f32[1,256]{1,0:T(1,128)S(1)} %bitcast.111, f32[1,256]{1,0:T(1,128)S(1)} %bitcast.105, f32[1,256]{1,0:T(1,128)S(1)} %bitcast.99, f32[1,256]{1,0:T(1,128)S(1)} %get-tuple-element.28.refs_4_.refs_5_, ...), custom_call_target="tpu_custom_call" | custom-call | tf_op jit(solution)/shard_map/back/pallas_call | solution.py:155
  88.2 1.2 %collective-permute-done.28 = f32[16384]{0:T(1024)S(1)} collective-permute-done((f32[16384]{0:T(1024)S(1)}, f32[16384]{0:T(1024)S(1)}, u32[]{:S(2)}, u32[]{:S(2)}) %collective-permute-start.28) | collective-permute-done | bytes 65568 | tf_op jit(solution)/shard_map/ppermute | solution.py:29
  89.5 1.6 %collective-permute-start.29 = (f32[16384]{0:T(1024)S(1)}, f32[16384]{0:T(1024)S(1)}, u32[]{:S(2)}, u32[]{:S(2)}) collective-permute-start(f32[16384]{0:T(1024)S(1)} %bitcast_add_fusion), channel_id=1, source_target_pairs={{0,2},{1,3},{2,0},{3,1},{4,6},{5,7},{6,4},{7,5},{8,10},{9,11},{10,... | collective-permute-start | bytes 196616 | tf_op jit(solution)/shard_map/ppermute | solution.py:29
  91.1 2.8 %collective-permute-done.29 = f32[16384]{0:T(1024)S(1)} collective-permute-done((f32[16384]{0:T(1024)S(1)}, f32[16384]{0:T(1024)S(1)}, u32[]{:S(2)}, u32[]{:S(2)}) %collective-permute-start.29) | collective-permute-done | bytes 65568 | tf_op jit(solution)/shard_map/ppermute | solution.py:29
  93.8 1.3 %forward.11 = (f32[128,128]{1,0:T(8,128)S(1)}, f32[1,256]{1,0:T(1,128)S(1)}) custom-call(f32[1,6]{1,0:T(1,128)S(1)} %bitcast.79, f32[128,128]{1,0:T(8,128)S(1)} %bitcast.56, f32[128,128]{1,0:T(8,128)S(1)} %bitcast.62, f32[128,128]{1,0:T(8,128)S(1)} %get-tuple-element.46.refs_3_, f32[192,16384]{1,0:T(8,128)S(1)} %load.1.refs_4_.refs_3_.refs_6_), custom_call_target="tpu_custom_call" | custom-call | tf_op jit(solution)/shard_map/forward/pallas_call | solution.py:165
  95.1 1.5 %collective-permute-start.32 = (f32[256]{0:T(256)S(1)}, f32[256]{0:T(256)S(1)}, u32[]{:S(2)}, u32[]{:S(2)}) collective-permute-start(f32[256]{0:T(256)S(1)} %bitcast.115), channel_id=1, source_target_pairs={{0,12},{1,13},{2,14},{3,15},{4,8},{5,9},{6,10},{7,11},{8,4},{9,5},... | collective-permute-start | bytes 3080 | tf_op jit(solution)/shard_map/ppermute | solution.py:29
  97.5 2.0 %collective-permute-start.30 = (f32[256]{0:T(256)S(1)}, f32[256]{0:T(256)S(1)}, u32[]{:S(2)}, u32[]{:S(2)}) collective-permute-start(f32[256]{0:T(256)S(1)} %bitcast.117), channel_id=1, source_target_pairs={{0,4},{1,5},{2,6},{3,7},{4,0},{5,1},{6,2},{7,3},{8,12},{9,13},{10,... | collective-permute-start | bytes 3080 | tf_op jit(solution)/shard_map/ppermute | solution.py:29
  (46 shorter events, 13.6 us)
Async XLA Ops:
  1.5 10.3 %collective-permute-start.2 = (f32[256]{0:T(256)S(1)}, f32[256]{0:T(256)S(1)}, u32[]{:S(2)}, u32[]{:S(2)}) collective-permute-start(f32[256]{0:T(256)S(1)} %dynamic_update_slice.3), channel_id=1, source_target_pairs={{0,12},{1,13},{2,14},{3,15},{4,8},{5,9},{6,10},{7,11},{8,4},{9,5},... | collective-permute-start | bytes 3080 | tf_op jit(solution)/shard_map/ppermute | solution.py:29
  6.6 5.3 %collective-permute-start.1 = (f32[256]{0:T(256)S(1)}, f32[256]{0:T(256)S(1)}, u32[]{:S(2)}, u32[]{:S(2)}) collective-permute-start(f32[256]{0:T(256)S(1)} %dynamic_update_slice.3), channel_id=1, source_target_pairs={{0,8},{1,9},{2,10},{3,11},{4,12},{5,13},{6,14},{7,15},{8,0},{9,1},... | collective-permute-start | bytes 3080 | tf_op jit(solution)/shard_map/ppermute | solution.py:29
  6.6 5.3 %collective-permute-start = (f32[256]{0:T(256)S(1)}, f32[256]{0:T(256)S(1)}, u32[]{:S(2)}, u32[]{:S(2)}) collective-permute-start(f32[256]{0:T(256)S(1)} %dynamic_update_slice.3), channel_id=1, source_target_pairs={{0,4},{1,5},{2,6},{3,7},{4,0},{5,1},{6,2},{7,3},{8,12},{9,13},{10,... | collective-permute-start | bytes 3080 | tf_op jit(solution)/shard_map/ppermute | solution.py:29
  11.8 6.8 %copy-start = (f32[6]{0:T(128)S(1)}, f32[6]{0:T(128)}, u32[]{:S(2)}) copy-start(f32[6]{0:T(128)} %param.5) | copy-start | bytes 76
  12.9 1.3 %collective-permute-start.3 = (f32[16384]{0:T(1024)S(1)}, f32[16384]{0:T(1024)S(1)}, u32[]{:S(2)}, u32[]{:S(2)}) collective-permute-start(f32[16384]{0:T(1024)S(1)} %bitcast.72), channel_id=1, source_target_pairs={{0,1},{1,0},{2,3},{3,2},{4,5},{5,4},{6,7},{7,6},{8,9},{9,8},{10,11... | collective-permute-start | bytes 196616 | tf_op jit(solution)/shard_map/ppermute | solution.py:29
  14.3 4.3 %collective-permute-start.4 = (f32[16384]{0:T(1024)S(1)}, f32[16384]{0:T(1024)S(1)}, u32[]{:S(2)}, u32[]{:S(2)}) collective-permute-start(f32[16384]{0:T(1024)S(1)} %bitcast_add_fusion.5), channel_id=1, source_target_pairs={{0,2},{1,3},{2,0},{3,1},{4,6},{5,7},{6,4},{7,5},{8,10},{9,11},{10,... | collective-permute-start | bytes 196616 | tf_op jit(solution)/shard_map/ppermute | solution.py:29
  19.9 5.4 %collective-permute-start.7 = (f32[256]{0:T(256)S(1)}, f32[256]{0:T(256)S(1)}, u32[]{:S(2)}, u32[]{:S(2)}) collective-permute-start(f32[256]{0:T(256)S(1)} %bitcast.93), channel_id=1, source_target_pairs={{0,12},{1,13},{2,14},{3,15},{4,8},{5,9},{6,10},{7,11},{8,4},{9,5},... | collective-permute-start | bytes 3080 | tf_op jit(solution)/shard_map/ppermute | solution.py:29
  23.7 4.5 %collective-permute-start.6 = (f32[256]{0:T(256)S(1)}, f32[256]{0:T(256)S(1)}, u32[]{:S(2)}, u32[]{:S(2)}) collective-permute-start(f32[256]{0:T(256)S(1)} %bitcast.94), channel_id=1, source_target_pairs={{0,8},{1,9},{2,10},{3,11},{4,12},{5,13},{6,14},{7,15},{8,0},{9,1},... | collective-permute-start | bytes 3080 | tf_op jit(solution)/shard_map/ppermute | solution.py:29
  23.7 4.5 %collective-permute-start.5 = (f32[256]{0:T(256)S(1)}, f32[256]{0:T(256)S(1)}, u32[]{:S(2)}, u32[]{:S(2)}) collective-permute-start(f32[256]{0:T(256)S(1)} %bitcast.95), channel_id=1, source_target_pairs={{0,4},{1,5},{2,6},{3,7},{4,0},{5,1},{6,2},{7,3},{8,12},{9,13},{10,... | collective-permute-start | bytes 3080 | tf_op jit(solution)/shard_map/ppermute | solution.py:29
  29.4 1.3 %collective-permute-start.8 = (f32[16384]{0:T(1024)S(1)}, f32[16384]{0:T(1024)S(1)}, u32[]{:S(2)}, u32[]{:S(2)}) collective-permute-start(f32[16384]{0:T(1024)S(1)} %bitcast.73), channel_id=1, source_target_pairs={{0,1},{1,0},{2,3},{3,2},{4,5},{5,4},{6,7},{7,6},{8,9},{9,8},{10,11... | collective-permute-start | bytes 196616 | tf_op jit(solution)/shard_map/ppermute | solution.py:29
  30.7 4.3 %collective-permute-start.9 = (f32[16384]{0:T(1024)S(1)}, f32[16384]{0:T(1024)S(1)}, u32[]{:S(2)}, u32[]{:S(2)}) collective-permute-start(f32[16384]{0:T(1024)S(1)} %bitcast_add_fusion.4), channel_id=1, source_target_pairs={{0,2},{1,3},{2,0},{3,1},{4,6},{5,7},{6,4},{7,5},{8,10},{9,11},{10,... | collective-permute-start | bytes 196616 | tf_op jit(solution)/shard_map/ppermute | solution.py:29
  36.3 5.4 %collective-permute-start.12 = (f32[256]{0:T(256)S(1)}, f32[256]{0:T(256)S(1)}, u32[]{:S(2)}, u32[]{:S(2)}) collective-permute-start(f32[256]{0:T(256)S(1)} %bitcast.81), channel_id=1, source_target_pairs={{0,12},{1,13},{2,14},{3,15},{4,8},{5,9},{6,10},{7,11},{8,4},{9,5},... | collective-permute-start | bytes 3080 | tf_op jit(solution)/shard_map/ppermute | solution.py:29
  37.8 4.5 %collective-permute-start.11 = (f32[256]{0:T(256)S(1)}, f32[256]{0:T(256)S(1)}, u32[]{:S(2)}, u32[]{:S(2)}) collective-permute-start(f32[256]{0:T(256)S(1)} %bitcast.82), channel_id=1, source_target_pairs={{0,8},{1,9},{2,10},{3,11},{4,12},{5,13},{6,14},{7,15},{8,0},{9,1},... | collective-permute-start | bytes 3080 | tf_op jit(solution)/shard_map/ppermute | solution.py:29
  38.5 3.8 %collective-permute-start.10 = (f32[256]{0:T(256)S(1)}, f32[256]{0:T(256)S(1)}, u32[]{:S(2)}, u32[]{:S(2)}) collective-permute-start(f32[256]{0:T(256)S(1)} %bitcast.83), channel_id=1, source_target_pairs={{0,4},{1,5},{2,6},{3,7},{4,0},{5,1},{6,2},{7,3},{8,12},{9,13},{10,... | collective-permute-start | bytes 3080 | tf_op jit(solution)/shard_map/ppermute | solution.py:29
  43.5 1.3 %collective-permute-start.13 = (f32[16384]{0:T(1024)S(1)}, f32[16384]{0:T(1024)S(1)}, u32[]{:S(2)}, u32[]{:S(2)}) collective-permute-start(f32[16384]{0:T(1024)S(1)} %bitcast.68), channel_id=1, source_target_pairs={{0,1},{1,0},{2,3},{3,2},{4,5},{5,4},{6,7},{7,6},{8,9},{9,8},{10,11... | collective-permute-start | bytes 196616 | tf_op jit(solution)/shard_map/ppermute | solution.py:29
  44.8 4.3 %collective-permute-start.14 = (f32[16384]{0:T(1024)S(1)}, f32[16384]{0:T(1024)S(1)}, u32[]{:S(2)}, u32[]{:S(2)}) collective-permute-start(f32[16384]{0:T(1024)S(1)} %bitcast_add_fusion.3), channel_id=1, source_target_pairs={{0,2},{1,3},{2,0},{3,1},{4,6},{5,7},{6,4},{7,5},{8,10},{9,11},{10,... | collective-permute-start | bytes 196616 | tf_op jit(solution)/shard_map/ppermute | solution.py:29
  50.4 5.4 %collective-permute-start.17 = (f32[256]{0:T(256)S(1)}, f32[256]{0:T(256)S(1)}, u32[]{:S(2)}, u32[]{:S(2)}) collective-permute-start(f32[256]{0:T(256)S(1)} %bitcast.84), channel_id=1, source_target_pairs={{0,12},{1,13},{2,14},{3,15},{4,8},{5,9},{6,10},{7,11},{8,4},{9,5},... | collective-permute-start | bytes 3080 | tf_op jit(solution)/shard_map/ppermute | solution.py:29
  53.1 4.5 %collective-permute-start.16 = (f32[256]{0:T(256)S(1)}, f32[256]{0:T(256)S(1)}, u32[]{:S(2)}, u32[]{:S(2)}) collective-permute-start(f32[256]{0:T(256)S(1)} %bitcast.85), channel_id=1, source_target_pairs={{0,8},{1,9},{2,10},{3,11},{4,12},{5,13},{6,14},{7,15},{8,0},{9,1},... | collective-permute-start | bytes 3080 | tf_op jit(solution)/shard_map/ppermute | solution.py:29
  54.0 3.6 %collective-permute-start.15 = (f32[256]{0:T(256)S(1)}, f32[256]{0:T(256)S(1)}, u32[]{:S(2)}, u32[]{:S(2)}) collective-permute-start(f32[256]{0:T(256)S(1)} %bitcast.86), channel_id=1, source_target_pairs={{0,4},{1,5},{2,6},{3,7},{4,0},{5,1},{6,2},{7,3},{8,12},{9,13},{10,... | collective-permute-start | bytes 3080 | tf_op jit(solution)/shard_map/ppermute | solution.py:29
  58.8 1.3 %collective-permute-start.18 = (f32[16384]{0:T(1024)S(1)}, f32[16384]{0:T(1024)S(1)}, u32[]{:S(2)}, u32[]{:S(2)}) collective-permute-start(f32[16384]{0:T(1024)S(1)} %bitcast.69), channel_id=1, source_target_pairs={{0,1},{1,0},{2,3},{3,2},{4,5},{5,4},{6,7},{7,6},{8,9},{9,8},{10,11... | collective-permute-start | bytes 196616 | tf_op jit(solution)/shard_map/ppermute | solution.py:29
  60.1 4.3 %collective-permute-start.19 = (f32[16384]{0:T(1024)S(1)}, f32[16384]{0:T(1024)S(1)}, u32[]{:S(2)}, u32[]{:S(2)}) collective-permute-start(f32[16384]{0:T(1024)S(1)} %bitcast_add_fusion.2), channel_id=1, source_target_pairs={{0,2},{1,3},{2,0},{3,1},{4,6},{5,7},{6,4},{7,5},{8,10},{9,11},{10,... | collective-permute-start | bytes 196616 | tf_op jit(solution)/shard_map/ppermute | solution.py:29
  65.7 5.4 %collective-permute-start.22 = (f32[256]{0:T(256)S(1)}, f32[256]{0:T(256)S(1)}, u32[]{:S(2)}, u32[]{:S(2)}) collective-permute-start(f32[256]{0:T(256)S(1)} %bitcast.87), channel_id=1, source_target_pairs={{0,12},{1,13},{2,14},{3,15},{4,8},{5,9},{6,10},{7,11},{8,4},{9,5},... | collective-permute-start | bytes 3080 | tf_op jit(solution)/shard_map/ppermute | solution.py:29
  67.2 4.5 %collective-permute-start.21 = (f32[256]{0:T(256)S(1)}, f32[256]{0:T(256)S(1)}, u32[]{:S(2)}, u32[]{:S(2)}) collective-permute-start(f32[256]{0:T(256)S(1)} %bitcast.88), channel_id=1, source_target_pairs={{0,8},{1,9},{2,10},{3,11},{4,12},{5,13},{6,14},{7,15},{8,0},{9,1},... | collective-permute-start | bytes 3080 | tf_op jit(solution)/shard_map/ppermute | solution.py:29
  68.1 3.6 %collective-permute-start.20 = (f32[256]{0:T(256)S(1)}, f32[256]{0:T(256)S(1)}, u32[]{:S(2)}, u32[]{:S(2)}) collective-permute-start(f32[256]{0:T(256)S(1)} %bitcast.89), channel_id=1, source_target_pairs={{0,4},{1,5},{2,6},{3,7},{4,0},{5,1},{6,2},{7,3},{8,12},{9,13},{10,... | collective-permute-start | bytes 3080 | tf_op jit(solution)/shard_map/ppermute | solution.py:29
  72.9 1.3 %collective-permute-start.23 = (f32[16384]{0:T(1024)S(1)}, f32[16384]{0:T(1024)S(1)}, u32[]{:S(2)}, u32[]{:S(2)}) collective-permute-start(f32[16384]{0:T(1024)S(1)} %bitcast.70), channel_id=1, source_target_pairs={{0,1},{1,0},{2,3},{3,2},{4,5},{5,4},{6,7},{7,6},{8,9},{9,8},{10,11... | collective-permute-start | bytes 196616 | tf_op jit(solution)/shard_map/ppermute | solution.py:29
  74.2 4.3 %collective-permute-start.24 = (f32[16384]{0:T(1024)S(1)}, f32[16384]{0:T(1024)S(1)}, u32[]{:S(2)}, u32[]{:S(2)}) collective-permute-start(f32[16384]{0:T(1024)S(1)} %bitcast_add_fusion.1), channel_id=1, source_target_pairs={{0,2},{1,3},{2,0},{3,1},{4,6},{5,7},{6,4},{7,5},{8,10},{9,11},{10,... | collective-permute-start | bytes 196616 | tf_op jit(solution)/shard_map/ppermute | solution.py:29
  79.8 5.4 %collective-permute-start.27 = (f32[256]{0:T(256)S(1)}, f32[256]{0:T(256)S(1)}, u32[]{:S(2)}, u32[]{:S(2)}) collective-permute-start(f32[256]{0:T(256)S(1)} %bitcast.90), channel_id=1, source_target_pairs={{0,12},{1,13},{2,14},{3,15},{4,8},{5,9},{6,10},{7,11},{8,4},{9,5},... | collective-permute-start | bytes 3080 | tf_op jit(solution)/shard_map/ppermute | solution.py:29
  82.5 4.5 %collective-permute-start.26 = (f32[256]{0:T(256)S(1)}, f32[256]{0:T(256)S(1)}, u32[]{:S(2)}, u32[]{:S(2)}) collective-permute-start(f32[256]{0:T(256)S(1)} %bitcast.91), channel_id=1, source_target_pairs={{0,8},{1,9},{2,10},{3,11},{4,12},{5,13},{6,14},{7,15},{8,0},{9,1},... | collective-permute-start | bytes 3080 | tf_op jit(solution)/shard_map/ppermute | solution.py:29
  83.4 3.6 %collective-permute-start.25 = (f32[256]{0:T(256)S(1)}, f32[256]{0:T(256)S(1)}, u32[]{:S(2)}, u32[]{:S(2)}) collective-permute-start(f32[256]{0:T(256)S(1)} %bitcast.92), channel_id=1, source_target_pairs={{0,4},{1,5},{2,6},{3,7},{4,0},{5,1},{6,2},{7,3},{8,12},{9,13},{10,... | collective-permute-start | bytes 3080 | tf_op jit(solution)/shard_map/ppermute | solution.py:29
  88.2 1.3 %collective-permute-start.28 = (f32[16384]{0:T(1024)S(1)}, f32[16384]{0:T(1024)S(1)}, u32[]{:S(2)}, u32[]{:S(2)}) collective-permute-start(f32[16384]{0:T(1024)S(1)} %bitcast.71), channel_id=1, source_target_pairs={{0,1},{1,0},{2,3},{3,2},{4,5},{5,4},{6,7},{7,6},{8,9},{9,8},{10,11... | collective-permute-start | bytes 196616 | tf_op jit(solution)/shard_map/ppermute | solution.py:29
  89.5 4.3 %collective-permute-start.29 = (f32[16384]{0:T(1024)S(1)}, f32[16384]{0:T(1024)S(1)}, u32[]{:S(2)}, u32[]{:S(2)}) collective-permute-start(f32[16384]{0:T(1024)S(1)} %bitcast_add_fusion), channel_id=1, source_target_pairs={{0,2},{1,3},{2,0},{3,1},{4,6},{5,7},{6,4},{7,5},{8,10},{9,11},{10,... | collective-permute-start | bytes 196616 | tf_op jit(solution)/shard_map/ppermute | solution.py:29
  95.1 5.4 %collective-permute-start.32 = (f32[256]{0:T(256)S(1)}, f32[256]{0:T(256)S(1)}, u32[]{:S(2)}, u32[]{:S(2)}) collective-permute-start(f32[256]{0:T(256)S(1)} %bitcast.115), channel_id=1, source_target_pairs={{0,12},{1,13},{2,14},{3,15},{4,8},{5,9},{6,10},{7,11},{8,4},{9,5},... | collective-permute-start | bytes 3080 | tf_op jit(solution)/shard_map/ppermute | solution.py:29
  96.6 4.5 %collective-permute-start.31 = (f32[256]{0:T(256)S(1)}, f32[256]{0:T(256)S(1)}, u32[]{:S(2)}, u32[]{:S(2)}) collective-permute-start(f32[256]{0:T(256)S(1)} %bitcast.116), channel_id=1, source_target_pairs={{0,8},{1,9},{2,10},{3,11},{4,12},{5,13},{6,14},{7,15},{8,0},{9,1},... | collective-permute-start | bytes 3080 | tf_op jit(solution)/shard_map/ppermute | solution.py:29
  97.5 3.6 %collective-permute-start.30 = (f32[256]{0:T(256)S(1)}, f32[256]{0:T(256)S(1)}, u32[]{:S(2)}, u32[]{:S(2)}) collective-permute-start(f32[256]{0:T(256)S(1)} %bitcast.117), channel_id=1, source_target_pairs={{0,4},{1,5},{2,6},{3,7},{4,0},{5,1},{6,2},{7,3},{8,12},{9,13},{10,... | collective-permute-start | bytes 3080 | tf_op jit(solution)/shard_map/ppermute | solution.py:29

commit v3 on v2

--- a/solution.py
+++ b/solution.py
@@ -60,6 +60,28 @@
     copy = pltpu.make_async_copy(source, target, semaphore)
     copy.start()
     copy.wait()
+
+
+def column_position():
+    return lax.axis_index("row") // (lax.axis_size("row") // COLS)
+
+
+def placed(piece, position, padded):
+    rest = jnp.zeros((1, padded - piece.shape[1]), jnp.float32)
+    return pltpu.roll(jnp.concatenate([piece, rest], axis=1), position * piece.shape[1], 1)
+
+
+def new_residual(pieces, measured, old, rows, all_rows):
+    total = column_total([piece[...] for piece in pieces])
+    onsager = total[:, rows : rows + 1] / all_rows
+    return measured[...] - total + onsager * old[...]
+
+
+def last_kernel(rows, all_rows, *refs):
+    *pieces, measured, old, out = refs
+    residual = new_residual(pieces, measured, old, rows, all_rows)
+    padded, own = residual.shape[1], out.shape[1]
+    out[...] = pltpu.roll(residual, padded - column_position() * own, 1)[:, :own]
 
 
 def back_kernel(first, rows, all_rows, *refs):
@@ -198,12 +220,16 @@
         )
         estimate = (new_estimate,)
         parts = all_columns(product)
-    total = column_total(parts)[0]
-    onsager = total[rows] / all_rows
-    final = measured_row[0] - total + onsager * others[1][0]
+    residual = pl.pallas_call(
+        functools.partial(last_kernel, rows, all_rows),
+        out_shape=jax.ShapeDtypeStruct((1, local_rows), jnp.float32),
+        in_specs=[in_vmem] * (len(parts) + len(others)),
+        out_specs=in_vmem,
+        compiler_params=params,
+        name="last",
+    )(*parts, *others)
     estimate = lax.dynamic_slice_in_dim(estimate[0].reshape(width), group_pos * share, share)
-    residual = lax.dynamic_slice_in_dim(final, column_pos * local_rows, local_rows)
-    return (estimate, residual)
+    return (estimate, residual.reshape(local_rows))
 
 
 def solution(mesh):

time: 103 us -> 102 us (level)
  transfers between devices with their start and end apart: 33 -> 33, of which waited for: 24 -> 24; matrix products, arithmetic and copies ran while one was open for 1% -> 1% of each run, Pallas kernels for 4% -> 5%
where the time goes in v3:
time: 102 us
  starting transfers between devices  42.3 us (41%)
  waiting for transfers between devices  37.1 us (36%)
  Pallas kernels  19.9 us (20%)
  local copies, waits for them, and re-layouts  1.47 us (1%)
    ppermute x33, starting transfers between devices, swapped(): return lax.ppermute(value, 'row', pairs)  42.3 us
    ppermute x33, waiting for transfers between devices, swapped(): return lax.ppermute(value, 'row', pairs)  37.1 us
    pallas_call x6, Pallas kernels, forward(): pl.pallas_call(functools.partial(forward_kernel, first, rows, step), out_...  7.59 us
    pallas_call x6, Pallas kernels, back(): pl.pallas_call(functools.partial(back_kernel, first, rows, all_rows), out...  7.04 us
    pallas_call x1, Pallas kernels, on_device(): pl.pallas_call(load_kernel, out_shape=VMEM(sensing.shape, sensing.dtype),...  4.58 us
  transfers between devices with their start and end apart: 33, of which 24 were waited for; matrix products, arithmetic and copies ran while one was open for 1% of the time, Pallas kernels for 5%

profile of v3, /device:TPU:0, one launch (start us, length us, event | category | flops | bytes accessed | tf_op | source)
XLA Modules:
  0.0 101.8 jit_solution(14924384844519755267)
XLA Ops:
  1.5 5.1 %collective-permute-start.2 = (f32[256]{0:T(256)S(1)}, f32[256]{0:T(256)S(1)}, u32[]{:S(2)}, u32[]{:S(2)}) collective-permute-start(f32[256]{0:T(256)S(1)} %dynamic_update_slice.3), channel_id=1, source_target_pairs={{0,12},{1,13},{2,14},{3,15},{4,8},{5,9},{6,10},{7,11},{8,4},{9,5},... | collective-permute-start | bytes 3080 | tf_op jit(solution)/shard_map/ppermute | solution.py:29
  7.2 4.6 %load.1.refs_4_.refs_3_.refs_6_ = f32[192,16384]{1,0:T(8,128)S(1)} custom-call(f32[192,16384]{1,0:T(8,128)} %source.1), custom_call_target="tpu_custom_call" | custom-call | bytes 25165824 | tf_op jit(solution)/shard_map/load/pallas_call | solution.py:160
  11.9 1.1 %back.6 = (f32[128,128]{1,0:T(8,128)S(1)}, f32[1,256]{1,0:T(1,128)S(1)}) custom-call(f32[1,256]{1,0:T(1,128)S(1)} %bitcast.113, f32[1,256]{1,0:T(1,128)S(1)} %bitcast.111, f32[1,256]{1,0:T(1,128)S(1)} %bitcast.105, f32[1,256]{1,0:T(1,128)S(1)} %bitcast.99, f32[192,16384]{1,0:T(8,128)S(1)} %load.1.refs_4_.refs_3_.refs_6_), custom_call_target="tpu_custom_call" | custom-call | tf_op jit(solution)/shard_map/back/pallas_call | solution.py:177
  13.0 1.2 %collective-permute-done.3 = f32[16384]{0:T(1024)S(1)} collective-permute-done((f32[16384]{0:T(1024)S(1)}, f32[16384]{0:T(1024)S(1)}, u32[]{:S(2)}, u32[]{:S(2)}) %collective-permute-start.3) | collective-permute-done | bytes 65568 | tf_op jit(solution)/shard_map/ppermute | solution.py:29
  14.3 1.7 %collective-permute-start.4 = (f32[16384]{0:T(1024)S(1)}, f32[16384]{0:T(1024)S(1)}, u32[]{:S(2)}, u32[]{:S(2)}) collective-permute-start(f32[16384]{0:T(1024)S(1)} %bitcast_add_fusion.5), channel_id=1, source_target_pairs={{0,2},{1,3},{2,0},{3,1},{4,6},{5,7},{6,4},{7,5},{8,10},{9,11},{10,... | collective-permute-start | bytes 196616 | tf_op jit(solution)/shard_map/ppermute | solution.py:29
  16.0 2.6 %collective-permute-done.4 = f32[16384]{0:T(1024)S(1)} collective-permute-done((f32[16384]{0:T(1024)S(1)}, f32[16384]{0:T(1024)S(1)}, u32[]{:S(2)}, u32[]{:S(2)}) %collective-permute-start.4) | collective-permute-done | bytes 65568 | tf_op jit(solution)/shard_map/ppermute | solution.py:29
  18.6 1.3 %forward.6 = (f32[128,128]{1,0:T(8,128)S(1)}, f32[1,256]{1,0:T(1,128)S(1)}) custom-call(f32[1,6]{1,0:T(1,128)S(1)} %bitcast.73, f32[128,128]{1,0:T(8,128)S(1)} %bitcast.60, f32[128,128]{1,0:T(8,128)S(1)} %bitcast.66, f32[192,16384]{1,0:T(8,128)S(1)} %load.1.refs_4_.refs_3_.refs_6_), custom_call_target="tpu_custom_call" | custom-call | tf_op jit(solution)/shard_map/forward/pallas_call | solution.py:187
  19.9 3.8 %collective-permute-start.7 = (f32[256]{0:T(256)S(1)}, f32[256]{0:T(256)S(1)}, u32[]{:S(2)}, u32[]{:S(2)}) collective-permute-start(f32[256]{0:T(256)S(1)} %bitcast.92), channel_id=1, source_target_pairs={{0,12},{1,13},{2,14},{3,15},{4,8},{5,9},{6,10},{7,11},{8,4},{9,5},... | collective-permute-start | bytes 3080 | tf_op jit(solution)/shard_map/ppermute | solution.py:29
  24.3 1.0 collective-permute-done.7
  25.3 2.8 %collective-permute-done.6 = f32[256]{0:T(256)S(1)} collective-permute-done((f32[256]{0:T(256)S(1)}, f32[256]{0:T(256)S(1)}, u32[]{:S(2)}, u32[]{:S(2)}) %collective-permute-start.6) | collective-permute-done | bytes 1056 | tf_op jit(solution)/shard_map/ppermute | solution.py:29
  28.1 1.2 %back.7 = (f32[128,128]{1,0:T(8,128)S(1)}, f32[1,256]{1,0:T(1,128)S(1)}) custom-call(f32[1,256]{1,0:T(1,128)S(1)} %get-tuple-element.27.refs_0_, f32[1,256]{1,0:T(1,128)S(1)} %bitcast.112, f32[1,256]{1,0:T(1,128)S(1)} %bitcast.106, f32[1,256]{1,0:T(1,128)S(1)} %bitcast.100, f32[1,256]{1,0:T(1,128)S(1)} %get-tuple-element.28.refs_4_.refs_5_, ...), custom_call_target="tpu_custom_call" | custom-call | tf_op jit(solution)/shard_map/back/pallas_call | solution.py:177
  29.4 1.2 %collective-permute-done.8 = f32[16384]{0:T(1024)S(1)} collective-permute-done((f32[16384]{0:T(1024)S(1)}, f32[16384]{0:T(1024)S(1)}, u32[]{:S(2)}, u32[]{:S(2)}) %collective-permute-start.8) | collective-permute-done | bytes 65568 | tf_op jit(solution)/shard_map/ppermute | solution.py:29
  30.7 1.6 %collective-permute-start.9 = (f32[16384]{0:T(1024)S(1)}, f32[16384]{0:T(1024)S(1)}, u32[]{:S(2)}, u32[]{:S(2)}) collective-permute-start(f32[16384]{0:T(1024)S(1)} %bitcast_add_fusion.4), channel_id=1, source_target_pairs={{0,2},{1,3},{2,0},{3,1},{4,6},{5,7},{6,4},{7,5},{8,10},{9,11},{10,... | collective-permute-start | bytes 196616 | tf_op jit(solution)/shard_map/ppermute | solution.py:29
  32.2 2.8 %collective-permute-done.9 = f32[16384]{0:T(1024)S(1)} collective-permute-done((f32[16384]{0:T(1024)S(1)}, f32[16384]{0:T(1024)S(1)}, u32[]{:S(2)}, u32[]{:S(2)}) %collective-permute-start.9) | collective-permute-done | bytes 65568 | tf_op jit(solution)/shard_map/ppermute | solution.py:29
  35.0 1.3 %forward.7 = (f32[128,128]{1,0:T(8,128)S(1)}, f32[1,256]{1,0:T(1,128)S(1)}) custom-call(f32[1,6]{1,0:T(1,128)S(1)} %bitcast.74, f32[128,128]{1,0:T(8,128)S(1)} %bitcast.56, f32[128,128]{1,0:T(8,128)S(1)} %bitcast.62, f32[128,128]{1,0:T(8,128)S(1)} %get-tuple-element.30.refs_3_, f32[192,16384]{1,0:T(8,128)S(1)} %load.1.refs_4_.refs_3_.refs_6_), custom_call_target="tpu_custom_call" | custom-call | tf_op jit(solution)/shard_map/forward/pallas_call | solution.py:187
  36.3 1.5 %collective-permute-start.12 = (f32[256]{0:T(256)S(1)}, f32[256]{0:T(256)S(1)}, u32[]{:S(2)}, u32[]{:S(2)}) collective-permute-start(f32[256]{0:T(256)S(1)} %bitcast.80), channel_id=1, source_target_pairs={{0,12},{1,13},{2,14},{3,15},{4,8},{5,9},{6,10},{7,11},{8,4},{9,5},... | collective-permute-start | bytes 3080 | tf_op jit(solution)/shard_map/ppermute | solution.py:29
  38.5 2.3 %collective-permute-start.10 = (f32[256]{0:T(256)S(1)}, f32[256]{0:T(256)S(1)}, u32[]{:S(2)}, u32[]{:S(2)}) collective-permute-start(f32[256]{0:T(256)S(1)} %bitcast.82), channel_id=1, source_target_pairs={{0,4},{1,5},{2,6},{3,7},{4,0},{5,1},{6,2},{7,3},{8,12},{9,13},{10,... | collective-permute-start | bytes 3080 | tf_op jit(solution)/shard_map/ppermute | solution.py:29
  40.7 1.0 collective-permute-done.12
  42.3 1.2 %back.8 = (f32[128,128]{1,0:T(8,128)S(1)}, f32[1,256]{1,0:T(1,128)S(1)}) custom-call(f32[1,256]{1,0:T(1,128)S(1)} %get-tuple-element.31.refs_0_, f32[1,256]{1,0:T(1,128)S(1)} %bitcast.107, f32[1,256]{1,0:T(1,128)S(1)} %bitcast.101, f32[1,256]{1,0:T(1,128)S(1)} %bitcast.95, f32[1,256]{1,0:T(1,128)S(1)} %get-tuple-element.28.refs_4_.refs_5_, ...), custom_call_target="tpu_custom_call" | custom-call | tf_op jit(solution)/shard_map/back/pallas_call | solution.py:177
  43.6 1.2 %collective-permute-done.13 = f32[16384]{0:T(1024)S(1)} collective-permute-done((f32[16384]{0:T(1024)S(1)}, f32[16384]{0:T(1024)S(1)}, u32[]{:S(2)}, u32[]{:S(2)}) %collective-permute-start.13) | collective-permute-done | bytes 65568 | tf_op jit(solution)/shard_map/ppermute | solution.py:29
  44.8 1.6 %collective-permute-start.14 = (f32[16384]{0:T(1024)S(1)}, f32[16384]{0:T(1024)S(1)}, u32[]{:S(2)}, u32[]{:S(2)}) collective-permute-start(f32[16384]{0:T(1024)S(1)} %bitcast_add_fusion.3), channel_id=1, source_target_pairs={{0,2},{1,3},{2,0},{3,1},{4,6},{5,7},{6,4},{7,5},{8,10},{9,11},{10,... | collective-permute-start | bytes 196616 | tf_op jit(solution)/shard_map/ppermute | solution.py:29
  46.4 2.8 %collective-permute-done.14 = f32[16384]{0:T(1024)S(1)} collective-permute-done((f32[16384]{0:T(1024)S(1)}, f32[16384]{0:T(1024)S(1)}, u32[]{:S(2)}, u32[]{:S(2)}) %collective-permute-start.14) | collective-permute-done | bytes 65568 | tf_op jit(solution)/shard_map/ppermute | solution.py:29
  49.2 1.3 %forward.8 = (f32[128,128]{1,0:T(8,128)S(1)}, f32[1,256]{1,0:T(1,128)S(1)}) custom-call(f32[1,6]{1,0:T(1,128)S(1)} %bitcast.75, f32[128,128]{1,0:T(8,128)S(1)} %bitcast.57, f32[128,128]{1,0:T(8,128)S(1)} %bitcast.63, f32[128,128]{1,0:T(8,128)S(1)} %get-tuple-element.34.refs_3_, f32[192,16384]{1,0:T(8,128)S(1)} %load.1.refs_4_.refs_3_.refs_6_), custom_call_target="tpu_custom_call" | custom-call | tf_op jit(solution)/shard_map/forward/pallas_call | solution.py:187
  50.4 2.6 %collective-permute-start.17 = (f32[256]{0:T(256)S(1)}, f32[256]{0:T(256)S(1)}, u32[]{:S(2)}, u32[]{:S(2)}) collective-permute-start(f32[256]{0:T(256)S(1)} %bitcast.83), channel_id=1, source_target_pairs={{0,12},{1,13},{2,14},{3,15},{4,8},{5,9},{6,10},{7,11},{8,4},{9,5},... | collective-permute-start | bytes 3080 | tf_op jit(solution)/shard_map/ppermute | solution.py:29
  55.9 1.7 %collective-permute-done.16 = f32[256]{0:T(256)S(1)} collective-permute-done((f32[256]{0:T(256)S(1)}, f32[256]{0:T(256)S(1)}, u32[]{:S(2)}, u32[]{:S(2)}) %collective-permute-start.16) | collective-permute-done | bytes 1056 | tf_op jit(solution)/shard_map/ppermute | solution.py:29
  57.5 1.2 %back.9 = (f32[128,128]{1,0:T(8,128)S(1)}, f32[1,256]{1,0:T(1,128)S(1)}) custom-call(f32[1,256]{1,0:T(1,128)S(1)} %get-tuple-element.35.refs_0_, f32[1,256]{1,0:T(1,128)S(1)} %bitcast.108, f32[1,256]{1,0:T(1,128)S(1)} %bitcast.102, f32[1,256]{1,0:T(1,128)S(1)} %bitcast.96, f32[1,256]{1,0:T(1,128)S(1)} %get-tuple-element.28.refs_4_.refs_5_, ...), custom_call_target="tpu_custom_call" | custom-call | tf_op jit(solution)/shard_map/back/pallas_call | solution.py:177
  58.8 1.2 %collective-permute-done.18 = f32[16384]{0:T(1024)S(1)} collective-permute-done((f32[16384]{0:T(1024)S(1)}, f32[16384]{0:T(1024)S(1)}, u32[]{:S(2)}, u32[]{:S(2)}) %collective-permute-start.18) | collective-permute-done | bytes 65568 | tf_op jit(solution)/shard_map/ppermute | solution.py:29
  60.1 1.6 %collective-permute-start.19 = (f32[16384]{0:T(1024)S(1)}, f32[16384]{0:T(1024)S(1)}, u32[]{:S(2)}, u32[]{:S(2)}) collective-permute-start(f32[16384]{0:T(1024)S(1)} %bitcast_add_fusion.2), channel_id=1, source_target_pairs={{0,2},{1,3},{2,0},{3,1},{4,6},{5,7},{6,4},{7,5},{8,10},{9,11},{10,... | collective-permute-start | bytes 196616 | tf_op jit(solution)/shard_map/ppermute | solution.py:29
  61.6 2.8 %collective-permute-done.19 = f32[16384]{0:T(1024)S(1)} collective-permute-done((f32[16384]{0:T(1024)S(1)}, f32[16384]{0:T(1024)S(1)}, u32[]{:S(2)}, u32[]{:S(2)}) %collective-permute-start.19) | collective-permute-done | bytes 65568 | tf_op jit(solution)/shard_map/ppermute | solution.py:29
  64.4 1.3 %forward.9 = (f32[128,128]{1,0:T(8,128)S(1)}, f32[1,256]{1,0:T(1,128)S(1)}) custom-call(f32[1,6]{1,0:T(1,128)S(1)} %bitcast.76, f32[128,128]{1,0:T(8,128)S(1)} %bitcast.58, f32[128,128]{1,0:T(8,128)S(1)} %bitcast.64, f32[128,128]{1,0:T(8,128)S(1)} %get-tuple-element.38.refs_3_, f32[192,16384]{1,0:T(8,128)S(1)} %load.1.refs_4_.refs_3_.refs_6_), custom_call_target="tpu_custom_call" | custom-call | tf_op jit(solution)/shard_map/forward/pallas_call | solution.py:187
  65.7 1.5 %collective-permute-start.22 = (f32[256]{0:T(256)S(1)}, f32[256]{0:T(256)S(1)}, u32[]{:S(2)}, u32[]{:S(2)}) collective-permute-start(f32[256]{0:T(256)S(1)} %bitcast.86), channel_id=1, source_target_pairs={{0,12},{1,13},{2,14},{3,15},{4,8},{5,9},{6,10},{7,11},{8,4},{9,5},... | collective-permute-start | bytes 3080 | tf_op jit(solution)/shard_map/ppermute | solution.py:29
  68.1 2.0 %collective-permute-start.20 = (f32[256]{0:T(256)S(1)}, f32[256]{0:T(256)S(1)}, u32[]{:S(2)}, u32[]{:S(2)}) collective-permute-start(f32[256]{0:T(256)S(1)} %bitcast.88), channel_id=1, source_target_pairs={{0,4},{1,5},{2,6},{3,7},{4,0},{5,1},{6,2},{7,3},{8,12},{9,13},{10,... | collective-permute-start | bytes 3080 | tf_op jit(solution)/shard_map/ppermute | solution.py:29
  70.2 1.0 collective-permute-done.22
  71.7 1.2 %back.10 = (f32[128,128]{1,0:T(8,128)S(1)}, f32[1,256]{1,0:T(1,128)S(1)}) custom-call(f32[1,256]{1,0:T(1,128)S(1)} %get-tuple-element.39.refs_0_, f32[1,256]{1,0:T(1,128)S(1)} %bitcast.109, f32[1,256]{1,0:T(1,128)S(1)} %bitcast.103, f32[1,256]{1,0:T(1,128)S(1)} %bitcast.97, f32[1,256]{1,0:T(1,128)S(1)} %get-tuple-element.28.refs_4_.refs_5_, ...), custom_call_target="tpu_custom_call" | custom-call | tf_op jit(solution)/shard_map/back/pallas_call | solution.py:177
  73.0 1.2 %collective-permute-done.23 = f32[16384]{0:T(1024)S(1)} collective-permute-done((f32[16384]{0:T(1024)S(1)}, f32[16384]{0:T(1024)S(1)}, u32[]{:S(2)}, u32[]{:S(2)}) %collective-permute-start.23) | collective-permute-done | bytes 65568 | tf_op jit(solution)/shard_map/ppermute | solution.py:29
  74.2 1.6 %collective-permute-start.24 = (f32[16384]{0:T(1024)S(1)}, f32[16384]{0:T(1024)S(1)}, u32[]{:S(2)}, u32[]{:S(2)}) collective-permute-start(f32[16384]{0:T(1024)S(1)} %bitcast_add_fusion.1), channel_id=1, source_target_pairs={{0,2},{1,3},{2,0},{3,1},{4,6},{5,7},{6,4},{7,5},{8,10},{9,11},{10,... | collective-permute-start | bytes 196616 | tf_op jit(solution)/shard_map/ppermute | solution.py:29
  75.8 2.8 %collective-permute-done.24 = f32[16384]{0:T(1024)S(1)} collective-permute-done((f32[16384]{0:T(1024)S(1)}, f32[16384]{0:T(1024)S(1)}, u32[]{:S(2)}, u32[]{:S(2)}) %collective-permute-start.24) | collective-permute-done | bytes 65568 | tf_op jit(solution)/shard_map/ppermute | solution.py:29
  78.6 1.3 %forward.10 = (f32[128,128]{1,0:T(8,128)S(1)}, f32[1,256]{1,0:T(1,128)S(1)}) custom-call(f32[1,6]{1,0:T(1,128)S(1)} %bitcast.77, f32[128,128]{1,0:T(8,128)S(1)} %bitcast.59, f32[128,128]{1,0:T(8,128)S(1)} %bitcast.65, f32[128,128]{1,0:T(8,128)S(1)} %get-tuple-element.42.refs_3_, f32[192,16384]{1,0:T(8,128)S(1)} %load.1.refs_4_.refs_3_.refs_6_), custom_call_target="tpu_custom_call" | custom-call | tf_op jit(solution)/shard_map/forward/pallas_call | solution.py:187
  79.8 2.6 %collective-permute-start.27 = (f32[256]{0:T(256)S(1)}, f32[256]{0:T(256)S(1)}, u32[]{:S(2)}, u32[]{:S(2)}) collective-permute-start(f32[256]{0:T(256)S(1)} %bitcast.89), channel_id=1, source_target_pairs={{0,12},{1,13},{2,14},{3,15},{4,8},{5,9},{6,10},{7,11},{8,4},{9,5},... | collective-permute-start | bytes 3080 | tf_op jit(solution)/shard_map/ppermute | solution.py:29
  84.3 1.0 collective-permute-done.27
  85.3 1.7 %collective-permute-done.26 = f32[256]{0:T(256)S(1)} collective-permute-done((f32[256]{0:T(256)S(1)}, f32[256]{0:T(256)S(1)}, u32[]{:S(2)}, u32[]{:S(2)}) %collective-permute-start.26) | collective-permute-done | bytes 1056 | tf_op jit(solution)/shard_map/ppermute | solution.py:29
  87.0 1.2 %back.11 = (f32[128,128]{1,0:T(8,128)S(1)}, f32[1,256]{1,0:T(1,128)S(1)}) custom-call(f32[1,256]{1,0:T(1,128)S(1)} %get-tuple-element.43.refs_0_, f32[1,256]{1,0:T(1,128)S(1)} %bitcast.110, f32[1,256]{1,0:T(1,128)S(1)} %bitcast.104, f32[1,256]{1,0:T(1,128)S(1)} %bitcast.98, f32[1,256]{1,0:T(1,128)S(1)} %get-tuple-element.28.refs_4_.refs_5_, ...), custom_call_target="tpu_custom_call" | custom-call | tf_op jit(solution)/shard_map/back/pallas_call | solution.py:177
  88.2 1.2 %collective-permute-done.28 = f32[16384]{0:T(1024)S(1)} collective-permute-done((f32[16384]{0:T(1024)S(1)}, f32[16384]{0:T(1024)S(1)}, u32[]{:S(2)}, u32[]{:S(2)}) %collective-permute-start.28) | collective-permute-done | bytes 65568 | tf_op jit(solution)/shard_map/ppermute | solution.py:29
  89.5 1.6 %collective-permute-start.29 = (f32[16384]{0:T(1024)S(1)}, f32[16384]{0:T(1024)S(1)}, u32[]{:S(2)}, u32[]{:S(2)}) collective-permute-start(f32[16384]{0:T(1024)S(1)} %bitcast_add_fusion), channel_id=1, source_target_pairs={{0,2},{1,3},{2,0},{3,1},{4,6},{5,7},{6,4},{7,5},{8,10},{9,11},{10,... | collective-permute-start | bytes 196616 | tf_op jit(solution)/shard_map/ppermute | solution.py:29
  91.1 2.8 %collective-permute-done.29 = f32[16384]{0:T(1024)S(1)} collective-permute-done((f32[16384]{0:T(1024)S(1)}, f32[16384]{0:T(1024)S(1)}, u32[]{:S(2)}, u32[]{:S(2)}) %collective-permute-start.29) | collective-permute-done | bytes 65568 | tf_op jit(solution)/shard_map/ppermute | solution.py:29
  93.8 1.3 %forward.11 = (f32[128,128]{1,0:T(8,128)S(1)}, f32[1,256]{1,0:T(1,128)S(1)}) custom-call(f32[1,6]{1,0:T(1,128)S(1)} %bitcast.78, f32[128,128]{1,0:T(8,128)S(1)} %bitcast.55, f32[128,128]{1,0:T(8,128)S(1)} %bitcast.61, f32[128,128]{1,0:T(8,128)S(1)} %get-tuple-element.46.refs_3_, f32[192,16384]{1,0:T(8,128)S(1)} %load.1.refs_4_.refs_3_.refs_6_), custom_call_target="tpu_custom_call" | custom-call | tf_op jit(solution)/shard_map/forward/pallas_call | solution.py:187
  95.1 1.5 %collective-permute-start.32 = (f32[256]{0:T(256)S(1)}, f32[256]{0:T(256)S(1)}, u32[]{:S(2)}, u32[]{:S(2)}) collective-permute-start(f32[256]{0:T(256)S(1)} %bitcast.114), channel_id=1, source_target_pairs={{0,12},{1,13},{2,14},{3,15},{4,8},{5,9},{6,10},{7,11},{8,4},{9,5},... | collective-permute-start | bytes 3080 | tf_op jit(solution)/shard_map/ppermute | solution.py:29
  97.5 2.0 %collective-permute-start.30 = (f32[256]{0:T(256)S(1)}, f32[256]{0:T(256)S(1)}, u32[]{:S(2)}, u32[]{:S(2)}) collective-permute-start(f32[256]{0:T(256)S(1)} %bitcast.116), channel_id=1, source_target_pairs={{0,4},{1,5},{2,6},{3,7},{4,0},{5,1},{6,2},{7,3},{8,12},{9,13},{10,... | collective-permute-start | bytes 3080 | tf_op jit(solution)/shard_map/ppermute | solution.py:29
  (43 shorter events, 13.1 us)
Async XLA Ops:
  1.5 10.3 %collective-permute-start.2 = (f32[256]{0:T(256)S(1)}, f32[256]{0:T(256)S(1)}, u32[]{:S(2)}, u32[]{:S(2)}) collective-permute-start(f32[256]{0:T(256)S(1)} %dynamic_update_slice.3), channel_id=1, source_target_pairs={{0,12},{1,13},{2,14},{3,15},{4,8},{5,9},{6,10},{7,11},{8,4},{9,5},... | collective-permute-start | bytes 3080 | tf_op jit(solution)/shard_map/ppermute | solution.py:29
  6.6 5.3 %collective-permute-start.1 = (f32[256]{0:T(256)S(1)}, f32[256]{0:T(256)S(1)}, u32[]{:S(2)}, u32[]{:S(2)}) collective-permute-start(f32[256]{0:T(256)S(1)} %dynamic_update_slice.3), channel_id=1, source_target_pairs={{0,8},{1,9},{2,10},{3,11},{4,12},{5,13},{6,14},{7,15},{8,0},{9,1},... | collective-permute-start | bytes 3080 | tf_op jit(solution)/shard_map/ppermute | solution.py:29
  6.6 5.3 %collective-permute-start = (f32[256]{0:T(256)S(1)}, f32[256]{0:T(256)S(1)}, u32[]{:S(2)}, u32[]{:S(2)}) collective-permute-start(f32[256]{0:T(256)S(1)} %dynamic_update_slice.3), channel_id=1, source_target_pairs={{0,4},{1,5},{2,6},{3,7},{4,0},{5,1},{6,2},{7,3},{8,12},{9,13},{10,... | collective-permute-start | bytes 3080 | tf_op jit(solution)/shard_map/ppermute | solution.py:29
  11.8 6.8 %copy-start = (f32[6]{0:T(128)S(1)}, f32[6]{0:T(128)}, u32[]{:S(2)}) copy-start(f32[6]{0:T(128)} %param.5) | copy-start | bytes 76
  12.9 1.3 %collective-permute-start.3 = (f32[16384]{0:T(1024)S(1)}, f32[16384]{0:T(1024)S(1)}, u32[]{:S(2)}, u32[]{:S(2)}) collective-permute-start(f32[16384]{0:T(1024)S(1)} %bitcast.71), channel_id=1, source_target_pairs={{0,1},{1,0},{2,3},{3,2},{4,5},{5,4},{6,7},{7,6},{8,9},{9,8},{10,11... | collective-permute-start | bytes 196616 | tf_op jit(solution)/shard_map/ppermute | solution.py:29
  14.3 4.3 %collective-permute-start.4 = (f32[16384]{0:T(1024)S(1)}, f32[16384]{0:T(1024)S(1)}, u32[]{:S(2)}, u32[]{:S(2)}) collective-permute-start(f32[16384]{0:T(1024)S(1)} %bitcast_add_fusion.5), channel_id=1, source_target_pairs={{0,2},{1,3},{2,0},{3,1},{4,6},{5,7},{6,4},{7,5},{8,10},{9,11},{10,... | collective-permute-start | bytes 196616 | tf_op jit(solution)/shard_map/ppermute | solution.py:29
  19.9 5.4 %collective-permute-start.7 = (f32[256]{0:T(256)S(1)}, f32[256]{0:T(256)S(1)}, u32[]{:S(2)}, u32[]{:S(2)}) collective-permute-start(f32[256]{0:T(256)S(1)} %bitcast.92), channel_id=1, source_target_pairs={{0,12},{1,13},{2,14},{3,15},{4,8},{5,9},{6,10},{7,11},{8,4},{9,5},... | collective-permute-start | bytes 3080 | tf_op jit(solution)/shard_map/ppermute | solution.py:29
  23.7 4.5 %collective-permute-start.6 = (f32[256]{0:T(256)S(1)}, f32[256]{0:T(256)S(1)}, u32[]{:S(2)}, u32[]{:S(2)}) collective-permute-start(f32[256]{0:T(256)S(1)} %bitcast.93), channel_id=1, source_target_pairs={{0,8},{1,9},{2,10},{3,11},{4,12},{5,13},{6,14},{7,15},{8,0},{9,1},... | collective-permute-start | bytes 3080 | tf_op jit(solution)/shard_map/ppermute | solution.py:29
  23.7 4.5 %collective-permute-start.5 = (f32[256]{0:T(256)S(1)}, f32[256]{0:T(256)S(1)}, u32[]{:S(2)}, u32[]{:S(2)}) collective-permute-start(f32[256]{0:T(256)S(1)} %bitcast.94), channel_id=1, source_target_pairs={{0,4},{1,5},{2,6},{3,7},{4,0},{5,1},{6,2},{7,3},{8,12},{9,13},{10,... | collective-permute-start | bytes 3080 | tf_op jit(solution)/shard_map/ppermute | solution.py:29
  29.4 1.3 %collective-permute-start.8 = (f32[16384]{0:T(1024)S(1)}, f32[16384]{0:T(1024)S(1)}, u32[]{:S(2)}, u32[]{:S(2)}) collective-permute-start(f32[16384]{0:T(1024)S(1)} %bitcast.72), channel_id=1, source_target_pairs={{0,1},{1,0},{2,3},{3,2},{4,5},{5,4},{6,7},{7,6},{8,9},{9,8},{10,11... | collective-permute-start | bytes 196616 | tf_op jit(solution)/shard_map/ppermute | solution.py:29
  30.7 4.3 %collective-permute-start.9 = (f32[16384]{0:T(1024)S(1)}, f32[16384]{0:T(1024)S(1)}, u32[]{:S(2)}, u32[]{:S(2)}) collective-permute-start(f32[16384]{0:T(1024)S(1)} %bitcast_add_fusion.4), channel_id=1, source_target_pairs={{0,2},{1,3},{2,0},{3,1},{4,6},{5,7},{6,4},{7,5},{8,10},{9,11},{10,... | collective-permute-start | bytes 196616 | tf_op jit(solution)/shard_map/ppermute | solution.py:29
  36.3 5.4 %collective-permute-start.12 = (f32[256]{0:T(256)S(1)}, f32[256]{0:T(256)S(1)}, u32[]{:S(2)}, u32[]{:S(2)}) collective-permute-start(f32[256]{0:T(256)S(1)} %bitcast.80), channel_id=1, source_target_pairs={{0,12},{1,13},{2,14},{3,15},{4,8},{5,9},{6,10},{7,11},{8,4},{9,5},... | collective-permute-start | bytes 3080 | tf_op jit(solution)/shard_map/ppermute | solution.py:29
  37.8 4.5 %collective-permute-start.11 = (f32[256]{0:T(256)S(1)}, f32[256]{0:T(256)S(1)}, u32[]{:S(2)}, u32[]{:S(2)}) collective-permute-start(f32[256]{0:T(256)S(1)} %bitcast.81), channel_id=1, source_target_pairs={{0,8},{1,9},{2,10},{3,11},{4,12},{5,13},{6,14},{7,15},{8,0},{9,1},... | collective-permute-start | bytes 3080 | tf_op jit(solution)/shard_map/ppermute | solution.py:29
  38.5 3.8 %collective-permute-start.10 = (f32[256]{0:T(256)S(1)}, f32[256]{0:T(256)S(1)}, u32[]{:S(2)}, u32[]{:S(2)}) collective-permute-start(f32[256]{0:T(256)S(1)} %bitcast.82), channel_id=1, source_target_pairs={{0,4},{1,5},{2,6},{3,7},{4,0},{5,1},{6,2},{7,3},{8,12},{9,13},{10,... | collective-permute-start | bytes 3080 | tf_op jit(solution)/shard_map/ppermute | solution.py:29
  43.5 1.3 %collective-permute-start.13 = (f32[16384]{0:T(1024)S(1)}, f32[16384]{0:T(1024)S(1)}, u32[]{:S(2)}, u32[]{:S(2)}) collective-permute-start(f32[16384]{0:T(1024)S(1)} %bitcast.67), channel_id=1, source_target_pairs={{0,1},{1,0},{2,3},{3,2},{4,5},{5,4},{6,7},{7,6},{8,9},{9,8},{10,11... | collective-permute-start | bytes 196616 | tf_op jit(solution)/shard_map/ppermute | solution.py:29
  44.8 4.3 %collective-permute-start.14 = (f32[16384]{0:T(1024)S(1)}, f32[16384]{0:T(1024)S(1)}, u32[]{:S(2)}, u32[]{:S(2)}) collective-permute-start(f32[16384]{0:T(1024)S(1)} %bitcast_add_fusion.3), channel_id=1, source_target_pairs={{0,2},{1,3},{2,0},{3,1},{4,6},{5,7},{6,4},{7,5},{8,10},{9,11},{10,... | collective-permute-start | bytes 196616 | tf_op jit(solution)/shard_map/ppermute | solution.py:29
  50.4 5.4 %collective-permute-start.17 = (f32[256]{0:T(256)S(1)}, f32[256]{0:T(256)S(1)}, u32[]{:S(2)}, u32[]{:S(2)}) collective-permute-start(f32[256]{0:T(256)S(1)} %bitcast.83), channel_id=1, source_target_pairs={{0,12},{1,13},{2,14},{3,15},{4,8},{5,9},{6,10},{7,11},{8,4},{9,5},... | collective-permute-start | bytes 3080 | tf_op jit(solution)/shard_map/ppermute | solution.py:29
  53.1 4.5 %collective-permute-start.16 = (f32[256]{0:T(256)S(1)}, f32[256]{0:T(256)S(1)}, u32[]{:S(2)}, u32[]{:S(2)}) collective-permute-start(f32[256]{0:T(256)S(1)} %bitcast.84), channel_id=1, source_target_pairs={{0,8},{1,9},{2,10},{3,11},{4,12},{5,13},{6,14},{7,15},{8,0},{9,1},... | collective-permute-start | bytes 3080 | tf_op jit(solution)/shard_map/ppermute | solution.py:29
  54.0 3.6 %collective-permute-start.15 = (f32[256]{0:T(256)S(1)}, f32[256]{0:T(256)S(1)}, u32[]{:S(2)}, u32[]{:S(2)}) collective-permute-start(f32[256]{0:T(256)S(1)} %bitcast.85), channel_id=1, source_target_pairs={{0,4},{1,5},{2,6},{3,7},{4,0},{5,1},{6,2},{7,3},{8,12},{9,13},{10,... | collective-permute-start | bytes 3080 | tf_op jit(solution)/shard_map/ppermute | solution.py:29
  58.8 1.3 %collective-permute-start.18 = (f32[16384]{0:T(1024)S(1)}, f32[16384]{0:T(1024)S(1)}, u32[]{:S(2)}, u32[]{:S(2)}) collective-permute-start(f32[16384]{0:T(1024)S(1)} %bitcast.68), channel_id=1, source_target_pairs={{0,1},{1,0},{2,3},{3,2},{4,5},{5,4},{6,7},{7,6},{8,9},{9,8},{10,11... | collective-permute-start | bytes 196616 | tf_op jit(solution)/shard_map/ppermute | solution.py:29
  60.1 4.3 %collective-permute-start.19 = (f32[16384]{0:T(1024)S(1)}, f32[16384]{0:T(1024)S(1)}, u32[]{:S(2)}, u32[]{:S(2)}) collective-permute-start(f32[16384]{0:T(1024)S(1)} %bitcast_add_fusion.2), channel_id=1, source_target_pairs={{0,2},{1,3},{2,0},{3,1},{4,6},{5,7},{6,4},{7,5},{8,10},{9,11},{10,... | collective-permute-start | bytes 196616 | tf_op jit(solution)/shard_map/ppermute | solution.py:29
  65.7 5.4 %collective-permute-start.22 = (f32[256]{0:T(256)S(1)}, f32[256]{0:T(256)S(1)}, u32[]{:S(2)}, u32[]{:S(2)}) collective-permute-start(f32[256]{0:T(256)S(1)} %bitcast.86), channel_id=1, source_target_pairs={{0,12},{1,13},{2,14},{3,15},{4,8},{5,9},{6,10},{7,11},{8,4},{9,5},... | collective-permute-start | bytes 3080 | tf_op jit(solution)/shard_map/ppermute | solution.py:29
  67.2 4.5 %collective-permute-start.21 = (f32[256]{0:T(256)S(1)}, f32[256]{0:T(256)S(1)}, u32[]{:S(2)}, u32[]{:S(2)}) collective-permute-start(f32[256]{0:T(256)S(1)} %bitcast.87), channel_id=1, source_target_pairs={{0,8},{1,9},{2,10},{3,11},{4,12},{5,13},{6,14},{7,15},{8,0},{9,1},... | collective-permute-start | bytes 3080 | tf_op jit(solution)/shard_map/ppermute | solution.py:29
  68.1 3.6 %collective-permute-start.20 = (f32[256]{0:T(256)S(1)}, f32[256]{0:T(256)S(1)}, u32[]{:S(2)}, u32[]{:S(2)}) collective-permute-start(f32[256]{0:T(256)S(1)} %bitcast.88), channel_id=1, source_target_pairs={{0,4},{1,5},{2,6},{3,7},{4,0},{5,1},{6,2},{7,3},{8,12},{9,13},{10,... | collective-permute-start | bytes 3080 | tf_op jit(solution)/shard_map/ppermute | solution.py:29
  72.9 1.3 %collective-permute-start.23 = (f32[16384]{0:T(1024)S(1)}, f32[16384]{0:T(1024)S(1)}, u32[]{:S(2)}, u32[]{:S(2)}) collective-permute-start(f32[16384]{0:T(1024)S(1)} %bitcast.69), channel_id=1, source_target_pairs={{0,1},{1,0},{2,3},{3,2},{4,5},{5,4},{6,7},{7,6},{8,9},{9,8},{10,11... | collective-permute-start | bytes 196616 | tf_op jit(solution)/shard_map/ppermute | solution.py:29
  74.2 4.3 %collective-permute-start.24 = (f32[16384]{0:T(1024)S(1)}, f32[16384]{0:T(1024)S(1)}, u32[]{:S(2)}, u32[]{:S(2)}) collective-permute-start(f32[16384]{0:T(1024)S(1)} %bitcast_add_fusion.1), channel_id=1, source_target_pairs={{0,2},{1,3},{2,0},{3,1},{4,6},{5,7},{6,4},{7,5},{8,10},{9,11},{10,... | collective-permute-start | bytes 196616 | tf_op jit(solution)/shard_map/ppermute | solution.py:29
  79.8 5.4 %collective-permute-start.27 = (f32[256]{0:T(256)S(1)}, f32[256]{0:T(256)S(1)}, u32[]{:S(2)}, u32[]{:S(2)}) collective-permute-start(f32[256]{0:T(256)S(1)} %bitcast.89), channel_id=1, source_target_pairs={{0,12},{1,13},{2,14},{3,15},{4,8},{5,9},{6,10},{7,11},{8,4},{9,5},... | collective-permute-start | bytes 3080 | tf_op jit(solution)/shard_map/ppermute | solution.py:29
  82.5 4.5 %collective-permute-start.26 = (f32[256]{0:T(256)S(1)}, f32[256]{0:T(256)S(1)}, u32[]{:S(2)}, u32[]{:S(2)}) collective-permute-start(f32[256]{0:T(256)S(1)} %bitcast.90), channel_id=1, source_target_pairs={{0,8},{1,9},{2,10},{3,11},{4,12},{5,13},{6,14},{7,15},{8,0},{9,1},... | collective-permute-start | bytes 3080 | tf_op jit(solution)/shard_map/ppermute | solution.py:29
  83.4 3.6 %collective-permute-start.25 = (f32[256]{0:T(256)S(1)}, f32[256]{0:T(256)S(1)}, u32[]{:S(2)}, u32[]{:S(2)}) collective-permute-start(f32[256]{0:T(256)S(1)} %bitcast.91), channel_id=1, source_target_pairs={{0,4},{1,5},{2,6},{3,7},{4,0},{5,1},{6,2},{7,3},{8,12},{9,13},{10,... | collective-permute-start | bytes 3080 | tf_op jit(solution)/shard_map/ppermute | solution.py:29
  88.2 1.3 %collective-permute-start.28 = (f32[16384]{0:T(1024)S(1)}, f32[16384]{0:T(1024)S(1)}, u32[]{:S(2)}, u32[]{:S(2)}) collective-permute-start(f32[16384]{0:T(1024)S(1)} %bitcast.70), channel_id=1, source_target_pairs={{0,1},{1,0},{2,3},{3,2},{4,5},{5,4},{6,7},{7,6},{8,9},{9,8},{10,11... | collective-permute-start | bytes 196616 | tf_op jit(solution)/shard_map/ppermute | solution.py:29
  89.5 4.3 %collective-permute-start.29 = (f32[16384]{0:T(1024)S(1)}, f32[16384]{0:T(1024)S(1)}, u32[]{:S(2)}, u32[]{:S(2)}) collective-permute-start(f32[16384]{0:T(1024)S(1)} %bitcast_add_fusion), channel_id=1, source_target_pairs={{0,2},{1,3},{2,0},{3,1},{4,6},{5,7},{6,4},{7,5},{8,10},{9,11},{10,... | collective-permute-start | bytes 196616 | tf_op jit(solution)/shard_map/ppermute | solution.py:29
  95.1 5.4 %collective-permute-start.32 = (f32[256]{0:T(256)S(1)}, f32[256]{0:T(256)S(1)}, u32[]{:S(2)}, u32[]{:S(2)}) collective-permute-start(f32[256]{0:T(256)S(1)} %bitcast.114), channel_id=1, source_target_pairs={{0,12},{1,13},{2,14},{3,15},{4,8},{5,9},{6,10},{7,11},{8,4},{9,5},... | collective-permute-start | bytes 3080 | tf_op jit(solution)/shard_map/ppermute | solution.py:29
  96.6 4.5 %collective-permute-start.31 = (f32[256]{0:T(256)S(1)}, f32[256]{0:T(256)S(1)}, u32[]{:S(2)}, u32[]{:S(2)}) collective-permute-start(f32[256]{0:T(256)S(1)} %bitcast.115), channel_id=1, source_target_pairs={{0,8},{1,9},{2,10},{3,11},{4,12},{5,13},{6,14},{7,15},{8,0},{9,1},... | collective-permute-start | bytes 3080 | tf_op jit(solution)/shard_map/ppermute | solution.py:29
  97.5 3.6 %collective-permute-start.30 = (f32[256]{0:T(256)S(1)}, f32[256]{0:T(256)S(1)}, u32[]{:S(2)}, u32[]{:S(2)}) collective-permute-start(f32[256]{0:T(256)S(1)} %bitcast.116), channel_id=1, source_target_pairs={{0,4},{1,5},{2,6},{3,7},{4,0},{5,1},{6,2},{7,3},{8,12},{9,13},{10,... | collective-permute-start | bytes 3080 | tf_op jit(solution)/shard_map/ppermute | solution.py:29

commit v4 on v3

--- a/solution.py
+++ b/solution.py
@@ -12,6 +12,8 @@
 SOFTNESS = 0.25
 LANES = 128
 UNROLL = 16
+COLUMN_ORDER = (1, 2, 3)
+ROW_ORDER = (3, 1, 2)
 VMEM = pltpu.VMEM
 LIMIT = 40 * 2**20
 ATANH = (
@@ -50,7 +52,14 @@
     return estimate, slope
 
 
-def column_total(parts):
+def exchanged(piece, unit, order):
+    flat = piece.reshape(-1)
+    return [piece] + [swapped(flat, unit * mask).reshape(piece.shape) for mask in order]
+
+
+def pairwise_total(pieces, order):
+    by_mask = dict(zip((0, *order), pieces))
+    parts = [by_mask[mask][...] for mask in range(len(by_mask))]
     while len(parts) > 1:
         parts = [parts[at] + parts[at + 1] for at in range(0, len(parts), 2)]
     return parts[0]
@@ -72,7 +81,7 @@
 
 
 def new_residual(pieces, measured, old, rows, all_rows):
-    total = column_total([piece[...] for piece in pieces])
+    total = pairwise_total(pieces, COLUMN_ORDER)
     onsager = total[:, rows : rows + 1] / all_rows
     return measured[...] - total + onsager * old[...]
 
@@ -89,7 +98,7 @@
         *parts, sensing, out, residual_out = refs
     else:
         *parts, measured, old, sensing, out, residual_out = refs
-    total = column_total([part[...] for part in parts])
+    total = pairwise_total(parts, COLUMN_ORDER)
     if first:
         residual = total
     else:
@@ -113,13 +122,11 @@
     lax.fori_loop(0, out.shape[0] // UNROLL, step, 0)
 
 
-def forward_kernel(first, rows, step_at, *refs):
-    if first:
-        thresholds, partial, other, sensing, estimate_out, out = refs
-        pseudo = partial[...] + other[...]
-    else:
-        thresholds, partial, other, old, sensing, estimate_out, out = refs
-        pseudo = old[...] + (partial[...] + other[...])
+def forward_kernel(first, rows, step_at, order, *refs):
+    thresholds, *pieces, sensing, estimate_out, out = refs
+    pseudo = pairwise_total(pieces[: len(order) + 1], order)
+    if not first:
+        pseudo = pieces[-1][...] + pseudo
     estimate, slopes = shrink_and_slope(pseudo, thresholds[:, step_at : step_at + 1])
     estimate_out[...] = estimate
     slope = jnp.sum(slopes, axis=0, keepdims=True)
@@ -149,6 +156,8 @@
     groups = devices // COLS
     all_rows = local_rows * devices
     low_bits = groups.bit_length() - 1
+    direct = min(low_bits, 2)
+    row_order = tuple(mask for mask in ROW_ORDER if mask < 2**direct)
     index = lax.axis_index("row")
     group_pos = index % groups
     column_pos = index // groups
@@ -185,7 +194,7 @@
 
     def forward(first, step, *others):
         return pl.pallas_call(
-            functools.partial(forward_kernel, first, rows, step),
+            functools.partial(forward_kernel, first, rows, step, row_order),
             out_shape=(signal, row),
             in_specs=[in_vmem] * (len(others) + 2),
             out_specs=(in_vmem, in_vmem),
@@ -193,16 +202,10 @@
             name="forward",
         )(thresholds.reshape(1, -1), *others, matrix)
 
-    def all_columns(piece):
-        flat = piece.reshape(padded)
-        return [piece] + [
-            swapped(flat, groups * mask).reshape(1, padded) for mask in range(1, COLS)
-        ]
-
     own = lax.dynamic_update_slice(
         jnp.zeros((padded,), jnp.float32), measured, (column_pos * local_rows,)
     ).reshape(1, padded)
-    parts = all_columns(own)
+    parts = exchanged(own, groups, COLUMN_ORDER)
     others = ()
     estimate = ()
     for step in range(ITERS):
@@ -210,16 +213,12 @@
         if step == 0:
             measured_row = residual
         others = (measured_row, residual)
-        flat = partial.reshape(width)
-        for position in range(low_bits - 1):
-            flat = flat + swapped(flat, 2**position)
-        other = swapped(flat, 2 ** (low_bits - 1))
-        shaped = (tiles, LANES)
-        new_estimate, product = forward(
-            step == 0, step, flat.reshape(shaped), other.reshape(shaped), *estimate
-        )
+        for position in range(low_bits - direct):
+            partial = sum(exchanged(partial, 2**position, (1,)))
+        sent = exchanged(partial, groups >> direct, row_order)
+        new_estimate, product = forward(step == 0, step, *sent, *estimate)
         estimate = (new_estimate,)
-        parts = all_columns(product)
+        parts = exchanged(product, groups, COLUMN_ORDER)
     residual = pl.pallas_call(
         functools.partial(last_kernel, rows, all_rows),
         out_shape=jax.ShapeDtypeStruct((1, local_rows), jnp.float32),

time: 102 us -> 99.1 us (0.972)
  waiting for transfers between devices: 37.1 us -> 31 us
  starting transfers between devices: 42.3 us -> 45.7 us
    ppermute x33 -> x39, waiting for transfers between devices: 37.1 us -> 31 us  [swapped(): return lax.ppermute(value, 'row', pairs)]
    ppermute x33 -> x39, starting transfers between devices: 42.3 us -> 45.7 us  [swapped(): return lax.ppermute(value, 'row', pairs)]
  transfers between devices with their start and end apart: 33 -> 39, of which waited for: 24 -> 24; matrix products, arithmetic and copies ran while one was open for 1% -> 1% of each run, Pallas kernels for 5% -> 5%
where the time goes in v4:
time: 99.1 us; the launch traced here: 99 us
  starting transfers between devices  45.7 us (46%)
  waiting for transfers between devices  31 us (31%)
  Pallas kernels  19.9 us (20%)
  local copies, waits for them, and re-layouts  1.47 us (1%)
    ppermute x39, starting transfers between devices, swapped(): return lax.ppermute(value, 'row', pairs)  45.7 us
    ppermute x39, waiting for transfers between devices, swapped(): return lax.ppermute(value, 'row', pairs)  31 us
    pallas_call x6, Pallas kernels, forward(): pl.pallas_call(functools.partial(forward_kernel, first, rows, step, row_o...  7.59 us
    pallas_call x6, Pallas kernels, back(): pl.pallas_call(functools.partial(back_kernel, first, rows, all_rows), out...  7.04 us
    pallas_call x1, Pallas kernels, on_device(): pl.pallas_call(load_kernel, out_shape=VMEM(sensing.shape, sensing.dtype),...  4.58 us
  transfers between devices with their start and end apart: 39, of which 24 were waited for; matrix products, arithmetic and copies ran while one was open for 1% of the time, Pallas kernels for 5%

profile of v4, /device:TPU:0, one launch (start us, length us, event | category | flops | bytes accessed | tf_op | source)
XLA Modules:
  0.0 99.0 jit_solution(3577461291198869071)
XLA Ops:
  1.5 5.1 %collective-permute-start.2 = (f32[256]{0:T(256)S(1)}, f32[256]{0:T(256)S(1)}, u32[]{:S(2)}, u32[]{:S(2)}) collective-permute-start(f32[256]{0:T(256)S(1)} %dynamic_update_slice.3), channel_id=1, source_target_pairs={{0,12},{1,13},{2,14},{3,15},{4,8},{5,9},{6,10},{7,11},{8,4},{9,5},... | collective-permute-start | bytes 3080 | tf_op jit(solution)/shard_map/ppermute | solution.py:31
  7.2 4.6 %load.1.refs_4_.refs_5_.refs_6_ = f32[192,16384]{1,0:T(8,128)S(1)} custom-call(f32[192,16384]{1,0:T(8,128)} %source.1), custom_call_target="tpu_custom_call" | custom-call | bytes 25165824 | tf_op jit(solution)/shard_map/load/pallas_call | solution.py:169
  11.9 1.1 %back.6 = (f32[128,128]{1,0:T(8,128)S(1)}, f32[1,256]{1,0:T(1,128)S(1)}) custom-call(f32[1,256]{1,0:T(1,128)S(1)} %bitcast.131, f32[1,256]{1,0:T(1,128)S(1)} %bitcast.129, f32[1,256]{1,0:T(1,128)S(1)} %bitcast.123, f32[1,256]{1,0:T(1,128)S(1)} %bitcast.117, f32[192,16384]{1,0:T(8,128)S(1)} %load.1.refs_4_.refs_5_.refs_6_), custom_call_target="tpu_custom_call" | custom-call | tf_op jit(solution)/shard_map/back/pallas_call | solution.py:186
  12.9 1.7 %collective-permute-start.5 = (f32[16384]{0:T(1024)S(1)}, f32[16384]{0:T(1024)S(1)}, u32[]{:S(2)}, u32[]{:S(2)}) collective-permute-start(f32[16384]{0:T(1024)S(1)} %bitcast.70), channel_id=1, source_target_pairs={{0,2},{1,3},{2,0},{3,1},{4,6},{5,7},{6,4},{7,5},{8,10},{9,11},{10,... | collective-permute-start | bytes 196616 | tf_op jit(solution)/shard_map/ppermute | solution.py:31
  15.1 2.1 %collective-permute-done.5 = f32[16384]{0:T(1024)S(1)} collective-permute-done((f32[16384]{0:T(1024)S(1)}, f32[16384]{0:T(1024)S(1)}, u32[]{:S(2)}, u32[]{:S(2)}) %collective-permute-start.5) | collective-permute-done | bytes 65568 | tf_op jit(solution)/shard_map/ppermute | solution.py:31
  17.3 1.1 %collective-permute-done.3 = f32[16384]{0:T(1024)S(1)} collective-permute-done((f32[16384]{0:T(1024)S(1)}, f32[16384]{0:T(1024)S(1)}, u32[]{:S(2)}, u32[]{:S(2)}) %collective-permute-start.3) | collective-permute-done | bytes 65568 | tf_op jit(solution)/shard_map/ppermute | solution.py:31
  18.4 1.3 %forward.6 = (f32[128,128]{1,0:T(8,128)S(1)}, f32[1,256]{1,0:T(1,128)S(1)}) custom-call(f32[1,6]{1,0:T(1,128)S(1)} %bitcast.91, f32[128,128]{1,0:T(8,128)S(1)} %get-tuple-element.26.refs_1_, f32[128,128]{1,0:T(8,128)S(1)} %bitcast.90, f32[128,128]{1,0:T(8,128)S(1)} %bitcast.84, f32[128,128]{1,0:T(8,128)S(1)} %bitcast.78, ...), custom_call_target="tpu_custom_call" | custom-call | tf_op jit(solution)/shard_map/forward/pallas_call | solution.py:196
  19.6 3.7 %collective-permute-start.8 = (f32[256]{0:T(256)S(1)}, f32[256]{0:T(256)S(1)}, u32[]{:S(2)}, u32[]{:S(2)}) collective-permute-start(f32[256]{0:T(256)S(1)} %bitcast.110), channel_id=1, source_target_pairs={{0,12},{1,13},{2,14},{3,15},{4,8},{5,9},{6,10},{7,11},{8,4},{9,5},... | collective-permute-start | bytes 3080 | tf_op jit(solution)/shard_map/ppermute | solution.py:31
  24.1 1.0 collective-permute-done.8
  25.1 2.7 %collective-permute-done.7 = f32[256]{0:T(256)S(1)} collective-permute-done((f32[256]{0:T(256)S(1)}, f32[256]{0:T(256)S(1)}, u32[]{:S(2)}, u32[]{:S(2)}) %collective-permute-start.7) | collective-permute-done | bytes 1056 | tf_op jit(solution)/shard_map/ppermute | solution.py:31
  27.8 1.2 %back.7 = (f32[128,128]{1,0:T(8,128)S(1)}, f32[1,256]{1,0:T(1,128)S(1)}) custom-call(f32[1,256]{1,0:T(1,128)S(1)} %get-tuple-element.27.refs_0_, f32[1,256]{1,0:T(1,128)S(1)} %bitcast.130, f32[1,256]{1,0:T(1,128)S(1)} %bitcast.124, f32[1,256]{1,0:T(1,128)S(1)} %bitcast.118, f32[1,256]{1,0:T(1,128)S(1)} %get-tuple-element.28.refs_4_.refs_5_, ...), custom_call_target="tpu_custom_call" | custom-call | tf_op jit(solution)/shard_map/back/pallas_call | solution.py:186
  29.0 1.3 %collective-permute-start.11 = (f32[16384]{0:T(1024)S(1)}, f32[16384]{0:T(1024)S(1)}, u32[]{:S(2)}, u32[]{:S(2)}) collective-permute-start(f32[16384]{0:T(1024)S(1)} %bitcast.67), channel_id=1, source_target_pairs={{0,2},{1,3},{2,0},{3,1},{4,6},{5,7},{6,4},{7,5},{8,10},{9,11},{10,... | collective-permute-start | bytes 196616 | tf_op jit(solution)/shard_map/ppermute | solution.py:31
  30.3 0.9 collective-permute-start.9
  31.2 2.3 %collective-permute-done.11 = f32[16384]{0:T(1024)S(1)} collective-permute-done((f32[16384]{0:T(1024)S(1)}, f32[16384]{0:T(1024)S(1)}, u32[]{:S(2)}, u32[]{:S(2)}) %collective-permute-start.11) | collective-permute-done | bytes 65568 | tf_op jit(solution)/shard_map/ppermute | solution.py:31
  34.2 1.3 %forward.7 = (f32[128,128]{1,0:T(8,128)S(1)}, f32[1,256]{1,0:T(1,128)S(1)}) custom-call(f32[1,6]{1,0:T(1,128)S(1)} %bitcast.92, f32[128,128]{1,0:T(8,128)S(1)} %get-tuple-element.29.refs_1_, f32[128,128]{1,0:T(8,128)S(1)} %bitcast.86, f32[128,128]{1,0:T(8,128)S(1)} %bitcast.80, f32[128,128]{1,0:T(8,128)S(1)} %bitcast.74, ...), custom_call_target="tpu_custom_call" | custom-call | tf_op jit(solution)/shard_map/forward/pallas_call | solution.py:196
  35.4 1.6 %collective-permute-start.14 = (f32[256]{0:T(256)S(1)}, f32[256]{0:T(256)S(1)}, u32[]{:S(2)}, u32[]{:S(2)}) collective-permute-start(f32[256]{0:T(256)S(1)} %bitcast.98), channel_id=1, source_target_pairs={{0,12},{1,13},{2,14},{3,15},{4,8},{5,9},{6,10},{7,11},{8,4},{9,5},... | collective-permute-start | bytes 3080 | tf_op jit(solution)/shard_map/ppermute | solution.py:31
  37.6 2.3 %collective-permute-start.12 = (f32[256]{0:T(256)S(1)}, f32[256]{0:T(256)S(1)}, u32[]{:S(2)}, u32[]{:S(2)}) collective-permute-start(f32[256]{0:T(256)S(1)} %bitcast.100), channel_id=1, source_target_pairs={{0,4},{1,5},{2,6},{3,7},{4,0},{5,1},{6,2},{7,3},{8,12},{9,13},{10,... | collective-permute-start | bytes 3080 | tf_op jit(solution)/shard_map/ppermute | solution.py:31
  39.9 1.0 collective-permute-done.14
  41.5 1.2 %back.8 = (f32[128,128]{1,0:T(8,128)S(1)}, f32[1,256]{1,0:T(1,128)S(1)}) custom-call(f32[1,256]{1,0:T(1,128)S(1)} %get-tuple-element.31.refs_0_, f32[1,256]{1,0:T(1,128)S(1)} %bitcast.125, f32[1,256]{1,0:T(1,128)S(1)} %bitcast.119, f32[1,256]{1,0:T(1,128)S(1)} %bitcast.113, f32[1,256]{1,0:T(1,128)S(1)} %get-tuple-element.28.refs_4_.refs_5_, ...), custom_call_target="tpu_custom_call" | custom-call | tf_op jit(solution)/shard_map/back/pallas_call | solution.py:186
  42.7 1.4 %collective-permute-start.17 = (f32[16384]{0:T(1024)S(1)}, f32[16384]{0:T(1024)S(1)}, u32[]{:S(2)}, u32[]{:S(2)}) collective-permute-start(f32[16384]{0:T(1024)S(1)} %bitcast.58), channel_id=1, source_target_pairs={{0,2},{1,3},{2,0},{3,1},{4,6},{5,7},{6,4},{7,5},{8,10},{9,11},{10,... | collective-permute-start | bytes 196616 | tf_op jit(solution)/shard_map/ppermute | solution.py:31
  44.9 2.1 %collective-permute-done.17 = f32[16384]{0:T(1024)S(1)} collective-permute-done((f32[16384]{0:T(1024)S(1)}, f32[16384]{0:T(1024)S(1)}, u32[]{:S(2)}, u32[]{:S(2)}) %collective-permute-start.17) | collective-permute-done | bytes 65568 | tf_op jit(solution)/shard_map/ppermute | solution.py:31
  47.8 1.3 %forward.8 = (f32[128,128]{1,0:T(8,128)S(1)}, f32[1,256]{1,0:T(1,128)S(1)}) custom-call(f32[1,6]{1,0:T(1,128)S(1)} %bitcast.93, f32[128,128]{1,0:T(8,128)S(1)} %get-tuple-element.33.refs_1_, f32[128,128]{1,0:T(8,128)S(1)} %bitcast.87, f32[128,128]{1,0:T(8,128)S(1)} %bitcast.81, f32[128,128]{1,0:T(8,128)S(1)} %bitcast.75, ...), custom_call_target="tpu_custom_call" | custom-call | tf_op jit(solution)/shard_map/forward/pallas_call | solution.py:196
  49.0 2.6 %collective-permute-start.20 = (f32[256]{0:T(256)S(1)}, f32[256]{0:T(256)S(1)}, u32[]{:S(2)}, u32[]{:S(2)}) collective-permute-start(f32[256]{0:T(256)S(1)} %bitcast.101), channel_id=1, source_target_pairs={{0,12},{1,13},{2,14},{3,15},{4,8},{5,9},{6,10},{7,11},{8,4},{9,5},... | collective-permute-start | bytes 3080 | tf_op jit(solution)/shard_map/ppermute | solution.py:31
  53.5 1.0 collective-permute-done.20
  54.5 1.7 %collective-permute-done.19 = f32[256]{0:T(256)S(1)} collective-permute-done((f32[256]{0:T(256)S(1)}, f32[256]{0:T(256)S(1)}, u32[]{:S(2)}, u32[]{:S(2)}) %collective-permute-start.19) | collective-permute-done | bytes 1056 | tf_op jit(solution)/shard_map/ppermute | solution.py:31
  56.2 1.2 %back.9 = (f32[128,128]{1,0:T(8,128)S(1)}, f32[1,256]{1,0:T(1,128)S(1)}) custom-call(f32[1,256]{1,0:T(1,128)S(1)} %get-tuple-element.35.refs_0_, f32[1,256]{1,0:T(1,128)S(1)} %bitcast.126, f32[1,256]{1,0:T(1,128)S(1)} %bitcast.120, f32[1,256]{1,0:T(1,128)S(1)} %bitcast.114, f32[1,256]{1,0:T(1,128)S(1)} %get-tuple-element.28.refs_4_.refs_5_, ...), custom_call_target="tpu_custom_call" | custom-call | tf_op jit(solution)/shard_map/back/pallas_call | solution.py:186
  57.4 1.5 %collective-permute-start.23 = (f32[16384]{0:T(1024)S(1)}, f32[16384]{0:T(1024)S(1)}, u32[]{:S(2)}, u32[]{:S(2)}) collective-permute-start(f32[16384]{0:T(1024)S(1)} %bitcast.61), channel_id=1, source_target_pairs={{0,2},{1,3},{2,0},{3,1},{4,6},{5,7},{6,4},{7,5},{8,10},{9,11},{10,... | collective-permute-start | bytes 196616 | tf_op jit(solution)/shard_map/ppermute | solution.py:31
  59.6 2.1 %collective-permute-done.23 = f32[16384]{0:T(1024)S(1)} collective-permute-done((f32[16384]{0:T(1024)S(1)}, f32[16384]{0:T(1024)S(1)}, u32[]{:S(2)}, u32[]{:S(2)}) %collective-permute-start.23) | collective-permute-done | bytes 65568 | tf_op jit(solution)/shard_map/ppermute | solution.py:31
  62.6 1.3 %forward.9 = (f32[128,128]{1,0:T(8,128)S(1)}, f32[1,256]{1,0:T(1,128)S(1)}) custom-call(f32[1,6]{1,0:T(1,128)S(1)} %bitcast.94, f32[128,128]{1,0:T(8,128)S(1)} %get-tuple-element.37.refs_1_, f32[128,128]{1,0:T(8,128)S(1)} %bitcast.88, f32[128,128]{1,0:T(8,128)S(1)} %bitcast.82, f32[128,128]{1,0:T(8,128)S(1)} %bitcast.76, ...), custom_call_target="tpu_custom_call" | custom-call | tf_op jit(solution)/shard_map/forward/pallas_call | solution.py:196
  63.9 1.5 %collective-permute-start.26 = (f32[256]{0:T(256)S(1)}, f32[256]{0:T(256)S(1)}, u32[]{:S(2)}, u32[]{:S(2)}) collective-permute-start(f32[256]{0:T(256)S(1)} %bitcast.104), channel_id=1, source_target_pairs={{0,12},{1,13},{2,14},{3,15},{4,8},{5,9},{6,10},{7,11},{8,4},{9,5},... | collective-permute-start | bytes 3080 | tf_op jit(solution)/shard_map/ppermute | solution.py:31
  65.4 0.9 collective-permute-start.25
  66.3 2.0 %collective-permute-start.24 = (f32[256]{0:T(256)S(1)}, f32[256]{0:T(256)S(1)}, u32[]{:S(2)}, u32[]{:S(2)}) collective-permute-start(f32[256]{0:T(256)S(1)} %bitcast.106), channel_id=1, source_target_pairs={{0,4},{1,5},{2,6},{3,7},{4,0},{5,1},{6,2},{7,3},{8,12},{9,13},{10,... | collective-permute-start | bytes 3080 | tf_op jit(solution)/shard_map/ppermute | solution.py:31
  68.3 1.0 collective-permute-done.26
  69.9 1.2 %back.10 = (f32[128,128]{1,0:T(8,128)S(1)}, f32[1,256]{1,0:T(1,128)S(1)}) custom-call(f32[1,256]{1,0:T(1,128)S(1)} %get-tuple-element.39.refs_0_, f32[1,256]{1,0:T(1,128)S(1)} %bitcast.127, f32[1,256]{1,0:T(1,128)S(1)} %bitcast.121, f32[1,256]{1,0:T(1,128)S(1)} %bitcast.115, f32[1,256]{1,0:T(1,128)S(1)} %get-tuple-element.28.refs_4_.refs_5_, ...), custom_call_target="tpu_custom_call" | custom-call | tf_op jit(solution)/shard_map/back/pallas_call | solution.py:186
  71.1 1.3 %collective-permute-start.29 = (f32[16384]{0:T(1024)S(1)}, f32[16384]{0:T(1024)S(1)}, u32[]{:S(2)}, u32[]{:S(2)}) collective-permute-start(f32[16384]{0:T(1024)S(1)} %bitcast.64), channel_id=1, source_target_pairs={{0,2},{1,3},{2,0},{3,1},{4,6},{5,7},{6,4},{7,5},{8,10},{9,11},{10,... | collective-permute-start | bytes 196616 | tf_op jit(solution)/shard_map/ppermute | solution.py:31
  73.3 2.1 %collective-permute-done.29 = f32[16384]{0:T(1024)S(1)} collective-permute-done((f32[16384]{0:T(1024)S(1)}, f32[16384]{0:T(1024)S(1)}, u32[]{:S(2)}, u32[]{:S(2)}) %collective-permute-start.29) | collective-permute-done | bytes 65568 | tf_op jit(solution)/shard_map/ppermute | solution.py:31
  76.2 1.3 %forward.10 = (f32[128,128]{1,0:T(8,128)S(1)}, f32[1,256]{1,0:T(1,128)S(1)}) custom-call(f32[1,6]{1,0:T(1,128)S(1)} %bitcast.95, f32[128,128]{1,0:T(8,128)S(1)} %get-tuple-element.41.refs_1_, f32[128,128]{1,0:T(8,128)S(1)} %bitcast.89, f32[128,128]{1,0:T(8,128)S(1)} %bitcast.83, f32[128,128]{1,0:T(8,128)S(1)} %bitcast.77, ...), custom_call_target="tpu_custom_call" | custom-call | tf_op jit(solution)/shard_map/forward/pallas_call | solution.py:196
  77.4 2.6 %collective-permute-start.32 = (f32[256]{0:T(256)S(1)}, f32[256]{0:T(256)S(1)}, u32[]{:S(2)}, u32[]{:S(2)}) collective-permute-start(f32[256]{0:T(256)S(1)} %bitcast.107), channel_id=1, source_target_pairs={{0,12},{1,13},{2,14},{3,15},{4,8},{5,9},{6,10},{7,11},{8,4},{9,5},... | collective-permute-start | bytes 3080 | tf_op jit(solution)/shard_map/ppermute | solution.py:31
  80.1 0.9 collective-permute-start.31
  81.9 1.0 collective-permute-done.32
  82.9 1.7 %collective-permute-done.31 = f32[256]{0:T(256)S(1)} collective-permute-done((f32[256]{0:T(256)S(1)}, f32[256]{0:T(256)S(1)}, u32[]{:S(2)}, u32[]{:S(2)}) %collective-permute-start.31) | collective-permute-done | bytes 1056 | tf_op jit(solution)/shard_map/ppermute | solution.py:31
  84.5 1.2 %back.11 = (f32[128,128]{1,0:T(8,128)S(1)}, f32[1,256]{1,0:T(1,128)S(1)}) custom-call(f32[1,256]{1,0:T(1,128)S(1)} %get-tuple-element.43.refs_0_, f32[1,256]{1,0:T(1,128)S(1)} %bitcast.128, f32[1,256]{1,0:T(1,128)S(1)} %bitcast.122, f32[1,256]{1,0:T(1,128)S(1)} %bitcast.116, f32[1,256]{1,0:T(1,128)S(1)} %get-tuple-element.28.refs_4_.refs_5_, ...), custom_call_target="tpu_custom_call" | custom-call | tf_op jit(solution)/shard_map/back/pallas_call | solution.py:186
  85.7 1.5 %collective-permute-start.35 = (f32[16384]{0:T(1024)S(1)}, f32[16384]{0:T(1024)S(1)}, u32[]{:S(2)}, u32[]{:S(2)}) collective-permute-start(f32[16384]{0:T(1024)S(1)} %bitcast.55), channel_id=1, source_target_pairs={{0,2},{1,3},{2,0},{3,1},{4,6},{5,7},{6,4},{7,5},{8,10},{9,11},{10,... | collective-permute-start | bytes 196616 | tf_op jit(solution)/shard_map/ppermute | solution.py:31
  88.0 2.1 %collective-permute-done.35 = f32[16384]{0:T(1024)S(1)} collective-permute-done((f32[16384]{0:T(1024)S(1)}, f32[16384]{0:T(1024)S(1)}, u32[]{:S(2)}, u32[]{:S(2)}) %collective-permute-start.35) | collective-permute-done | bytes 65568 | tf_op jit(solution)/shard_map/ppermute | solution.py:31
  91.0 1.3 %forward.11 = (f32[128,128]{1,0:T(8,128)S(1)}, f32[1,256]{1,0:T(1,128)S(1)}) custom-call(f32[1,6]{1,0:T(1,128)S(1)} %bitcast.96, f32[128,128]{1,0:T(8,128)S(1)} %get-tuple-element.45.refs_1_, f32[128,128]{1,0:T(8,128)S(1)} %bitcast.85, f32[128,128]{1,0:T(8,128)S(1)} %bitcast.79, f32[128,128]{1,0:T(8,128)S(1)} %bitcast.73, ...), custom_call_target="tpu_custom_call" | custom-call | tf_op jit(solution)/shard_map/forward/pallas_call | solution.py:196
  92.2 1.5 %collective-permute-start.38 = (f32[256]{0:T(256)S(1)}, f32[256]{0:T(256)S(1)}, u32[]{:S(2)}, u32[]{:S(2)}) collective-permute-start(f32[256]{0:T(256)S(1)} %bitcast.132), channel_id=1, source_target_pairs={{0,12},{1,13},{2,14},{3,15},{4,8},{5,9},{6,10},{7,11},{8,4},{9,5},... | collective-permute-start | bytes 3080 | tf_op jit(solution)/shard_map/ppermute | solution.py:31
  93.8 0.9 collective-permute-start.37
  94.7 2.0 %collective-permute-start.36 = (f32[256]{0:T(256)S(1)}, f32[256]{0:T(256)S(1)}, u32[]{:S(2)}, u32[]{:S(2)}) collective-permute-start(f32[256]{0:T(256)S(1)} %bitcast.134), channel_id=1, source_target_pairs={{0,4},{1,5},{2,6},{3,7},{4,0},{5,1},{6,2},{7,3},{8,12},{9,13},{10,... | collective-permute-start | bytes 3080 | tf_op jit(solution)/shard_map/ppermute | solution.py:31
  (49 shorter events, 16.8 us)
Async XLA Ops:
  1.5 10.3 %collective-permute-start.2 = (f32[256]{0:T(256)S(1)}, f32[256]{0:T(256)S(1)}, u32[]{:S(2)}, u32[]{:S(2)}) collective-permute-start(f32[256]{0:T(256)S(1)} %dynamic_update_slice.3), channel_id=1, source_target_pairs={{0,12},{1,13},{2,14},{3,15},{4,8},{5,9},{6,10},{7,11},{8,4},{9,5},... | collective-permute-start | bytes 3080 | tf_op jit(solution)/shard_map/ppermute | solution.py:31
  6.6 5.3 %collective-permute-start.1 = (f32[256]{0:T(256)S(1)}, f32[256]{0:T(256)S(1)}, u32[]{:S(2)}, u32[]{:S(2)}) collective-permute-start(f32[256]{0:T(256)S(1)} %dynamic_update_slice.3), channel_id=1, source_target_pairs={{0,8},{1,9},{2,10},{3,11},{4,12},{5,13},{6,14},{7,15},{8,0},{9,1},... | collective-permute-start | bytes 3080 | tf_op jit(solution)/shard_map/ppermute | solution.py:31
  6.6 5.3 %collective-permute-start = (f32[256]{0:T(256)S(1)}, f32[256]{0:T(256)S(1)}, u32[]{:S(2)}, u32[]{:S(2)}) collective-permute-start(f32[256]{0:T(256)S(1)} %dynamic_update_slice.3), channel_id=1, source_target_pairs={{0,4},{1,5},{2,6},{3,7},{4,0},{5,1},{6,2},{7,3},{8,12},{9,13},{10,... | collective-permute-start | bytes 3080 | tf_op jit(solution)/shard_map/ppermute | solution.py:31
  11.8 6.6 %copy-start = (f32[6]{0:T(128)S(1)}, f32[6]{0:T(128)}, u32[]{:S(2)}) copy-start(f32[6]{0:T(128)} %param.5) | copy-start | bytes 76
  12.9 4.3 %collective-permute-start.5 = (f32[16384]{0:T(1024)S(1)}, f32[16384]{0:T(1024)S(1)}, u32[]{:S(2)}, u32[]{:S(2)}) collective-permute-start(f32[16384]{0:T(1024)S(1)} %bitcast.70), channel_id=1, source_target_pairs={{0,2},{1,3},{2,0},{3,1},{4,6},{5,7},{6,4},{7,5},{8,10},{9,11},{10,... | collective-permute-start | bytes 196616 | tf_op jit(solution)/shard_map/ppermute | solution.py:31
  14.6 2.6 %collective-permute-start.4 = (f32[16384]{0:T(1024)S(1)}, f32[16384]{0:T(1024)S(1)}, u32[]{:S(2)}, u32[]{:S(2)}) collective-permute-start(f32[16384]{0:T(1024)S(1)} %bitcast.71), channel_id=1, source_target_pairs={{0,1},{1,0},{2,3},{3,2},{4,5},{5,4},{6,7},{7,6},{8,9},{9,8},{10,11... | collective-permute-start | bytes 196616 | tf_op jit(solution)/shard_map/ppermute | solution.py:31
  14.6 3.7 %collective-permute-start.3 = (f32[16384]{0:T(1024)S(1)}, f32[16384]{0:T(1024)S(1)}, u32[]{:S(2)}, u32[]{:S(2)}) collective-permute-start(f32[16384]{0:T(1024)S(1)} %bitcast.72), channel_id=1, source_target_pairs={{0,3},{1,2},{2,1},{3,0},{4,7},{5,6},{6,5},{7,4},{8,11},{9,10},{10,... | collective-permute-start | bytes 196616 | tf_op jit(solution)/shard_map/ppermute | solution.py:31
  19.6 5.4 %collective-permute-start.8 = (f32[256]{0:T(256)S(1)}, f32[256]{0:T(256)S(1)}, u32[]{:S(2)}, u32[]{:S(2)}) collective-permute-start(f32[256]{0:T(256)S(1)} %bitcast.110), channel_id=1, source_target_pairs={{0,12},{1,13},{2,14},{3,15},{4,8},{5,9},{6,10},{7,11},{8,4},{9,5},... | collective-permute-start | bytes 3080 | tf_op jit(solution)/shard_map/ppermute | solution.py:31
  23.3 4.5 %collective-permute-start.7 = (f32[256]{0:T(256)S(1)}, f32[256]{0:T(256)S(1)}, u32[]{:S(2)}, u32[]{:S(2)}) collective-permute-start(f32[256]{0:T(256)S(1)} %bitcast.111), channel_id=1, source_target_pairs={{0,8},{1,9},{2,10},{3,11},{4,12},{5,13},{6,14},{7,15},{8,0},{9,1},... | collective-permute-start | bytes 3080 | tf_op jit(solution)/shard_map/ppermute | solution.py:31
  23.3 4.5 %collective-permute-start.6 = (f32[256]{0:T(256)S(1)}, f32[256]{0:T(256)S(1)}, u32[]{:S(2)}, u32[]{:S(2)}) collective-permute-start(f32[256]{0:T(256)S(1)} %bitcast.112), channel_id=1, source_target_pairs={{0,4},{1,5},{2,6},{3,7},{4,0},{5,1},{6,2},{7,3},{8,12},{9,13},{10,... | collective-permute-start | bytes 3080 | tf_op jit(solution)/shard_map/ppermute | solution.py:31
  29.0 4.5 %collective-permute-start.11 = (f32[16384]{0:T(1024)S(1)}, f32[16384]{0:T(1024)S(1)}, u32[]{:S(2)}, u32[]{:S(2)}) collective-permute-start(f32[16384]{0:T(1024)S(1)} %bitcast.67), channel_id=1, source_target_pairs={{0,2},{1,3},{2,0},{3,1},{4,6},{5,7},{6,4},{7,5},{8,10},{9,11},{10,... | collective-permute-start | bytes 196616 | tf_op jit(solution)/shard_map/ppermute | solution.py:31
  30.3 3.2 %collective-permute-start.10 = (f32[16384]{0:T(1024)S(1)}, f32[16384]{0:T(1024)S(1)}, u32[]{:S(2)}, u32[]{:S(2)}) collective-permute-start(f32[16384]{0:T(1024)S(1)} %bitcast.68), channel_id=1, source_target_pairs={{0,1},{1,0},{2,3},{3,2},{4,5},{5,4},{6,7},{7,6},{8,9},{9,8},{10,11... | collective-permute-start | bytes 196616 | tf_op jit(solution)/shard_map/ppermute | solution.py:31
  30.3 3.9 %collective-permute-start.9 = (f32[16384]{0:T(1024)S(1)}, f32[16384]{0:T(1024)S(1)}, u32[]{:S(2)}, u32[]{:S(2)}) collective-permute-start(f32[16384]{0:T(1024)S(1)} %bitcast.69), channel_id=1, source_target_pairs={{0,3},{1,2},{2,1},{3,0},{4,7},{5,6},{6,5},{7,4},{8,11},{9,10},{10,... | collective-permute-start | bytes 196616 | tf_op jit(solution)/shard_map/ppermute | solution.py:31
  35.4 5.5 %collective-permute-start.14 = (f32[256]{0:T(256)S(1)}, f32[256]{0:T(256)S(1)}, u32[]{:S(2)}, u32[]{:S(2)}) collective-permute-start(f32[256]{0:T(256)S(1)} %bitcast.98), channel_id=1, source_target_pairs={{0,12},{1,13},{2,14},{3,15},{4,8},{5,9},{6,10},{7,11},{8,4},{9,5},... | collective-permute-start | bytes 3080 | tf_op jit(solution)/shard_map/ppermute | solution.py:31
  37.0 4.5 %collective-permute-start.13 = (f32[256]{0:T(256)S(1)}, f32[256]{0:T(256)S(1)}, u32[]{:S(2)}, u32[]{:S(2)}) collective-permute-start(f32[256]{0:T(256)S(1)} %bitcast.99), channel_id=1, source_target_pairs={{0,8},{1,9},{2,10},{3,11},{4,12},{5,13},{6,14},{7,15},{8,0},{9,1},... | collective-permute-start | bytes 3080 | tf_op jit(solution)/shard_map/ppermute | solution.py:31
  37.6 3.8 %collective-permute-start.12 = (f32[256]{0:T(256)S(1)}, f32[256]{0:T(256)S(1)}, u32[]{:S(2)}, u32[]{:S(2)}) collective-permute-start(f32[256]{0:T(256)S(1)} %bitcast.100), channel_id=1, source_target_pairs={{0,4},{1,5},{2,6},{3,7},{4,0},{5,1},{6,2},{7,3},{8,12},{9,13},{10,... | collective-permute-start | bytes 3080 | tf_op jit(solution)/shard_map/ppermute | solution.py:31
  42.7 4.3 %collective-permute-start.17 = (f32[16384]{0:T(1024)S(1)}, f32[16384]{0:T(1024)S(1)}, u32[]{:S(2)}, u32[]{:S(2)}) collective-permute-start(f32[16384]{0:T(1024)S(1)} %bitcast.58), channel_id=1, source_target_pairs={{0,2},{1,3},{2,0},{3,1},{4,6},{5,7},{6,4},{7,5},{8,10},{9,11},{10,... | collective-permute-start | bytes 196616 | tf_op jit(solution)/shard_map/ppermute | solution.py:31
  44.0 3.0 %collective-permute-start.16 = (f32[16384]{0:T(1024)S(1)}, f32[16384]{0:T(1024)S(1)}, u32[]{:S(2)}, u32[]{:S(2)}) collective-permute-start(f32[16384]{0:T(1024)S(1)} %bitcast.59), channel_id=1, source_target_pairs={{0,1},{1,0},{2,3},{3,2},{4,5},{5,4},{6,7},{7,6},{8,9},{9,8},{10,11... | collective-permute-start | bytes 196616 | tf_op jit(solution)/shard_map/ppermute | solution.py:31
  44.0 3.7 %collective-permute-start.15 = (f32[16384]{0:T(1024)S(1)}, f32[16384]{0:T(1024)S(1)}, u32[]{:S(2)}, u32[]{:S(2)}) collective-permute-start(f32[16384]{0:T(1024)S(1)} %bitcast.60), channel_id=1, source_target_pairs={{0,3},{1,2},{2,1},{3,0},{4,7},{5,6},{6,5},{7,4},{8,11},{9,10},{10,... | collective-permute-start | bytes 196616 | tf_op jit(solution)/shard_map/ppermute | solution.py:31
  49.0 5.4 %collective-permute-start.20 = (f32[256]{0:T(256)S(1)}, f32[256]{0:T(256)S(1)}, u32[]{:S(2)}, u32[]{:S(2)}) collective-permute-start(f32[256]{0:T(256)S(1)} %bitcast.101), channel_id=1, source_target_pairs={{0,12},{1,13},{2,14},{3,15},{4,8},{5,9},{6,10},{7,11},{8,4},{9,5},... | collective-permute-start | bytes 3080 | tf_op jit(solution)/shard_map/ppermute | solution.py:31
  51.7 4.5 %collective-permute-start.19 = (f32[256]{0:T(256)S(1)}, f32[256]{0:T(256)S(1)}, u32[]{:S(2)}, u32[]{:S(2)}) collective-permute-start(f32[256]{0:T(256)S(1)} %bitcast.102), channel_id=1, source_target_pairs={{0,8},{1,9},{2,10},{3,11},{4,12},{5,13},{6,14},{7,15},{8,0},{9,1},... | collective-permute-start | bytes 3080 | tf_op jit(solution)/shard_map/ppermute | solution.py:31
  52.6 3.6 %collective-permute-start.18 = (f32[256]{0:T(256)S(1)}, f32[256]{0:T(256)S(1)}, u32[]{:S(2)}, u32[]{:S(2)}) collective-permute-start(f32[256]{0:T(256)S(1)} %bitcast.103), channel_id=1, source_target_pairs={{0,4},{1,5},{2,6},{3,7},{4,0},{5,1},{6,2},{7,3},{8,12},{9,13},{10,... | collective-permute-start | bytes 3080 | tf_op jit(solution)/shard_map/ppermute | solution.py:31
  57.4 4.3 %collective-permute-start.23 = (f32[16384]{0:T(1024)S(1)}, f32[16384]{0:T(1024)S(1)}, u32[]{:S(2)}, u32[]{:S(2)}) collective-permute-start(f32[16384]{0:T(1024)S(1)} %bitcast.61), channel_id=1, source_target_pairs={{0,2},{1,3},{2,0},{3,1},{4,6},{5,7},{6,4},{7,5},{8,10},{9,11},{10,... | collective-permute-start | bytes 196616 | tf_op jit(solution)/shard_map/ppermute | solution.py:31
  58.8 2.9 %collective-permute-start.22 = (f32[16384]{0:T(1024)S(1)}, f32[16384]{0:T(1024)S(1)}, u32[]{:S(2)}, u32[]{:S(2)}) collective-permute-start(f32[16384]{0:T(1024)S(1)} %bitcast.62), channel_id=1, source_target_pairs={{0,1},{1,0},{2,3},{3,2},{4,5},{5,4},{6,7},{7,6},{8,9},{9,8},{10,11... | collective-permute-start | bytes 196616 | tf_op jit(solution)/shard_map/ppermute | solution.py:31
  58.8 3.7 %collective-permute-start.21 = (f32[16384]{0:T(1024)S(1)}, f32[16384]{0:T(1024)S(1)}, u32[]{:S(2)}, u32[]{:S(2)}) collective-permute-start(f32[16384]{0:T(1024)S(1)} %bitcast.63), channel_id=1, source_target_pairs={{0,3},{1,2},{2,1},{3,0},{4,7},{5,6},{6,5},{7,4},{8,11},{9,10},{10,... | collective-permute-start | bytes 196616 | tf_op jit(solution)/shard_map/ppermute | solution.py:31
  63.9 5.4 %collective-permute-start.26 = (f32[256]{0:T(256)S(1)}, f32[256]{0:T(256)S(1)}, u32[]{:S(2)}, u32[]{:S(2)}) collective-permute-start(f32[256]{0:T(256)S(1)} %bitcast.104), channel_id=1, source_target_pairs={{0,12},{1,13},{2,14},{3,15},{4,8},{5,9},{6,10},{7,11},{8,4},{9,5},... | collective-permute-start | bytes 3080 | tf_op jit(solution)/shard_map/ppermute | solution.py:31
  65.4 4.5 %collective-permute-start.25 = (f32[256]{0:T(256)S(1)}, f32[256]{0:T(256)S(1)}, u32[]{:S(2)}, u32[]{:S(2)}) collective-permute-start(f32[256]{0:T(256)S(1)} %bitcast.105), channel_id=1, source_target_pairs={{0,8},{1,9},{2,10},{3,11},{4,12},{5,13},{6,14},{7,15},{8,0},{9,1},... | collective-permute-start | bytes 3080 | tf_op jit(solution)/shard_map/ppermute | solution.py:31
  66.3 3.6 %collective-permute-start.24 = (f32[256]{0:T(256)S(1)}, f32[256]{0:T(256)S(1)}, u32[]{:S(2)}, u32[]{:S(2)}) collective-permute-start(f32[256]{0:T(256)S(1)} %bitcast.106), channel_id=1, source_target_pairs={{0,4},{1,5},{2,6},{3,7},{4,0},{5,1},{6,2},{7,3},{8,12},{9,13},{10,... | collective-permute-start | bytes 3080 | tf_op jit(solution)/shard_map/ppermute | solution.py:31
  71.1 4.3 %collective-permute-start.29 = (f32[16384]{0:T(1024)S(1)}, f32[16384]{0:T(1024)S(1)}, u32[]{:S(2)}, u32[]{:S(2)}) collective-permute-start(f32[16384]{0:T(1024)S(1)} %bitcast.64), channel_id=1, source_target_pairs={{0,2},{1,3},{2,0},{3,1},{4,6},{5,7},{6,4},{7,5},{8,10},{9,11},{10,... | collective-permute-start | bytes 196616 | tf_op jit(solution)/shard_map/ppermute | solution.py:31
  72.4 3.0 %collective-permute-start.28 = (f32[16384]{0:T(1024)S(1)}, f32[16384]{0:T(1024)S(1)}, u32[]{:S(2)}, u32[]{:S(2)}) collective-permute-start(f32[16384]{0:T(1024)S(1)} %bitcast.65), channel_id=1, source_target_pairs={{0,1},{1,0},{2,3},{3,2},{4,5},{5,4},{6,7},{7,6},{8,9},{9,8},{10,11... | collective-permute-start | bytes 196616 | tf_op jit(solution)/shard_map/ppermute | solution.py:31
  72.4 3.7 %collective-permute-start.27 = (f32[16384]{0:T(1024)S(1)}, f32[16384]{0:T(1024)S(1)}, u32[]{:S(2)}, u32[]{:S(2)}) collective-permute-start(f32[16384]{0:T(1024)S(1)} %bitcast.66), channel_id=1, source_target_pairs={{0,3},{1,2},{2,1},{3,0},{4,7},{5,6},{6,5},{7,4},{8,11},{9,10},{10,... | collective-permute-start | bytes 196616 | tf_op jit(solution)/shard_map/ppermute | solution.py:31
  77.4 5.4 %collective-permute-start.32 = (f32[256]{0:T(256)S(1)}, f32[256]{0:T(256)S(1)}, u32[]{:S(2)}, u32[]{:S(2)}) collective-permute-start(f32[256]{0:T(256)S(1)} %bitcast.107), channel_id=1, source_target_pairs={{0,12},{1,13},{2,14},{3,15},{4,8},{5,9},{6,10},{7,11},{8,4},{9,5},... | collective-permute-start | bytes 3080 | tf_op jit(solution)/shard_map/ppermute | solution.py:31
  80.1 4.5 %collective-permute-start.31 = (f32[256]{0:T(256)S(1)}, f32[256]{0:T(256)S(1)}, u32[]{:S(2)}, u32[]{:S(2)}) collective-permute-start(f32[256]{0:T(256)S(1)} %bitcast.108), channel_id=1, source_target_pairs={{0,8},{1,9},{2,10},{3,11},{4,12},{5,13},{6,14},{7,15},{8,0},{9,1},... | collective-permute-start | bytes 3080 | tf_op jit(solution)/shard_map/ppermute | solution.py:31
  81.0 3.6 %collective-permute-start.30 = (f32[256]{0:T(256)S(1)}, f32[256]{0:T(256)S(1)}, u32[]{:S(2)}, u32[]{:S(2)}) collective-permute-start(f32[256]{0:T(256)S(1)} %bitcast.109), channel_id=1, source_target_pairs={{0,4},{1,5},{2,6},{3,7},{4,0},{5,1},{6,2},{7,3},{8,12},{9,13},{10,... | collective-permute-start | bytes 3080 | tf_op jit(solution)/shard_map/ppermute | solution.py:31
  85.7 4.3 %collective-permute-start.35 = (f32[16384]{0:T(1024)S(1)}, f32[16384]{0:T(1024)S(1)}, u32[]{:S(2)}, u32[]{:S(2)}) collective-permute-start(f32[16384]{0:T(1024)S(1)} %bitcast.55), channel_id=1, source_target_pairs={{0,2},{1,3},{2,0},{3,1},{4,6},{5,7},{6,4},{7,5},{8,10},{9,11},{10,... | collective-permute-start | bytes 196616 | tf_op jit(solution)/shard_map/ppermute | solution.py:31
  87.2 2.9 %collective-permute-start.34 = (f32[16384]{0:T(1024)S(1)}, f32[16384]{0:T(1024)S(1)}, u32[]{:S(2)}, u32[]{:S(2)}) collective-permute-start(f32[16384]{0:T(1024)S(1)} %bitcast.56), channel_id=1, source_target_pairs={{0,1},{1,0},{2,3},{3,2},{4,5},{5,4},{6,7},{7,6},{8,9},{9,8},{10,11... | collective-permute-start | bytes 196616 | tf_op jit(solution)/shard_map/ppermute | solution.py:31
  87.2 3.7 %collective-permute-start.33 = (f32[16384]{0:T(1024)S(1)}, f32[16384]{0:T(1024)S(1)}, u32[]{:S(2)}, u32[]{:S(2)}) collective-permute-start(f32[16384]{0:T(1024)S(1)} %bitcast.57), channel_id=1, source_target_pairs={{0,3},{1,2},{2,1},{3,0},{4,7},{5,6},{6,5},{7,4},{8,11},{9,10},{10,... | collective-permute-start | bytes 196616 | tf_op jit(solution)/shard_map/ppermute | solution.py:31
  92.2 5.4 %collective-permute-start.38 = (f32[256]{0:T(256)S(1)}, f32[256]{0:T(256)S(1)}, u32[]{:S(2)}, u32[]{:S(2)}) collective-permute-start(f32[256]{0:T(256)S(1)} %bitcast.132), channel_id=1, source_target_pairs={{0,12},{1,13},{2,14},{3,15},{4,8},{5,9},{6,10},{7,11},{8,4},{9,5},... | collective-permute-start | bytes 3080 | tf_op jit(solution)/shard_map/ppermute | solution.py:31
  93.8 4.5 %collective-permute-start.37 = (f32[256]{0:T(256)S(1)}, f32[256]{0:T(256)S(1)}, u32[]{:S(2)}, u32[]{:S(2)}) collective-permute-start(f32[256]{0:T(256)S(1)} %bitcast.133), channel_id=1, source_target_pairs={{0,8},{1,9},{2,10},{3,11},{4,12},{5,13},{6,14},{7,15},{8,0},{9,1},... | collective-permute-start | bytes 3080 | tf_op jit(solution)/shard_map/ppermute | solution.py:31
  94.7 3.6 %collective-permute-start.36 = (f32[256]{0:T(256)S(1)}, f32[256]{0:T(256)S(1)}, u32[]{:S(2)}, u32[]{:S(2)}) collective-permute-start(f32[256]{0:T(256)S(1)} %bitcast.134), channel_id=1, source_target_pairs={{0,4},{1,5},{2,6},{3,7},{4,0},{5,1},{6,2},{7,3},{8,12},{9,13},{10,... | collective-permute-start | bytes 3080 | tf_op jit(solution)/shard_map/ppermute | solution.py:31

commit v5 on v4

--- a/solution.py
+++ b/solution.py
@@ -14,6 +14,7 @@
 UNROLL = 16
 COLUMN_ORDER = (1, 2, 3)
 ROW_ORDER = (3, 1, 2)
+GATHER_ORDER = (1, 3, 2)
 VMEM = pltpu.VMEM
 LIMIT = 40 * 2**20
 ATANH = (
@@ -98,7 +99,7 @@
         *parts, sensing, out, residual_out = refs
     else:
         *parts, measured, old, sensing, out, residual_out = refs
-    total = pairwise_total(parts, COLUMN_ORDER)
+    total = pairwise_total(parts, GATHER_ORDER if first else COLUMN_ORDER)
     if first:
         residual = total
     else:
@@ -109,11 +110,12 @@
 
     def step(group, carry):
         start = pl.multiple_of(group * UNROLL * LANES, UNROLL * LANES)
-        sums = [jnp.zeros((8, LANES), jnp.float32)] * UNROLL
+        sums = [None] * UNROLL
         for at in range(0, rows, 8):
             block = sensing[pl.ds(at, 8), pl.ds(start, UNROLL * LANES)]
             for tile in range(UNROLL):
-                sums[tile] += block[:, tile * LANES : (tile + 1) * LANES] * columns[at : at + 8]
+                term = block[:, tile * LANES : (tile + 1) * LANES] * columns[at : at + 8]
+                sums[tile] = term if at == 0 else sums[tile] + term
         out[pl.ds(pl.multiple_of(group * UNROLL, UNROLL), UNROLL), :] = jnp.concatenate(
             [jnp.sum(total, axis=0, keepdims=True) for total in sums]
         )
@@ -202,10 +204,11 @@
             name="forward",
         )(thresholds.reshape(1, -1), *others, matrix)
 
-    own = lax.dynamic_update_slice(
-        jnp.zeros((padded,), jnp.float32), measured, (column_pos * local_rows,)
+    own = jnp.concatenate(
+        [jnp.where(index // groups == at, measured, 0.0) for at in range(COLS)]
+        + [jnp.zeros((padded - COLS * local_rows,), jnp.float32)]
     ).reshape(1, padded)
-    parts = exchanged(own, groups, COLUMN_ORDER)
+    parts = exchanged(own, groups, GATHER_ORDER)
     others = ()
     estimate = ()
     for step in range(ITERS):

time: 99.1 us -> 98.5 us (level)
  no operation moved by 1% of the time
where the time goes in v5:
time: 98.5 us; the launch traced here: 98.4 us
  starting transfers between devices  45.6 us (46%)
  waiting for transfers between devices  30.7 us (31%)
  Pallas kernels  19.9 us (20%)
    ppermute x39, starting transfers between devices, swapped(): return lax.ppermute(value, 'row', pairs)  45.6 us
    ppermute x39, waiting for transfers between devices, swapped(): return lax.ppermute(value, 'row', pairs)  30.7 us
    pallas_call x6, Pallas kernels, forward(): pl.pallas_call(functools.partial(forward_kernel, first, rows, step, row_o...  7.59 us
    pallas_call x6, Pallas kernels, back(): pl.pallas_call(functools.partial(back_kernel, first, rows, all_rows), out...  7.04 us
    pallas_call x1, Pallas kernels, on_device(): pl.pallas_call(load_kernel, out_shape=VMEM(sensing.shape, sensing.dtype),...  4.58 us
  transfers between devices with their start and end apart: 39, of which 24 were waited for; matrix products, arithmetic and copies ran while one was open for 1% of the time, Pallas kernels for 5%

profile of v5, /device:TPU:0, one launch (start us, length us, event | category | flops | bytes accessed | tf_op | source)
XLA Modules:
  0.0 98.4 jit_solution(15653696142239198650)
XLA Ops:
  1.4 4.0 %collective-permute-start.2 = (f32[256]{0:T(256)S(1)}, f32[256]{0:T(256)S(1)}, u32[]{:S(2)}, u32[]{:S(2)}) collective-permute-start(f32[256]{0:T(256)S(1)} %concatenate.3), channel_id=1, source_target_pairs={{0,8},{1,9},{2,10},{3,11},{4,12},{5,13},{6,14},{7,15},{8,0},{9,1},... | collective-permute-start | bytes 3080 | tf_op jit(solution)/shard_map/ppermute | solution.py:32
  5.4 1.3 %collective-permute-start.1 = (f32[256]{0:T(256)S(1)}, f32[256]{0:T(256)S(1)}, u32[]{:S(2)}, u32[]{:S(2)}) collective-permute-start(f32[256]{0:T(256)S(1)} %concatenate.3), channel_id=1, source_target_pairs={{0,12},{1,13},{2,14},{3,15},{4,8},{5,9},{6,10},{7,11},{8,4},{9,5},... | collective-permute-start | bytes 3080 | tf_op jit(solution)/shard_map/ppermute | solution.py:32
  7.0 4.6 %load.1.refs_4_.refs_5_.refs_6_ = f32[192,16384]{1,0:T(8,128)S(1)} custom-call(f32[192,16384]{1,0:T(8,128)} %source.1), custom_call_target="tpu_custom_call" | custom-call | bytes 25165824 | tf_op jit(solution)/shard_map/load/pallas_call | solution.py:171
  11.6 1.1 %back.6 = (f32[128,128]{1,0:T(8,128)S(1)}, f32[1,256]{1,0:T(1,128)S(1)}) custom-call(f32[1,256]{1,0:T(1,128)S(1)} %bitcast.97, f32[1,256]{1,0:T(1,128)S(1)} %bitcast.130, f32[1,256]{1,0:T(1,128)S(1)} %bitcast.124, f32[1,256]{1,0:T(1,128)S(1)} %bitcast.118, f32[192,16384]{1,0:T(8,128)S(1)} %load.1.refs_4_.refs_5_.refs_6_), custom_call_target="tpu_custom_call" | custom-call | tf_op jit(solution)/shard_map/back/pallas_call | solution.py:188
  12.7 1.6 %collective-permute-start.5 = (f32[16384]{0:T(1024)S(1)}, f32[16384]{0:T(1024)S(1)}, u32[]{:S(2)}, u32[]{:S(2)}) collective-permute-start(f32[16384]{0:T(1024)S(1)} %bitcast.70), channel_id=1, source_target_pairs={{0,2},{1,3},{2,0},{3,1},{4,6},{5,7},{6,4},{7,5},{8,10},{9,11},{10,... | collective-permute-start | bytes 196616 | tf_op jit(solution)/shard_map/ppermute | solution.py:32
  14.9 2.1 %collective-permute-done.5 = f32[16384]{0:T(1024)S(1)} collective-permute-done((f32[16384]{0:T(1024)S(1)}, f32[16384]{0:T(1024)S(1)}, u32[]{:S(2)}, u32[]{:S(2)}) %collective-permute-start.5) | collective-permute-done | bytes 65568 | tf_op jit(solution)/shard_map/ppermute | solution.py:32
  18.0 1.3 %forward.6 = (f32[128,128]{1,0:T(8,128)S(1)}, f32[1,256]{1,0:T(1,128)S(1)}) custom-call(f32[1,6]{1,0:T(1,128)S(1)} %bitcast.91, f32[128,128]{1,0:T(8,128)S(1)} %get-tuple-element.26.refs_1_, f32[128,128]{1,0:T(8,128)S(1)} %bitcast.90, f32[128,128]{1,0:T(8,128)S(1)} %bitcast.84, f32[128,128]{1,0:T(8,128)S(1)} %bitcast.78, ...), custom_call_target="tpu_custom_call" | custom-call | tf_op jit(solution)/shard_map/forward/pallas_call | solution.py:198
  19.3 3.0 %collective-permute-start.8 = (f32[256]{0:T(256)S(1)}, f32[256]{0:T(256)S(1)}, u32[]{:S(2)}, u32[]{:S(2)}) collective-permute-start(f32[256]{0:T(256)S(1)} %bitcast.111), channel_id=1, source_target_pairs={{0,12},{1,13},{2,14},{3,15},{4,8},{5,9},{6,10},{7,11},{8,4},{9,5},... | collective-permute-start | bytes 3080 | tf_op jit(solution)/shard_map/ppermute | solution.py:32
  22.6 1.1 %collective-permute-start.6 = (f32[256]{0:T(256)S(1)}, f32[256]{0:T(256)S(1)}, u32[]{:S(2)}, u32[]{:S(2)}) collective-permute-start(f32[256]{0:T(256)S(1)} %bitcast.113), channel_id=1, source_target_pairs={{0,4},{1,5},{2,6},{3,7},{4,0},{5,1},{6,2},{7,3},{8,12},{9,13},{10,... | collective-permute-start | bytes 3080 | tf_op jit(solution)/shard_map/ppermute | solution.py:32
  23.7 1.0 collective-permute-done.8
  24.7 2.0 %collective-permute-done.7 = f32[256]{0:T(256)S(1)} collective-permute-done((f32[256]{0:T(256)S(1)}, f32[256]{0:T(256)S(1)}, u32[]{:S(2)}, u32[]{:S(2)}) %collective-permute-start.7) | collective-permute-done | bytes 1056 | tf_op jit(solution)/shard_map/ppermute | solution.py:32
  26.7 1.2 %back.7 = (f32[128,128]{1,0:T(8,128)S(1)}, f32[1,256]{1,0:T(1,128)S(1)}) custom-call(f32[1,256]{1,0:T(1,128)S(1)} %get-tuple-element.27.refs_0_, f32[1,256]{1,0:T(1,128)S(1)} %bitcast.131, f32[1,256]{1,0:T(1,128)S(1)} %bitcast.125, f32[1,256]{1,0:T(1,128)S(1)} %bitcast.119, f32[1,256]{1,0:T(1,128)S(1)} %get-tuple-element.28.refs_4_.refs_5_, ...), custom_call_target="tpu_custom_call" | custom-call | tf_op jit(solution)/shard_map/back/pallas_call | solution.py:188
  28.0 1.3 %collective-permute-start.11 = (f32[16384]{0:T(1024)S(1)}, f32[16384]{0:T(1024)S(1)}, u32[]{:S(2)}, u32[]{:S(2)}) collective-permute-start(f32[16384]{0:T(1024)S(1)} %bitcast.67), channel_id=1, source_target_pairs={{0,2},{1,3},{2,0},{3,1},{4,6},{5,7},{6,4},{7,5},{8,10},{9,11},{10,... | collective-permute-start | bytes 196616 | tf_op jit(solution)/shard_map/ppermute | solution.py:32
  30.2 2.3 %collective-permute-done.11 = f32[16384]{0:T(1024)S(1)} collective-permute-done((f32[16384]{0:T(1024)S(1)}, f32[16384]{0:T(1024)S(1)}, u32[]{:S(2)}, u32[]{:S(2)}) %collective-permute-start.11) | collective-permute-done | bytes 65568 | tf_op jit(solution)/shard_map/ppermute | solution.py:32
  33.1 1.3 %forward.7 = (f32[128,128]{1,0:T(8,128)S(1)}, f32[1,256]{1,0:T(1,128)S(1)}) custom-call(f32[1,6]{1,0:T(1,128)S(1)} %bitcast.92, f32[128,128]{1,0:T(8,128)S(1)} %get-tuple-element.29.refs_1_, f32[128,128]{1,0:T(8,128)S(1)} %bitcast.86, f32[128,128]{1,0:T(8,128)S(1)} %bitcast.80, f32[128,128]{1,0:T(8,128)S(1)} %bitcast.74, ...), custom_call_target="tpu_custom_call" | custom-call | tf_op jit(solution)/shard_map/forward/pallas_call | solution.py:198
  34.4 2.0 %collective-permute-start.14 = (f32[256]{0:T(256)S(1)}, f32[256]{0:T(256)S(1)}, u32[]{:S(2)}, u32[]{:S(2)}) collective-permute-start(f32[256]{0:T(256)S(1)} %bitcast.99), channel_id=1, source_target_pairs={{0,12},{1,13},{2,14},{3,15},{4,8},{5,9},{6,10},{7,11},{8,4},{9,5},... | collective-permute-start | bytes 3080 | tf_op jit(solution)/shard_map/ppermute | solution.py:32
  36.6 2.3 %collective-permute-start.12 = (f32[256]{0:T(256)S(1)}, f32[256]{0:T(256)S(1)}, u32[]{:S(2)}, u32[]{:S(2)}) collective-permute-start(f32[256]{0:T(256)S(1)} %bitcast.101), channel_id=1, source_target_pairs={{0,4},{1,5},{2,6},{3,7},{4,0},{5,1},{6,2},{7,3},{8,12},{9,13},{10,... | collective-permute-start | bytes 3080 | tf_op jit(solution)/shard_map/ppermute | solution.py:32
  39.8 1.0 %collective-permute-done.13 = f32[256]{0:T(256)S(1)} collective-permute-done((f32[256]{0:T(256)S(1)}, f32[256]{0:T(256)S(1)}, u32[]{:S(2)}, u32[]{:S(2)}) %collective-permute-start.13) | collective-permute-done | bytes 1056 | tf_op jit(solution)/shard_map/ppermute | solution.py:32
  40.9 1.2 %back.8 = (f32[128,128]{1,0:T(8,128)S(1)}, f32[1,256]{1,0:T(1,128)S(1)}) custom-call(f32[1,256]{1,0:T(1,128)S(1)} %get-tuple-element.31.refs_0_, f32[1,256]{1,0:T(1,128)S(1)} %bitcast.126, f32[1,256]{1,0:T(1,128)S(1)} %bitcast.120, f32[1,256]{1,0:T(1,128)S(1)} %bitcast.114, f32[1,256]{1,0:T(1,128)S(1)} %get-tuple-element.28.refs_4_.refs_5_, ...), custom_call_target="tpu_custom_call" | custom-call | tf_op jit(solution)/shard_map/back/pallas_call | solution.py:188
  42.1 1.4 %collective-permute-start.17 = (f32[16384]{0:T(1024)S(1)}, f32[16384]{0:T(1024)S(1)}, u32[]{:S(2)}, u32[]{:S(2)}) collective-permute-start(f32[16384]{0:T(1024)S(1)} %bitcast.58), channel_id=1, source_target_pairs={{0,2},{1,3},{2,0},{3,1},{4,6},{5,7},{6,4},{7,5},{8,10},{9,11},{10,... | collective-permute-start | bytes 196616 | tf_op jit(solution)/shard_map/ppermute | solution.py:32
  44.3 2.1 %collective-permute-done.17 = f32[16384]{0:T(1024)S(1)} collective-permute-done((f32[16384]{0:T(1024)S(1)}, f32[16384]{0:T(1024)S(1)}, u32[]{:S(2)}, u32[]{:S(2)}) %collective-permute-start.17) | collective-permute-done | bytes 65568 | tf_op jit(solution)/shard_map/ppermute | solution.py:32
  47.2 1.3 %forward.8 = (f32[128,128]{1,0:T(8,128)S(1)}, f32[1,256]{1,0:T(1,128)S(1)}) custom-call(f32[1,6]{1,0:T(1,128)S(1)} %bitcast.93, f32[128,128]{1,0:T(8,128)S(1)} %get-tuple-element.33.refs_1_, f32[128,128]{1,0:T(8,128)S(1)} %bitcast.87, f32[128,128]{1,0:T(8,128)S(1)} %bitcast.81, f32[128,128]{1,0:T(8,128)S(1)} %bitcast.75, ...), custom_call_target="tpu_custom_call" | custom-call | tf_op jit(solution)/shard_map/forward/pallas_call | solution.py:198
  48.4 2.2 %collective-permute-start.20 = (f32[256]{0:T(256)S(1)}, f32[256]{0:T(256)S(1)}, u32[]{:S(2)}, u32[]{:S(2)}) collective-permute-start(f32[256]{0:T(256)S(1)} %bitcast.102), channel_id=1, source_target_pairs={{0,12},{1,13},{2,14},{3,15},{4,8},{5,9},{6,10},{7,11},{8,4},{9,5},... | collective-permute-start | bytes 3080 | tf_op jit(solution)/shard_map/ppermute | solution.py:32
  51.5 1.3 %collective-permute-start.18 = (f32[256]{0:T(256)S(1)}, f32[256]{0:T(256)S(1)}, u32[]{:S(2)}, u32[]{:S(2)}) collective-permute-start(f32[256]{0:T(256)S(1)} %bitcast.104), channel_id=1, source_target_pairs={{0,4},{1,5},{2,6},{3,7},{4,0},{5,1},{6,2},{7,3},{8,12},{9,13},{10,... | collective-permute-start | bytes 3080 | tf_op jit(solution)/shard_map/ppermute | solution.py:32
  52.9 1.0 collective-permute-done.20
  53.9 1.2 %collective-permute-done.19 = f32[256]{0:T(256)S(1)} collective-permute-done((f32[256]{0:T(256)S(1)}, f32[256]{0:T(256)S(1)}, u32[]{:S(2)}, u32[]{:S(2)}) %collective-permute-start.19) | collective-permute-done | bytes 1056 | tf_op jit(solution)/shard_map/ppermute | solution.py:32
  55.1 1.2 %back.9 = (f32[128,128]{1,0:T(8,128)S(1)}, f32[1,256]{1,0:T(1,128)S(1)}) custom-call(f32[1,256]{1,0:T(1,128)S(1)} %get-tuple-element.35.refs_0_, f32[1,256]{1,0:T(1,128)S(1)} %bitcast.127, f32[1,256]{1,0:T(1,128)S(1)} %bitcast.121, f32[1,256]{1,0:T(1,128)S(1)} %bitcast.115, f32[1,256]{1,0:T(1,128)S(1)} %get-tuple-element.28.refs_4_.refs_5_, ...), custom_call_target="tpu_custom_call" | custom-call | tf_op jit(solution)/shard_map/back/pallas_call | solution.py:188
  56.3 1.5 %collective-permute-start.23 = (f32[16384]{0:T(1024)S(1)}, f32[16384]{0:T(1024)S(1)}, u32[]{:S(2)}, u32[]{:S(2)}) collective-permute-start(f32[16384]{0:T(1024)S(1)} %bitcast.61), channel_id=1, source_target_pairs={{0,2},{1,3},{2,0},{3,1},{4,6},{5,7},{6,4},{7,5},{8,10},{9,11},{10,... | collective-permute-start | bytes 196616 | tf_op jit(solution)/shard_map/ppermute | solution.py:32
  58.5 2.1 %collective-permute-done.23 = f32[16384]{0:T(1024)S(1)} collective-permute-done((f32[16384]{0:T(1024)S(1)}, f32[16384]{0:T(1024)S(1)}, u32[]{:S(2)}, u32[]{:S(2)}) %collective-permute-start.23) | collective-permute-done | bytes 65568 | tf_op jit(solution)/shard_map/ppermute | solution.py:32
  61.5 1.3 %forward.9 = (f32[128,128]{1,0:T(8,128)S(1)}, f32[1,256]{1,0:T(1,128)S(1)}) custom-call(f32[1,6]{1,0:T(1,128)S(1)} %bitcast.94, f32[128,128]{1,0:T(8,128)S(1)} %get-tuple-element.37.refs_1_, f32[128,128]{1,0:T(8,128)S(1)} %bitcast.88, f32[128,128]{1,0:T(8,128)S(1)} %bitcast.82, f32[128,128]{1,0:T(8,128)S(1)} %bitcast.76, ...), custom_call_target="tpu_custom_call" | custom-call | tf_op jit(solution)/shard_map/forward/pallas_call | solution.py:198
  62.8 2.0 %collective-permute-start.26 = (f32[256]{0:T(256)S(1)}, f32[256]{0:T(256)S(1)}, u32[]{:S(2)}, u32[]{:S(2)}) collective-permute-start(f32[256]{0:T(256)S(1)} %bitcast.105), channel_id=1, source_target_pairs={{0,12},{1,13},{2,14},{3,15},{4,8},{5,9},{6,10},{7,11},{8,4},{9,5},... | collective-permute-start | bytes 3080 | tf_op jit(solution)/shard_map/ppermute | solution.py:32
  65.7 1.6 %collective-permute-start.24 = (f32[256]{0:T(256)S(1)}, f32[256]{0:T(256)S(1)}, u32[]{:S(2)}, u32[]{:S(2)}) collective-permute-start(f32[256]{0:T(256)S(1)} %bitcast.107), channel_id=1, source_target_pairs={{0,4},{1,5},{2,6},{3,7},{4,0},{5,1},{6,2},{7,3},{8,12},{9,13},{10,... | collective-permute-start | bytes 3080 | tf_op jit(solution)/shard_map/ppermute | solution.py:32
  67.3 1.0 collective-permute-done.26
  68.3 1.0 %collective-permute-done.25 = f32[256]{0:T(256)S(1)} collective-permute-done((f32[256]{0:T(256)S(1)}, f32[256]{0:T(256)S(1)}, u32[]{:S(2)}, u32[]{:S(2)}) %collective-permute-start.25) | collective-permute-done | bytes 1056 | tf_op jit(solution)/shard_map/ppermute | solution.py:32
  69.3 1.2 %back.10 = (f32[128,128]{1,0:T(8,128)S(1)}, f32[1,256]{1,0:T(1,128)S(1)}) custom-call(f32[1,256]{1,0:T(1,128)S(1)} %get-tuple-element.39.refs_0_, f32[1,256]{1,0:T(1,128)S(1)} %bitcast.128, f32[1,256]{1,0:T(1,128)S(1)} %bitcast.122, f32[1,256]{1,0:T(1,128)S(1)} %bitcast.116, f32[1,256]{1,0:T(1,128)S(1)} %get-tuple-element.28.refs_4_.refs_5_, ...), custom_call_target="tpu_custom_call" | custom-call | tf_op jit(solution)/shard_map/back/pallas_call | solution.py:188
  70.5 1.3 %collective-permute-start.29 = (f32[16384]{0:T(1024)S(1)}, f32[16384]{0:T(1024)S(1)}, u32[]{:S(2)}, u32[]{:S(2)}) collective-permute-start(f32[16384]{0:T(1024)S(1)} %bitcast.64), channel_id=1, source_target_pairs={{0,2},{1,3},{2,0},{3,1},{4,6},{5,7},{6,4},{7,5},{8,10},{9,11},{10,... | collective-permute-start | bytes 196616 | tf_op jit(solution)/shard_map/ppermute | solution.py:32
  72.7 2.1 %collective-permute-done.29 = f32[16384]{0:T(1024)S(1)} collective-permute-done((f32[16384]{0:T(1024)S(1)}, f32[16384]{0:T(1024)S(1)}, u32[]{:S(2)}, u32[]{:S(2)}) %collective-permute-start.29) | collective-permute-done | bytes 65568 | tf_op jit(solution)/shard_map/ppermute | solution.py:32
  75.6 1.3 %forward.10 = (f32[128,128]{1,0:T(8,128)S(1)}, f32[1,256]{1,0:T(1,128)S(1)}) custom-call(f32[1,6]{1,0:T(1,128)S(1)} %bitcast.95, f32[128,128]{1,0:T(8,128)S(1)} %get-tuple-element.41.refs_1_, f32[128,128]{1,0:T(8,128)S(1)} %bitcast.89, f32[128,128]{1,0:T(8,128)S(1)} %bitcast.83, f32[128,128]{1,0:T(8,128)S(1)} %bitcast.77, ...), custom_call_target="tpu_custom_call" | custom-call | tf_op jit(solution)/shard_map/forward/pallas_call | solution.py:198
  76.8 2.2 %collective-permute-start.32 = (f32[256]{0:T(256)S(1)}, f32[256]{0:T(256)S(1)}, u32[]{:S(2)}, u32[]{:S(2)}) collective-permute-start(f32[256]{0:T(256)S(1)} %bitcast.108), channel_id=1, source_target_pairs={{0,12},{1,13},{2,14},{3,15},{4,8},{5,9},{6,10},{7,11},{8,4},{9,5},... | collective-permute-start | bytes 3080 | tf_op jit(solution)/shard_map/ppermute | solution.py:32
  79.9 1.3 %collective-permute-start.30 = (f32[256]{0:T(256)S(1)}, f32[256]{0:T(256)S(1)}, u32[]{:S(2)}, u32[]{:S(2)}) collective-permute-start(f32[256]{0:T(256)S(1)} %bitcast.110), channel_id=1, source_target_pairs={{0,4},{1,5},{2,6},{3,7},{4,0},{5,1},{6,2},{7,3},{8,12},{9,13},{10,... | collective-permute-start | bytes 3080 | tf_op jit(solution)/shard_map/ppermute | solution.py:32
  82.3 1.2 %collective-permute-done.31 = f32[256]{0:T(256)S(1)} collective-permute-done((f32[256]{0:T(256)S(1)}, f32[256]{0:T(256)S(1)}, u32[]{:S(2)}, u32[]{:S(2)}) %collective-permute-start.31) | collective-permute-done | bytes 1056 | tf_op jit(solution)/shard_map/ppermute | solution.py:32
  83.5 1.2 %back.11 = (f32[128,128]{1,0:T(8,128)S(1)}, f32[1,256]{1,0:T(1,128)S(1)}) custom-call(f32[1,256]{1,0:T(1,128)S(1)} %get-tuple-element.43.refs_0_, f32[1,256]{1,0:T(1,128)S(1)} %bitcast.129, f32[1,256]{1,0:T(1,128)S(1)} %bitcast.123, f32[1,256]{1,0:T(1,128)S(1)} %bitcast.117, f32[1,256]{1,0:T(1,128)S(1)} %get-tuple-element.28.refs_4_.refs_5_, ...), custom_call_target="tpu_custom_call" | custom-call | tf_op jit(solution)/shard_map/back/pallas_call | solution.py:188
  84.7 1.5 %collective-permute-start.35 = (f32[16384]{0:T(1024)S(1)}, f32[16384]{0:T(1024)S(1)}, u32[]{:S(2)}, u32[]{:S(2)}) collective-permute-start(f32[16384]{0:T(1024)S(1)} %bitcast.55), channel_id=1, source_target_pairs={{0,2},{1,3},{2,0},{3,1},{4,6},{5,7},{6,4},{7,5},{8,10},{9,11},{10,... | collective-permute-start | bytes 196616 | tf_op jit(solution)/shard_map/ppermute | solution.py:32
  86.9 2.1 %collective-permute-done.35 = f32[16384]{0:T(1024)S(1)} collective-permute-done((f32[16384]{0:T(1024)S(1)}, f32[16384]{0:T(1024)S(1)}, u32[]{:S(2)}, u32[]{:S(2)}) %collective-permute-start.35) | collective-permute-done | bytes 65568 | tf_op jit(solution)/shard_map/ppermute | solution.py:32
  89.9 1.3 %forward.11 = (f32[128,128]{1,0:T(8,128)S(1)}, f32[1,256]{1,0:T(1,128)S(1)}) custom-call(f32[1,6]{1,0:T(1,128)S(1)} %bitcast.96, f32[128,128]{1,0:T(8,128)S(1)} %get-tuple-element.45.refs_1_, f32[128,128]{1,0:T(8,128)S(1)} %bitcast.85, f32[128,128]{1,0:T(8,128)S(1)} %bitcast.79, f32[128,128]{1,0:T(8,128)S(1)} %bitcast.73, ...), custom_call_target="tpu_custom_call" | custom-call | tf_op jit(solution)/shard_map/forward/pallas_call | solution.py:198
  91.2 2.0 %collective-permute-start.38 = (f32[256]{0:T(256)S(1)}, f32[256]{0:T(256)S(1)}, u32[]{:S(2)}, u32[]{:S(2)}) collective-permute-start(f32[256]{0:T(256)S(1)} %bitcast.132), channel_id=1, source_target_pairs={{0,12},{1,13},{2,14},{3,15},{4,8},{5,9},{6,10},{7,11},{8,4},{9,5},... | collective-permute-start | bytes 3080 | tf_op jit(solution)/shard_map/ppermute | solution.py:32
  94.1 1.6 %collective-permute-start.36 = (f32[256]{0:T(256)S(1)}, f32[256]{0:T(256)S(1)}, u32[]{:S(2)}, u32[]{:S(2)}) collective-permute-start(f32[256]{0:T(256)S(1)} %bitcast.134), channel_id=1, source_target_pairs={{0,4},{1,5},{2,6},{3,7},{4,0},{5,1},{6,2},{7,3},{8,12},{9,13},{10,... | collective-permute-start | bytes 3080 | tf_op jit(solution)/shard_map/ppermute | solution.py:32
  96.6 1.0 %collective-permute-done.37 = f32[256]{0:T(256)S(1)} collective-permute-done((f32[256]{0:T(256)S(1)}, f32[256]{0:T(256)S(1)}, u32[]{:S(2)}, u32[]{:S(2)}) %collective-permute-start.37) | collective-permute-done | bytes 1056 | tf_op jit(solution)/shard_map/ppermute | solution.py:32
  (50 shorter events, 18.6 us)
Async XLA Ops:
  1.4 10.2 %collective-permute-start.2 = (f32[256]{0:T(256)S(1)}, f32[256]{0:T(256)S(1)}, u32[]{:S(2)}, u32[]{:S(2)}) collective-permute-start(f32[256]{0:T(256)S(1)} %concatenate.3), channel_id=1, source_target_pairs={{0,8},{1,9},{2,10},{3,11},{4,12},{5,13},{6,14},{7,15},{8,0},{9,1},... | collective-permute-start | bytes 3080 | tf_op jit(solution)/shard_map/ppermute | solution.py:32
  5.4 6.2 %collective-permute-start.1 = (f32[256]{0:T(256)S(1)}, f32[256]{0:T(256)S(1)}, u32[]{:S(2)}, u32[]{:S(2)}) collective-permute-start(f32[256]{0:T(256)S(1)} %concatenate.3), channel_id=1, source_target_pairs={{0,12},{1,13},{2,14},{3,15},{4,8},{5,9},{6,10},{7,11},{8,4},{9,5},... | collective-permute-start | bytes 3080 | tf_op jit(solution)/shard_map/ppermute | solution.py:32
  6.8 4.9 %collective-permute-start = (f32[256]{0:T(256)S(1)}, f32[256]{0:T(256)S(1)}, u32[]{:S(2)}, u32[]{:S(2)}) collective-permute-start(f32[256]{0:T(256)S(1)} %concatenate.3), channel_id=1, source_target_pairs={{0,4},{1,5},{2,6},{3,7},{4,0},{5,1},{6,2},{7,3},{8,12},{9,13},{10,... | collective-permute-start | bytes 3080 | tf_op jit(solution)/shard_map/ppermute | solution.py:32
  11.6 6.4 %copy-start = (f32[6]{0:T(128)S(1)}, f32[6]{0:T(128)}, u32[]{:S(2)}) copy-start(f32[6]{0:T(128)} %param.5) | copy-start | bytes 76
  12.7 4.3 %collective-permute-start.5 = (f32[16384]{0:T(1024)S(1)}, f32[16384]{0:T(1024)S(1)}, u32[]{:S(2)}, u32[]{:S(2)}) collective-permute-start(f32[16384]{0:T(1024)S(1)} %bitcast.70), channel_id=1, source_target_pairs={{0,2},{1,3},{2,0},{3,1},{4,6},{5,7},{6,4},{7,5},{8,10},{9,11},{10,... | collective-permute-start | bytes 196616 | tf_op jit(solution)/shard_map/ppermute | solution.py:32
  14.3 2.8 %collective-permute-start.4 = (f32[16384]{0:T(1024)S(1)}, f32[16384]{0:T(1024)S(1)}, u32[]{:S(2)}, u32[]{:S(2)}) collective-permute-start(f32[16384]{0:T(1024)S(1)} %bitcast.71), channel_id=1, source_target_pairs={{0,1},{1,0},{2,3},{3,2},{4,5},{5,4},{6,7},{7,6},{8,9},{9,8},{10,11... | collective-permute-start | bytes 196616 | tf_op jit(solution)/shard_map/ppermute | solution.py:32
  14.3 3.7 %collective-permute-start.3 = (f32[16384]{0:T(1024)S(1)}, f32[16384]{0:T(1024)S(1)}, u32[]{:S(2)}, u32[]{:S(2)}) collective-permute-start(f32[16384]{0:T(1024)S(1)} %bitcast.72), channel_id=1, source_target_pairs={{0,3},{1,2},{2,1},{3,0},{4,7},{5,6},{6,5},{7,4},{8,11},{9,10},{10,... | collective-permute-start | bytes 196616 | tf_op jit(solution)/shard_map/ppermute | solution.py:32
  19.3 5.4 %collective-permute-start.8 = (f32[256]{0:T(256)S(1)}, f32[256]{0:T(256)S(1)}, u32[]{:S(2)}, u32[]{:S(2)}) collective-permute-start(f32[256]{0:T(256)S(1)} %bitcast.111), channel_id=1, source_target_pairs={{0,12},{1,13},{2,14},{3,15},{4,8},{5,9},{6,10},{7,11},{8,4},{9,5},... | collective-permute-start | bytes 3080 | tf_op jit(solution)/shard_map/ppermute | solution.py:32
  22.3 4.5 %collective-permute-start.7 = (f32[256]{0:T(256)S(1)}, f32[256]{0:T(256)S(1)}, u32[]{:S(2)}, u32[]{:S(2)}) collective-permute-start(f32[256]{0:T(256)S(1)} %bitcast.112), channel_id=1, source_target_pairs={{0,8},{1,9},{2,10},{3,11},{4,12},{5,13},{6,14},{7,15},{8,0},{9,1},... | collective-permute-start | bytes 3080 | tf_op jit(solution)/shard_map/ppermute | solution.py:32
  22.6 4.1 %collective-permute-start.6 = (f32[256]{0:T(256)S(1)}, f32[256]{0:T(256)S(1)}, u32[]{:S(2)}, u32[]{:S(2)}) collective-permute-start(f32[256]{0:T(256)S(1)} %bitcast.113), channel_id=1, source_target_pairs={{0,4},{1,5},{2,6},{3,7},{4,0},{5,1},{6,2},{7,3},{8,12},{9,13},{10,... | collective-permute-start | bytes 3080 | tf_op jit(solution)/shard_map/ppermute | solution.py:32
  28.0 4.5 %collective-permute-start.11 = (f32[16384]{0:T(1024)S(1)}, f32[16384]{0:T(1024)S(1)}, u32[]{:S(2)}, u32[]{:S(2)}) collective-permute-start(f32[16384]{0:T(1024)S(1)} %bitcast.67), channel_id=1, source_target_pairs={{0,2},{1,3},{2,0},{3,1},{4,6},{5,7},{6,4},{7,5},{8,10},{9,11},{10,... | collective-permute-start | bytes 196616 | tf_op jit(solution)/shard_map/ppermute | solution.py:32
  29.2 3.2 %collective-permute-start.10 = (f32[16384]{0:T(1024)S(1)}, f32[16384]{0:T(1024)S(1)}, u32[]{:S(2)}, u32[]{:S(2)}) collective-permute-start(f32[16384]{0:T(1024)S(1)} %bitcast.68), channel_id=1, source_target_pairs={{0,1},{1,0},{2,3},{3,2},{4,5},{5,4},{6,7},{7,6},{8,9},{9,8},{10,11... | collective-permute-start | bytes 196616 | tf_op jit(solution)/shard_map/ppermute | solution.py:32
  29.2 3.9 %collective-permute-start.9 = (f32[16384]{0:T(1024)S(1)}, f32[16384]{0:T(1024)S(1)}, u32[]{:S(2)}, u32[]{:S(2)}) collective-permute-start(f32[16384]{0:T(1024)S(1)} %bitcast.69), channel_id=1, source_target_pairs={{0,3},{1,2},{2,1},{3,0},{4,7},{5,6},{6,5},{7,4},{8,11},{9,10},{10,... | collective-permute-start | bytes 196616 | tf_op jit(solution)/shard_map/ppermute | solution.py:32
  34.4 5.5 %collective-permute-start.14 = (f32[256]{0:T(256)S(1)}, f32[256]{0:T(256)S(1)}, u32[]{:S(2)}, u32[]{:S(2)}) collective-permute-start(f32[256]{0:T(256)S(1)} %bitcast.99), channel_id=1, source_target_pairs={{0,12},{1,13},{2,14},{3,15},{4,8},{5,9},{6,10},{7,11},{8,4},{9,5},... | collective-permute-start | bytes 3080 | tf_op jit(solution)/shard_map/ppermute | solution.py:32
  36.4 4.5 %collective-permute-start.13 = (f32[256]{0:T(256)S(1)}, f32[256]{0:T(256)S(1)}, u32[]{:S(2)}, u32[]{:S(2)}) collective-permute-start(f32[256]{0:T(256)S(1)} %bitcast.100), channel_id=1, source_target_pairs={{0,8},{1,9},{2,10},{3,11},{4,12},{5,13},{6,14},{7,15},{8,0},{9,1},... | collective-permute-start | bytes 3080 | tf_op jit(solution)/shard_map/ppermute | solution.py:32
  36.6 4.3 %collective-permute-start.12 = (f32[256]{0:T(256)S(1)}, f32[256]{0:T(256)S(1)}, u32[]{:S(2)}, u32[]{:S(2)}) collective-permute-start(f32[256]{0:T(256)S(1)} %bitcast.101), channel_id=1, source_target_pairs={{0,4},{1,5},{2,6},{3,7},{4,0},{5,1},{6,2},{7,3},{8,12},{9,13},{10,... | collective-permute-start | bytes 3080 | tf_op jit(solution)/shard_map/ppermute | solution.py:32
  42.1 4.3 %collective-permute-start.17 = (f32[16384]{0:T(1024)S(1)}, f32[16384]{0:T(1024)S(1)}, u32[]{:S(2)}, u32[]{:S(2)}) collective-permute-start(f32[16384]{0:T(1024)S(1)} %bitcast.58), channel_id=1, source_target_pairs={{0,2},{1,3},{2,0},{3,1},{4,6},{5,7},{6,4},{7,5},{8,10},{9,11},{10,... | collective-permute-start | bytes 196616 | tf_op jit(solution)/shard_map/ppermute | solution.py:32
  43.4 3.0 %collective-permute-start.16 = (f32[16384]{0:T(1024)S(1)}, f32[16384]{0:T(1024)S(1)}, u32[]{:S(2)}, u32[]{:S(2)}) collective-permute-start(f32[16384]{0:T(1024)S(1)} %bitcast.59), channel_id=1, source_target_pairs={{0,1},{1,0},{2,3},{3,2},{4,5},{5,4},{6,7},{7,6},{8,9},{9,8},{10,11... | collective-permute-start | bytes 196616 | tf_op jit(solution)/shard_map/ppermute | solution.py:32
  43.4 3.7 %collective-permute-start.15 = (f32[16384]{0:T(1024)S(1)}, f32[16384]{0:T(1024)S(1)}, u32[]{:S(2)}, u32[]{:S(2)}) collective-permute-start(f32[16384]{0:T(1024)S(1)} %bitcast.60), channel_id=1, source_target_pairs={{0,3},{1,2},{2,1},{3,0},{4,7},{5,6},{6,5},{7,4},{8,11},{9,10},{10,... | collective-permute-start | bytes 196616 | tf_op jit(solution)/shard_map/ppermute | solution.py:32
  48.4 5.4 %collective-permute-start.20 = (f32[256]{0:T(256)S(1)}, f32[256]{0:T(256)S(1)}, u32[]{:S(2)}, u32[]{:S(2)}) collective-permute-start(f32[256]{0:T(256)S(1)} %bitcast.102), channel_id=1, source_target_pairs={{0,12},{1,13},{2,14},{3,15},{4,8},{5,9},{6,10},{7,11},{8,4},{9,5},... | collective-permute-start | bytes 3080 | tf_op jit(solution)/shard_map/ppermute | solution.py:32
  50.6 4.5 %collective-permute-start.19 = (f32[256]{0:T(256)S(1)}, f32[256]{0:T(256)S(1)}, u32[]{:S(2)}, u32[]{:S(2)}) collective-permute-start(f32[256]{0:T(256)S(1)} %bitcast.103), channel_id=1, source_target_pairs={{0,8},{1,9},{2,10},{3,11},{4,12},{5,13},{6,14},{7,15},{8,0},{9,1},... | collective-permute-start | bytes 3080 | tf_op jit(solution)/shard_map/ppermute | solution.py:32
  51.5 3.6 %collective-permute-start.18 = (f32[256]{0:T(256)S(1)}, f32[256]{0:T(256)S(1)}, u32[]{:S(2)}, u32[]{:S(2)}) collective-permute-start(f32[256]{0:T(256)S(1)} %bitcast.104), channel_id=1, source_target_pairs={{0,4},{1,5},{2,6},{3,7},{4,0},{5,1},{6,2},{7,3},{8,12},{9,13},{10,... | collective-permute-start | bytes 3080 | tf_op jit(solution)/shard_map/ppermute | solution.py:32
  56.3 4.3 %collective-permute-start.23 = (f32[16384]{0:T(1024)S(1)}, f32[16384]{0:T(1024)S(1)}, u32[]{:S(2)}, u32[]{:S(2)}) collective-permute-start(f32[16384]{0:T(1024)S(1)} %bitcast.61), channel_id=1, source_target_pairs={{0,2},{1,3},{2,0},{3,1},{4,6},{5,7},{6,4},{7,5},{8,10},{9,11},{10,... | collective-permute-start | bytes 196616 | tf_op jit(solution)/shard_map/ppermute | solution.py:32
  57.8 2.9 %collective-permute-start.22 = (f32[16384]{0:T(1024)S(1)}, f32[16384]{0:T(1024)S(1)}, u32[]{:S(2)}, u32[]{:S(2)}) collective-permute-start(f32[16384]{0:T(1024)S(1)} %bitcast.62), channel_id=1, source_target_pairs={{0,1},{1,0},{2,3},{3,2},{4,5},{5,4},{6,7},{7,6},{8,9},{9,8},{10,11... | collective-permute-start | bytes 196616 | tf_op jit(solution)/shard_map/ppermute | solution.py:32
  57.8 3.7 %collective-permute-start.21 = (f32[16384]{0:T(1024)S(1)}, f32[16384]{0:T(1024)S(1)}, u32[]{:S(2)}, u32[]{:S(2)}) collective-permute-start(f32[16384]{0:T(1024)S(1)} %bitcast.63), channel_id=1, source_target_pairs={{0,3},{1,2},{2,1},{3,0},{4,7},{5,6},{6,5},{7,4},{8,11},{9,10},{10,... | collective-permute-start | bytes 196616 | tf_op jit(solution)/shard_map/ppermute | solution.py:32
  62.8 5.4 %collective-permute-start.26 = (f32[256]{0:T(256)S(1)}, f32[256]{0:T(256)S(1)}, u32[]{:S(2)}, u32[]{:S(2)}) collective-permute-start(f32[256]{0:T(256)S(1)} %bitcast.105), channel_id=1, source_target_pairs={{0,12},{1,13},{2,14},{3,15},{4,8},{5,9},{6,10},{7,11},{8,4},{9,5},... | collective-permute-start | bytes 3080 | tf_op jit(solution)/shard_map/ppermute | solution.py:32
  64.8 4.5 %collective-permute-start.25 = (f32[256]{0:T(256)S(1)}, f32[256]{0:T(256)S(1)}, u32[]{:S(2)}, u32[]{:S(2)}) collective-permute-start(f32[256]{0:T(256)S(1)} %bitcast.106), channel_id=1, source_target_pairs={{0,8},{1,9},{2,10},{3,11},{4,12},{5,13},{6,14},{7,15},{8,0},{9,1},... | collective-permute-start | bytes 3080 | tf_op jit(solution)/shard_map/ppermute | solution.py:32
  65.7 3.6 %collective-permute-start.24 = (f32[256]{0:T(256)S(1)}, f32[256]{0:T(256)S(1)}, u32[]{:S(2)}, u32[]{:S(2)}) collective-permute-start(f32[256]{0:T(256)S(1)} %bitcast.107), channel_id=1, source_target_pairs={{0,4},{1,5},{2,6},{3,7},{4,0},{5,1},{6,2},{7,3},{8,12},{9,13},{10,... | collective-permute-start | bytes 3080 | tf_op jit(solution)/shard_map/ppermute | solution.py:32
  70.5 4.3 %collective-permute-start.29 = (f32[16384]{0:T(1024)S(1)}, f32[16384]{0:T(1024)S(1)}, u32[]{:S(2)}, u32[]{:S(2)}) collective-permute-start(f32[16384]{0:T(1024)S(1)} %bitcast.64), channel_id=1, source_target_pairs={{0,2},{1,3},{2,0},{3,1},{4,6},{5,7},{6,4},{7,5},{8,10},{9,11},{10,... | collective-permute-start | bytes 196616 | tf_op jit(solution)/shard_map/ppermute | solution.py:32
  71.8 3.0 %collective-permute-start.28 = (f32[16384]{0:T(1024)S(1)}, f32[16384]{0:T(1024)S(1)}, u32[]{:S(2)}, u32[]{:S(2)}) collective-permute-start(f32[16384]{0:T(1024)S(1)} %bitcast.65), channel_id=1, source_target_pairs={{0,1},{1,0},{2,3},{3,2},{4,5},{5,4},{6,7},{7,6},{8,9},{9,8},{10,11... | collective-permute-start | bytes 196616 | tf_op jit(solution)/shard_map/ppermute | solution.py:32
  71.8 3.7 %collective-permute-start.27 = (f32[16384]{0:T(1024)S(1)}, f32[16384]{0:T(1024)S(1)}, u32[]{:S(2)}, u32[]{:S(2)}) collective-permute-start(f32[16384]{0:T(1024)S(1)} %bitcast.66), channel_id=1, source_target_pairs={{0,3},{1,2},{2,1},{3,0},{4,7},{5,6},{6,5},{7,4},{8,11},{9,10},{10,... | collective-permute-start | bytes 196616 | tf_op jit(solution)/shard_map/ppermute | solution.py:32
  76.8 5.4 %collective-permute-start.32 = (f32[256]{0:T(256)S(1)}, f32[256]{0:T(256)S(1)}, u32[]{:S(2)}, u32[]{:S(2)}) collective-permute-start(f32[256]{0:T(256)S(1)} %bitcast.108), channel_id=1, source_target_pairs={{0,12},{1,13},{2,14},{3,15},{4,8},{5,9},{6,10},{7,11},{8,4},{9,5},... | collective-permute-start | bytes 3080 | tf_op jit(solution)/shard_map/ppermute | solution.py:32
  79.0 4.5 %collective-permute-start.31 = (f32[256]{0:T(256)S(1)}, f32[256]{0:T(256)S(1)}, u32[]{:S(2)}, u32[]{:S(2)}) collective-permute-start(f32[256]{0:T(256)S(1)} %bitcast.109), channel_id=1, source_target_pairs={{0,8},{1,9},{2,10},{3,11},{4,12},{5,13},{6,14},{7,15},{8,0},{9,1},... | collective-permute-start | bytes 3080 | tf_op jit(solution)/shard_map/ppermute | solution.py:32
  79.9 3.6 %collective-permute-start.30 = (f32[256]{0:T(256)S(1)}, f32[256]{0:T(256)S(1)}, u32[]{:S(2)}, u32[]{:S(2)}) collective-permute-start(f32[256]{0:T(256)S(1)} %bitcast.110), channel_id=1, source_target_pairs={{0,4},{1,5},{2,6},{3,7},{4,0},{5,1},{6,2},{7,3},{8,12},{9,13},{10,... | collective-permute-start | bytes 3080 | tf_op jit(solution)/shard_map/ppermute | solution.py:32
  84.7 4.3 %collective-permute-start.35 = (f32[16384]{0:T(1024)S(1)}, f32[16384]{0:T(1024)S(1)}, u32[]{:S(2)}, u32[]{:S(2)}) collective-permute-start(f32[16384]{0:T(1024)S(1)} %bitcast.55), channel_id=1, source_target_pairs={{0,2},{1,3},{2,0},{3,1},{4,6},{5,7},{6,4},{7,5},{8,10},{9,11},{10,... | collective-permute-start | bytes 196616 | tf_op jit(solution)/shard_map/ppermute | solution.py:32
  86.2 2.9 %collective-permute-start.34 = (f32[16384]{0:T(1024)S(1)}, f32[16384]{0:T(1024)S(1)}, u32[]{:S(2)}, u32[]{:S(2)}) collective-permute-start(f32[16384]{0:T(1024)S(1)} %bitcast.56), channel_id=1, source_target_pairs={{0,1},{1,0},{2,3},{3,2},{4,5},{5,4},{6,7},{7,6},{8,9},{9,8},{10,11... | collective-permute-start | bytes 196616 | tf_op jit(solution)/shard_map/ppermute | solution.py:32
  86.2 3.7 %collective-permute-start.33 = (f32[16384]{0:T(1024)S(1)}, f32[16384]{0:T(1024)S(1)}, u32[]{:S(2)}, u32[]{:S(2)}) collective-permute-start(f32[16384]{0:T(1024)S(1)} %bitcast.57), channel_id=1, source_target_pairs={{0,3},{1,2},{2,1},{3,0},{4,7},{5,6},{6,5},{7,4},{8,11},{9,10},{10,... | collective-permute-start | bytes 196616 | tf_op jit(solution)/shard_map/ppermute | solution.py:32
  91.2 5.4 %collective-permute-start.38 = (f32[256]{0:T(256)S(1)}, f32[256]{0:T(256)S(1)}, u32[]{:S(2)}, u32[]{:S(2)}) collective-permute-start(f32[256]{0:T(256)S(1)} %bitcast.132), channel_id=1, source_target_pairs={{0,12},{1,13},{2,14},{3,15},{4,8},{5,9},{6,10},{7,11},{8,4},{9,5},... | collective-permute-start | bytes 3080 | tf_op jit(solution)/shard_map/ppermute | solution.py:32
  93.2 4.5 %collective-permute-start.37 = (f32[256]{0:T(256)S(1)}, f32[256]{0:T(256)S(1)}, u32[]{:S(2)}, u32[]{:S(2)}) collective-permute-start(f32[256]{0:T(256)S(1)} %bitcast.133), channel_id=1, source_target_pairs={{0,8},{1,9},{2,10},{3,11},{4,12},{5,13},{6,14},{7,15},{8,0},{9,1},... | collective-permute-start | bytes 3080 | tf_op jit(solution)/shard_map/ppermute | solution.py:32
  94.1 3.6 %collective-permute-start.36 = (f32[256]{0:T(256)S(1)}, f32[256]{0:T(256)S(1)}, u32[]{:S(2)}, u32[]{:S(2)}) collective-permute-start(f32[256]{0:T(256)S(1)} %bitcast.134), channel_id=1, source_target_pairs={{0,4},{1,5},{2,6},{3,7},{4,0},{5,1},{6,2},{7,3},{8,12},{9,13},{10,... | collective-permute-start | bytes 3080 | tf_op jit(solution)/shard_map/ppermute | solution.py:32

commit v6 on v5

--- a/solution.py
+++ b/solution.py
@@ -12,6 +12,7 @@
 SOFTNESS = 0.25
 LANES = 128
 UNROLL = 16
+BACK_UNROLL = 32
 COLUMN_ORDER = (1, 2, 3)
 ROW_ORDER = (3, 1, 2)
 GATHER_ORDER = (1, 3, 2)
@@ -109,19 +110,19 @@
     columns = jnp.broadcast_to(residual, (LANES, residual.shape[1])).T
 
     def step(group, carry):
-        start = pl.multiple_of(group * UNROLL * LANES, UNROLL * LANES)
-        sums = [None] * UNROLL
+        start = pl.multiple_of(group * BACK_UNROLL * LANES, BACK_UNROLL * LANES)
+        sums = [None] * BACK_UNROLL
         for at in range(0, rows, 8):
-            block = sensing[pl.ds(at, 8), pl.ds(start, UNROLL * LANES)]
-            for tile in range(UNROLL):
+            block = sensing[pl.ds(at, 8), pl.ds(start, BACK_UNROLL * LANES)]
+            for tile in range(BACK_UNROLL):
                 term = block[:, tile * LANES : (tile + 1) * LANES] * columns[at : at + 8]
                 sums[tile] = term if at == 0 else sums[tile] + term
-        out[pl.ds(pl.multiple_of(group * UNROLL, UNROLL), UNROLL), :] = jnp.concatenate(
+        out[pl.ds(pl.multiple_of(group * BACK_UNROLL, BACK_UNROLL), BACK_UNROLL), :] = jnp.concatenate(
             [jnp.sum(total, axis=0, keepdims=True) for total in sums]
         )
         return carry
 
-    lax.fori_loop(0, out.shape[0] // UNROLL, step, 0)
+    lax.fori_loop(0, out.shape[0] // BACK_UNROLL, step, 0)
 
 
 def forward_kernel(first, rows, step_at, order, *refs):

time: 98.5 us -> 98.4 us (level)
  no operation moved by 1% of the time
where the time goes in v6:
time: 98.4 us; the launch traced here: 98.2 us
  starting transfers between devices  45.6 us (46%)
  waiting for transfers between devices  30.7 us (31%)
  Pallas kernels  19.8 us (20%)
    ppermute x39, starting transfers between devices, swapped(): return lax.ppermute(value, 'row', pairs)  45.6 us
    ppermute x39, waiting for transfers between devices, swapped(): return lax.ppermute(value, 'row', pairs)  30.7 us
    pallas_call x6, Pallas kernels, forward(): pl.pallas_call(functools.partial(forward_kernel, first, rows, step, row_o...  7.59 us
    pallas_call x6, Pallas kernels, back(): pl.pallas_call(functools.partial(back_kernel, first, rows, all_rows), out...  6.9 us
    pallas_call x1, Pallas kernels, on_device(): pl.pallas_call(load_kernel, out_shape=VMEM(sensing.shape, sensing.dtype),...  4.58 us
  transfers between devices with their start and end apart: 39, of which 24 were waited for; matrix products, arithmetic and copies ran while one was open for 1% of the time, Pallas kernels for 5%

profile of v6, /device:TPU:0, one launch (start us, length us, event | category | flops | bytes accessed | tf_op | source)
XLA Modules:
  0.0 98.2 jit_solution(5007790465157049568)
XLA Ops:
  1.4 4.0 %collective-permute-start.2 = (f32[256]{0:T(256)S(1)}, f32[256]{0:T(256)S(1)}, u32[]{:S(2)}, u32[]{:S(2)}) collective-permute-start(f32[256]{0:T(256)S(1)} %concatenate.3), channel_id=1, source_target_pairs={{0,8},{1,9},{2,10},{3,11},{4,12},{5,13},{6,14},{7,15},{8,0},{9,1},... | collective-permute-start | bytes 3080 | tf_op jit(solution)/shard_map/ppermute | solution.py:33
  5.4 1.3 %collective-permute-start.1 = (f32[256]{0:T(256)S(1)}, f32[256]{0:T(256)S(1)}, u32[]{:S(2)}, u32[]{:S(2)}) collective-permute-start(f32[256]{0:T(256)S(1)} %concatenate.3), channel_id=1, source_target_pairs={{0,12},{1,13},{2,14},{3,15},{4,8},{5,9},{6,10},{7,11},{8,4},{9,5},... | collective-permute-start | bytes 3080 | tf_op jit(solution)/shard_map/ppermute | solution.py:33
  7.0 4.6 %load.1.refs_4_.refs_5_.refs_6_ = f32[192,16384]{1,0:T(8,128)S(1)} custom-call(f32[192,16384]{1,0:T(8,128)} %source.1), custom_call_target="tpu_custom_call" | custom-call | bytes 25165824 | tf_op jit(solution)/shard_map/load/pallas_call | solution.py:172
  11.6 1.0 %back.6 = (f32[128,128]{1,0:T(8,128)S(1)}, f32[1,256]{1,0:T(1,128)S(1)}) custom-call(f32[1,256]{1,0:T(1,128)S(1)} %bitcast.97, f32[1,256]{1,0:T(1,128)S(1)} %bitcast.130, f32[1,256]{1,0:T(1,128)S(1)} %bitcast.124, f32[1,256]{1,0:T(1,128)S(1)} %bitcast.118, f32[192,16384]{1,0:T(8,128)S(1)} %load.1.refs_4_.refs_5_.refs_6_), custom_call_target="tpu_custom_call" | custom-call | tf_op jit(solution)/shard_map/back/pallas_call | solution.py:189
  12.7 1.6 %collective-permute-start.5 = (f32[16384]{0:T(1024)S(1)}, f32[16384]{0:T(1024)S(1)}, u32[]{:S(2)}, u32[]{:S(2)}) collective-permute-start(f32[16384]{0:T(1024)S(1)} %bitcast.70), channel_id=1, source_target_pairs={{0,2},{1,3},{2,0},{3,1},{4,6},{5,7},{6,4},{7,5},{8,10},{9,11},{10,... | collective-permute-start | bytes 196616 | tf_op jit(solution)/shard_map/ppermute | solution.py:33
  14.9 2.1 %collective-permute-done.5 = f32[16384]{0:T(1024)S(1)} collective-permute-done((f32[16384]{0:T(1024)S(1)}, f32[16384]{0:T(1024)S(1)}, u32[]{:S(2)}, u32[]{:S(2)}) %collective-permute-start.5) | collective-permute-done | bytes 65568 | tf_op jit(solution)/shard_map/ppermute | solution.py:33
  18.0 1.3 %forward.6 = (f32[128,128]{1,0:T(8,128)S(1)}, f32[1,256]{1,0:T(1,128)S(1)}) custom-call(f32[1,6]{1,0:T(1,128)S(1)} %bitcast.91, f32[128,128]{1,0:T(8,128)S(1)} %get-tuple-element.26.refs_1_, f32[128,128]{1,0:T(8,128)S(1)} %bitcast.90, f32[128,128]{1,0:T(8,128)S(1)} %bitcast.84, f32[128,128]{1,0:T(8,128)S(1)} %bitcast.78, ...), custom_call_target="tpu_custom_call" | custom-call | tf_op jit(solution)/shard_map/forward/pallas_call | solution.py:199
  19.3 3.0 %collective-permute-start.8 = (f32[256]{0:T(256)S(1)}, f32[256]{0:T(256)S(1)}, u32[]{:S(2)}, u32[]{:S(2)}) collective-permute-start(f32[256]{0:T(256)S(1)} %bitcast.111), channel_id=1, source_target_pairs={{0,12},{1,13},{2,14},{3,15},{4,8},{5,9},{6,10},{7,11},{8,4},{9,5},... | collective-permute-start | bytes 3080 | tf_op jit(solution)/shard_map/ppermute | solution.py:33
  22.6 1.1 %collective-permute-start.6 = (f32[256]{0:T(256)S(1)}, f32[256]{0:T(256)S(1)}, u32[]{:S(2)}, u32[]{:S(2)}) collective-permute-start(f32[256]{0:T(256)S(1)} %bitcast.113), channel_id=1, source_target_pairs={{0,4},{1,5},{2,6},{3,7},{4,0},{5,1},{6,2},{7,3},{8,12},{9,13},{10,... | collective-permute-start | bytes 3080 | tf_op jit(solution)/shard_map/ppermute | solution.py:33
  23.7 1.0 collective-permute-done.8
  24.7 2.0 %collective-permute-done.7 = f32[256]{0:T(256)S(1)} collective-permute-done((f32[256]{0:T(256)S(1)}, f32[256]{0:T(256)S(1)}, u32[]{:S(2)}, u32[]{:S(2)}) %collective-permute-start.7) | collective-permute-done | bytes 1056 | tf_op jit(solution)/shard_map/ppermute | solution.py:33
  26.7 1.2 %back.7 = (f32[128,128]{1,0:T(8,128)S(1)}, f32[1,256]{1,0:T(1,128)S(1)}) custom-call(f32[1,256]{1,0:T(1,128)S(1)} %get-tuple-element.27.refs_0_, f32[1,256]{1,0:T(1,128)S(1)} %bitcast.131, f32[1,256]{1,0:T(1,128)S(1)} %bitcast.125, f32[1,256]{1,0:T(1,128)S(1)} %bitcast.119, f32[1,256]{1,0:T(1,128)S(1)} %get-tuple-element.28.refs_4_.refs_5_, ...), custom_call_target="tpu_custom_call" | custom-call | tf_op jit(solution)/shard_map/back/pallas_call | solution.py:189
  27.9 1.3 %collective-permute-start.11 = (f32[16384]{0:T(1024)S(1)}, f32[16384]{0:T(1024)S(1)}, u32[]{:S(2)}, u32[]{:S(2)}) collective-permute-start(f32[16384]{0:T(1024)S(1)} %bitcast.67), channel_id=1, source_target_pairs={{0,2},{1,3},{2,0},{3,1},{4,6},{5,7},{6,4},{7,5},{8,10},{9,11},{10,... | collective-permute-start | bytes 196616 | tf_op jit(solution)/shard_map/ppermute | solution.py:33
  30.1 2.3 %collective-permute-done.11 = f32[16384]{0:T(1024)S(1)} collective-permute-done((f32[16384]{0:T(1024)S(1)}, f32[16384]{0:T(1024)S(1)}, u32[]{:S(2)}, u32[]{:S(2)}) %collective-permute-start.11) | collective-permute-done | bytes 65568 | tf_op jit(solution)/shard_map/ppermute | solution.py:33
  33.1 1.3 %forward.7 = (f32[128,128]{1,0:T(8,128)S(1)}, f32[1,256]{1,0:T(1,128)S(1)}) custom-call(f32[1,6]{1,0:T(1,128)S(1)} %bitcast.92, f32[128,128]{1,0:T(8,128)S(1)} %get-tuple-element.29.refs_1_, f32[128,128]{1,0:T(8,128)S(1)} %bitcast.86, f32[128,128]{1,0:T(8,128)S(1)} %bitcast.80, f32[128,128]{1,0:T(8,128)S(1)} %bitcast.74, ...), custom_call_target="tpu_custom_call" | custom-call | tf_op jit(solution)/shard_map/forward/pallas_call | solution.py:199
  34.3 2.0 %collective-permute-start.14 = (f32[256]{0:T(256)S(1)}, f32[256]{0:T(256)S(1)}, u32[]{:S(2)}, u32[]{:S(2)}) collective-permute-start(f32[256]{0:T(256)S(1)} %bitcast.99), channel_id=1, source_target_pairs={{0,12},{1,13},{2,14},{3,15},{4,8},{5,9},{6,10},{7,11},{8,4},{9,5},... | collective-permute-start | bytes 3080 | tf_op jit(solution)/shard_map/ppermute | solution.py:33
  36.5 2.3 %collective-permute-start.12 = (f32[256]{0:T(256)S(1)}, f32[256]{0:T(256)S(1)}, u32[]{:S(2)}, u32[]{:S(2)}) collective-permute-start(f32[256]{0:T(256)S(1)} %bitcast.101), channel_id=1, source_target_pairs={{0,4},{1,5},{2,6},{3,7},{4,0},{5,1},{6,2},{7,3},{8,12},{9,13},{10,... | collective-permute-start | bytes 3080 | tf_op jit(solution)/shard_map/ppermute | solution.py:33
  38.8 1.0 collective-permute-done.14
  39.8 1.0 %collective-permute-done.13 = f32[256]{0:T(256)S(1)} collective-permute-done((f32[256]{0:T(256)S(1)}, f32[256]{0:T(256)S(1)}, u32[]{:S(2)}, u32[]{:S(2)}) %collective-permute-start.13) | collective-permute-done | bytes 1056 | tf_op jit(solution)/shard_map/ppermute | solution.py:33
  40.8 1.2 %back.8 = (f32[128,128]{1,0:T(8,128)S(1)}, f32[1,256]{1,0:T(1,128)S(1)}) custom-call(f32[1,256]{1,0:T(1,128)S(1)} %get-tuple-element.31.refs_0_, f32[1,256]{1,0:T(1,128)S(1)} %bitcast.126, f32[1,256]{1,0:T(1,128)S(1)} %bitcast.120, f32[1,256]{1,0:T(1,128)S(1)} %bitcast.114, f32[1,256]{1,0:T(1,128)S(1)} %get-tuple-element.28.refs_4_.refs_5_, ...), custom_call_target="tpu_custom_call" | custom-call | tf_op jit(solution)/shard_map/back/pallas_call | solution.py:189
  42.0 1.4 %collective-permute-start.17 = (f32[16384]{0:T(1024)S(1)}, f32[16384]{0:T(1024)S(1)}, u32[]{:S(2)}, u32[]{:S(2)}) collective-permute-start(f32[16384]{0:T(1024)S(1)} %bitcast.58), channel_id=1, source_target_pairs={{0,2},{1,3},{2,0},{3,1},{4,6},{5,7},{6,4},{7,5},{8,10},{9,11},{10,... | collective-permute-start | bytes 196616 | tf_op jit(solution)/shard_map/ppermute | solution.py:33
  44.2 2.1 %collective-permute-done.17 = f32[16384]{0:T(1024)S(1)} collective-permute-done((f32[16384]{0:T(1024)S(1)}, f32[16384]{0:T(1024)S(1)}, u32[]{:S(2)}, u32[]{:S(2)}) %collective-permute-start.17) | collective-permute-done | bytes 65568 | tf_op jit(solution)/shard_map/ppermute | solution.py:33
  47.1 1.3 %forward.8 = (f32[128,128]{1,0:T(8,128)S(1)}, f32[1,256]{1,0:T(1,128)S(1)}) custom-call(f32[1,6]{1,0:T(1,128)S(1)} %bitcast.93, f32[128,128]{1,0:T(8,128)S(1)} %get-tuple-element.33.refs_1_, f32[128,128]{1,0:T(8,128)S(1)} %bitcast.87, f32[128,128]{1,0:T(8,128)S(1)} %bitcast.81, f32[128,128]{1,0:T(8,128)S(1)} %bitcast.75, ...), custom_call_target="tpu_custom_call" | custom-call | tf_op jit(solution)/shard_map/forward/pallas_call | solution.py:199
  48.4 2.2 %collective-permute-start.20 = (f32[256]{0:T(256)S(1)}, f32[256]{0:T(256)S(1)}, u32[]{:S(2)}, u32[]{:S(2)}) collective-permute-start(f32[256]{0:T(256)S(1)} %bitcast.102), channel_id=1, source_target_pairs={{0,12},{1,13},{2,14},{3,15},{4,8},{5,9},{6,10},{7,11},{8,4},{9,5},... | collective-permute-start | bytes 3080 | tf_op jit(solution)/shard_map/ppermute | solution.py:33
  51.5 1.3 %collective-permute-start.18 = (f32[256]{0:T(256)S(1)}, f32[256]{0:T(256)S(1)}, u32[]{:S(2)}, u32[]{:S(2)}) collective-permute-start(f32[256]{0:T(256)S(1)} %bitcast.104), channel_id=1, source_target_pairs={{0,4},{1,5},{2,6},{3,7},{4,0},{5,1},{6,2},{7,3},{8,12},{9,13},{10,... | collective-permute-start | bytes 3080 | tf_op jit(solution)/shard_map/ppermute | solution.py:33
  53.8 1.2 %collective-permute-done.19 = f32[256]{0:T(256)S(1)} collective-permute-done((f32[256]{0:T(256)S(1)}, f32[256]{0:T(256)S(1)}, u32[]{:S(2)}, u32[]{:S(2)}) %collective-permute-start.19) | collective-permute-done | bytes 1056 | tf_op jit(solution)/shard_map/ppermute | solution.py:33
  55.0 1.2 %back.9 = (f32[128,128]{1,0:T(8,128)S(1)}, f32[1,256]{1,0:T(1,128)S(1)}) custom-call(f32[1,256]{1,0:T(1,128)S(1)} %get-tuple-element.35.refs_0_, f32[1,256]{1,0:T(1,128)S(1)} %bitcast.127, f32[1,256]{1,0:T(1,128)S(1)} %bitcast.121, f32[1,256]{1,0:T(1,128)S(1)} %bitcast.115, f32[1,256]{1,0:T(1,128)S(1)} %get-tuple-element.28.refs_4_.refs_5_, ...), custom_call_target="tpu_custom_call" | custom-call | tf_op jit(solution)/shard_map/back/pallas_call | solution.py:189
  56.2 1.5 %collective-permute-start.23 = (f32[16384]{0:T(1024)S(1)}, f32[16384]{0:T(1024)S(1)}, u32[]{:S(2)}, u32[]{:S(2)}) collective-permute-start(f32[16384]{0:T(1024)S(1)} %bitcast.61), channel_id=1, source_target_pairs={{0,2},{1,3},{2,0},{3,1},{4,6},{5,7},{6,4},{7,5},{8,10},{9,11},{10,... | collective-permute-start | bytes 196616 | tf_op jit(solution)/shard_map/ppermute | solution.py:33
  58.4 2.1 %collective-permute-done.23 = f32[16384]{0:T(1024)S(1)} collective-permute-done((f32[16384]{0:T(1024)S(1)}, f32[16384]{0:T(1024)S(1)}, u32[]{:S(2)}, u32[]{:S(2)}) %collective-permute-start.23) | collective-permute-done | bytes 65568 | tf_op jit(solution)/shard_map/ppermute | solution.py:33
  61.4 1.3 %forward.9 = (f32[128,128]{1,0:T(8,128)S(1)}, f32[1,256]{1,0:T(1,128)S(1)}) custom-call(f32[1,6]{1,0:T(1,128)S(1)} %bitcast.94, f32[128,128]{1,0:T(8,128)S(1)} %get-tuple-element.37.refs_1_, f32[128,128]{1,0:T(8,128)S(1)} %bitcast.88, f32[128,128]{1,0:T(8,128)S(1)} %bitcast.82, f32[128,128]{1,0:T(8,128)S(1)} %bitcast.76, ...), custom_call_target="tpu_custom_call" | custom-call | tf_op jit(solution)/shard_map/forward/pallas_call | solution.py:199
  62.7 2.0 %collective-permute-start.26 = (f32[256]{0:T(256)S(1)}, f32[256]{0:T(256)S(1)}, u32[]{:S(2)}, u32[]{:S(2)}) collective-permute-start(f32[256]{0:T(256)S(1)} %bitcast.105), channel_id=1, source_target_pairs={{0,12},{1,13},{2,14},{3,15},{4,8},{5,9},{6,10},{7,11},{8,4},{9,5},... | collective-permute-start | bytes 3080 | tf_op jit(solution)/shard_map/ppermute | solution.py:33
  65.6 1.6 %collective-permute-start.24 = (f32[256]{0:T(256)S(1)}, f32[256]{0:T(256)S(1)}, u32[]{:S(2)}, u32[]{:S(2)}) collective-permute-start(f32[256]{0:T(256)S(1)} %bitcast.107), channel_id=1, source_target_pairs={{0,4},{1,5},{2,6},{3,7},{4,0},{5,1},{6,2},{7,3},{8,12},{9,13},{10,... | collective-permute-start | bytes 3080 | tf_op jit(solution)/shard_map/ppermute | solution.py:33
  67.2 1.0 collective-permute-done.26
  68.2 1.0 %collective-permute-done.25 = f32[256]{0:T(256)S(1)} collective-permute-done((f32[256]{0:T(256)S(1)}, f32[256]{0:T(256)S(1)}, u32[]{:S(2)}, u32[]{:S(2)}) %collective-permute-start.25) | collective-permute-done | bytes 1056 | tf_op jit(solution)/shard_map/ppermute | solution.py:33
  69.2 1.2 %back.10 = (f32[128,128]{1,0:T(8,128)S(1)}, f32[1,256]{1,0:T(1,128)S(1)}) custom-call(f32[1,256]{1,0:T(1,128)S(1)} %get-tuple-element.39.refs_0_, f32[1,256]{1,0:T(1,128)S(1)} %bitcast.128, f32[1,256]{1,0:T(1,128)S(1)} %bitcast.122, f32[1,256]{1,0:T(1,128)S(1)} %bitcast.116, f32[1,256]{1,0:T(1,128)S(1)} %get-tuple-element.28.refs_4_.refs_5_, ...), custom_call_target="tpu_custom_call" | custom-call | tf_op jit(solution)/shard_map/back/pallas_call | solution.py:189
  70.4 1.3 %collective-permute-start.29 = (f32[16384]{0:T(1024)S(1)}, f32[16384]{0:T(1024)S(1)}, u32[]{:S(2)}, u32[]{:S(2)}) collective-permute-start(f32[16384]{0:T(1024)S(1)} %bitcast.64), channel_id=1, source_target_pairs={{0,2},{1,3},{2,0},{3,1},{4,6},{5,7},{6,4},{7,5},{8,10},{9,11},{10,... | collective-permute-start | bytes 196616 | tf_op jit(solution)/shard_map/ppermute | solution.py:33
  72.6 2.1 %collective-permute-done.29 = f32[16384]{0:T(1024)S(1)} collective-permute-done((f32[16384]{0:T(1024)S(1)}, f32[16384]{0:T(1024)S(1)}, u32[]{:S(2)}, u32[]{:S(2)}) %collective-permute-start.29) | collective-permute-done | bytes 65568 | tf_op jit(solution)/shard_map/ppermute | solution.py:33
  75.4 1.3 %forward.10 = (f32[128,128]{1,0:T(8,128)S(1)}, f32[1,256]{1,0:T(1,128)S(1)}) custom-call(f32[1,6]{1,0:T(1,128)S(1)} %bitcast.95, f32[128,128]{1,0:T(8,128)S(1)} %get-tuple-element.41.refs_1_, f32[128,128]{1,0:T(8,128)S(1)} %bitcast.89, f32[128,128]{1,0:T(8,128)S(1)} %bitcast.83, f32[128,128]{1,0:T(8,128)S(1)} %bitcast.77, ...), custom_call_target="tpu_custom_call" | custom-call | tf_op jit(solution)/shard_map/forward/pallas_call | solution.py:199
  76.7 2.2 %collective-permute-start.32 = (f32[256]{0:T(256)S(1)}, f32[256]{0:T(256)S(1)}, u32[]{:S(2)}, u32[]{:S(2)}) collective-permute-start(f32[256]{0:T(256)S(1)} %bitcast.108), channel_id=1, source_target_pairs={{0,12},{1,13},{2,14},{3,15},{4,8},{5,9},{6,10},{7,11},{8,4},{9,5},... | collective-permute-start | bytes 3080 | tf_op jit(solution)/shard_map/ppermute | solution.py:33
  79.8 1.3 %collective-permute-start.30 = (f32[256]{0:T(256)S(1)}, f32[256]{0:T(256)S(1)}, u32[]{:S(2)}, u32[]{:S(2)}) collective-permute-start(f32[256]{0:T(256)S(1)} %bitcast.110), channel_id=1, source_target_pairs={{0,4},{1,5},{2,6},{3,7},{4,0},{5,1},{6,2},{7,3},{8,12},{9,13},{10,... | collective-permute-start | bytes 3080 | tf_op jit(solution)/shard_map/ppermute | solution.py:33
  82.1 1.2 %collective-permute-done.31 = f32[256]{0:T(256)S(1)} collective-permute-done((f32[256]{0:T(256)S(1)}, f32[256]{0:T(256)S(1)}, u32[]{:S(2)}, u32[]{:S(2)}) %collective-permute-start.31) | collective-permute-done | bytes 1056 | tf_op jit(solution)/shard_map/ppermute | solution.py:33
  83.4 1.2 %back.11 = (f32[128,128]{1,0:T(8,128)S(1)}, f32[1,256]{1,0:T(1,128)S(1)}) custom-call(f32[1,256]{1,0:T(1,128)S(1)} %get-tuple-element.43.refs_0_, f32[1,256]{1,0:T(1,128)S(1)} %bitcast.129, f32[1,256]{1,0:T(1,128)S(1)} %bitcast.123, f32[1,256]{1,0:T(1,128)S(1)} %bitcast.117, f32[1,256]{1,0:T(1,128)S(1)} %get-tuple-element.28.refs_4_.refs_5_, ...), custom_call_target="tpu_custom_call" | custom-call | tf_op jit(solution)/shard_map/back/pallas_call | solution.py:189
  84.6 1.5 %collective-permute-start.35 = (f32[16384]{0:T(1024)S(1)}, f32[16384]{0:T(1024)S(1)}, u32[]{:S(2)}, u32[]{:S(2)}) collective-permute-start(f32[16384]{0:T(1024)S(1)} %bitcast.55), channel_id=1, source_target_pairs={{0,2},{1,3},{2,0},{3,1},{4,6},{5,7},{6,4},{7,5},{8,10},{9,11},{10,... | collective-permute-start | bytes 196616 | tf_op jit(solution)/shard_map/ppermute | solution.py:33
  86.8 2.1 %collective-permute-done.35 = f32[16384]{0:T(1024)S(1)} collective-permute-done((f32[16384]{0:T(1024)S(1)}, f32[16384]{0:T(1024)S(1)}, u32[]{:S(2)}, u32[]{:S(2)}) %collective-permute-start.35) | collective-permute-done | bytes 65568 | tf_op jit(solution)/shard_map/ppermute | solution.py:33
  89.8 1.3 %forward.11 = (f32[128,128]{1,0:T(8,128)S(1)}, f32[1,256]{1,0:T(1,128)S(1)}) custom-call(f32[1,6]{1,0:T(1,128)S(1)} %bitcast.96, f32[128,128]{1,0:T(8,128)S(1)} %get-tuple-element.45.refs_1_, f32[128,128]{1,0:T(8,128)S(1)} %bitcast.85, f32[128,128]{1,0:T(8,128)S(1)} %bitcast.79, f32[128,128]{1,0:T(8,128)S(1)} %bitcast.73, ...), custom_call_target="tpu_custom_call" | custom-call | tf_op jit(solution)/shard_map/forward/pallas_call | solution.py:199
  91.1 2.0 %collective-permute-start.38 = (f32[256]{0:T(256)S(1)}, f32[256]{0:T(256)S(1)}, u32[]{:S(2)}, u32[]{:S(2)}) collective-permute-start(f32[256]{0:T(256)S(1)} %bitcast.132), channel_id=1, source_target_pairs={{0,12},{1,13},{2,14},{3,15},{4,8},{5,9},{6,10},{7,11},{8,4},{9,5},... | collective-permute-start | bytes 3080 | tf_op jit(solution)/shard_map/ppermute | solution.py:33
  93.9 1.6 %collective-permute-start.36 = (f32[256]{0:T(256)S(1)}, f32[256]{0:T(256)S(1)}, u32[]{:S(2)}, u32[]{:S(2)}) collective-permute-start(f32[256]{0:T(256)S(1)} %bitcast.134), channel_id=1, source_target_pairs={{0,4},{1,5},{2,6},{3,7},{4,0},{5,1},{6,2},{7,3},{8,12},{9,13},{10,... | collective-permute-start | bytes 3080 | tf_op jit(solution)/shard_map/ppermute | solution.py:33
  96.5 1.0 %collective-permute-done.37 = f32[256]{0:T(256)S(1)} collective-permute-done((f32[256]{0:T(256)S(1)}, f32[256]{0:T(256)S(1)}, u32[]{:S(2)}, u32[]{:S(2)}) %collective-permute-start.37) | collective-permute-done | bytes 1056 | tf_op jit(solution)/shard_map/ppermute | solution.py:33
  (50 shorter events, 18.6 us)
Async XLA Ops:
  1.4 10.2 %collective-permute-start.2 = (f32[256]{0:T(256)S(1)}, f32[256]{0:T(256)S(1)}, u32[]{:S(2)}, u32[]{:S(2)}) collective-permute-start(f32[256]{0:T(256)S(1)} %concatenate.3), channel_id=1, source_target_pairs={{0,8},{1,9},{2,10},{3,11},{4,12},{5,13},{6,14},{7,15},{8,0},{9,1},... | collective-permute-start | bytes 3080 | tf_op jit(solution)/shard_map/ppermute | solution.py:33
  5.4 6.2 %collective-permute-start.1 = (f32[256]{0:T(256)S(1)}, f32[256]{0:T(256)S(1)}, u32[]{:S(2)}, u32[]{:S(2)}) collective-permute-start(f32[256]{0:T(256)S(1)} %concatenate.3), channel_id=1, source_target_pairs={{0,12},{1,13},{2,14},{3,15},{4,8},{5,9},{6,10},{7,11},{8,4},{9,5},... | collective-permute-start | bytes 3080 | tf_op jit(solution)/shard_map/ppermute | solution.py:33
  6.8 4.9 %collective-permute-start = (f32[256]{0:T(256)S(1)}, f32[256]{0:T(256)S(1)}, u32[]{:S(2)}, u32[]{:S(2)}) collective-permute-start(f32[256]{0:T(256)S(1)} %concatenate.3), channel_id=1, source_target_pairs={{0,4},{1,5},{2,6},{3,7},{4,0},{5,1},{6,2},{7,3},{8,12},{9,13},{10,... | collective-permute-start | bytes 3080 | tf_op jit(solution)/shard_map/ppermute | solution.py:33
  11.6 6.4 %copy-start = (f32[6]{0:T(128)S(1)}, f32[6]{0:T(128)}, u32[]{:S(2)}) copy-start(f32[6]{0:T(128)} %param.5) | copy-start | bytes 76
  12.7 4.3 %collective-permute-start.5 = (f32[16384]{0:T(1024)S(1)}, f32[16384]{0:T(1024)S(1)}, u32[]{:S(2)}, u32[]{:S(2)}) collective-permute-start(f32[16384]{0:T(1024)S(1)} %bitcast.70), channel_id=1, source_target_pairs={{0,2},{1,3},{2,0},{3,1},{4,6},{5,7},{6,4},{7,5},{8,10},{9,11},{10,... | collective-permute-start | bytes 196616 | tf_op jit(solution)/shard_map/ppermute | solution.py:33
  14.2 2.8 %collective-permute-start.4 = (f32[16384]{0:T(1024)S(1)}, f32[16384]{0:T(1024)S(1)}, u32[]{:S(2)}, u32[]{:S(2)}) collective-permute-start(f32[16384]{0:T(1024)S(1)} %bitcast.71), channel_id=1, source_target_pairs={{0,1},{1,0},{2,3},{3,2},{4,5},{5,4},{6,7},{7,6},{8,9},{9,8},{10,11... | collective-permute-start | bytes 196616 | tf_op jit(solution)/shard_map/ppermute | solution.py:33
  14.3 3.7 %collective-permute-start.3 = (f32[16384]{0:T(1024)S(1)}, f32[16384]{0:T(1024)S(1)}, u32[]{:S(2)}, u32[]{:S(2)}) collective-permute-start(f32[16384]{0:T(1024)S(1)} %bitcast.72), channel_id=1, source_target_pairs={{0,3},{1,2},{2,1},{3,0},{4,7},{5,6},{6,5},{7,4},{8,11},{9,10},{10,... | collective-permute-start | bytes 196616 | tf_op jit(solution)/shard_map/ppermute | solution.py:33
  19.3 5.4 %collective-permute-start.8 = (f32[256]{0:T(256)S(1)}, f32[256]{0:T(256)S(1)}, u32[]{:S(2)}, u32[]{:S(2)}) collective-permute-start(f32[256]{0:T(256)S(1)} %bitcast.111), channel_id=1, source_target_pairs={{0,12},{1,13},{2,14},{3,15},{4,8},{5,9},{6,10},{7,11},{8,4},{9,5},... | collective-permute-start | bytes 3080 | tf_op jit(solution)/shard_map/ppermute | solution.py:33
  22.3 4.5 %collective-permute-start.7 = (f32[256]{0:T(256)S(1)}, f32[256]{0:T(256)S(1)}, u32[]{:S(2)}, u32[]{:S(2)}) collective-permute-start(f32[256]{0:T(256)S(1)} %bitcast.112), channel_id=1, source_target_pairs={{0,8},{1,9},{2,10},{3,11},{4,12},{5,13},{6,14},{7,15},{8,0},{9,1},... | collective-permute-start | bytes 3080 | tf_op jit(solution)/shard_map/ppermute | solution.py:33
  22.6 4.1 %collective-permute-start.6 = (f32[256]{0:T(256)S(1)}, f32[256]{0:T(256)S(1)}, u32[]{:S(2)}, u32[]{:S(2)}) collective-permute-start(f32[256]{0:T(256)S(1)} %bitcast.113), channel_id=1, source_target_pairs={{0,4},{1,5},{2,6},{3,7},{4,0},{5,1},{6,2},{7,3},{8,12},{9,13},{10,... | collective-permute-start | bytes 3080 | tf_op jit(solution)/shard_map/ppermute | solution.py:33
  27.9 4.5 %collective-permute-start.11 = (f32[16384]{0:T(1024)S(1)}, f32[16384]{0:T(1024)S(1)}, u32[]{:S(2)}, u32[]{:S(2)}) collective-permute-start(f32[16384]{0:T(1024)S(1)} %bitcast.67), channel_id=1, source_target_pairs={{0,2},{1,3},{2,0},{3,1},{4,6},{5,7},{6,4},{7,5},{8,10},{9,11},{10,... | collective-permute-start | bytes 196616 | tf_op jit(solution)/shard_map/ppermute | solution.py:33
  29.2 3.2 %collective-permute-start.10 = (f32[16384]{0:T(1024)S(1)}, f32[16384]{0:T(1024)S(1)}, u32[]{:S(2)}, u32[]{:S(2)}) collective-permute-start(f32[16384]{0:T(1024)S(1)} %bitcast.68), channel_id=1, source_target_pairs={{0,1},{1,0},{2,3},{3,2},{4,5},{5,4},{6,7},{7,6},{8,9},{9,8},{10,11... | collective-permute-start | bytes 196616 | tf_op jit(solution)/shard_map/ppermute | solution.py:33
  29.2 3.9 %collective-permute-start.9 = (f32[16384]{0:T(1024)S(1)}, f32[16384]{0:T(1024)S(1)}, u32[]{:S(2)}, u32[]{:S(2)}) collective-permute-start(f32[16384]{0:T(1024)S(1)} %bitcast.69), channel_id=1, source_target_pairs={{0,3},{1,2},{2,1},{3,0},{4,7},{5,6},{6,5},{7,4},{8,11},{9,10},{10,... | collective-permute-start | bytes 196616 | tf_op jit(solution)/shard_map/ppermute | solution.py:33
  34.3 5.5 %collective-permute-start.14 = (f32[256]{0:T(256)S(1)}, f32[256]{0:T(256)S(1)}, u32[]{:S(2)}, u32[]{:S(2)}) collective-permute-start(f32[256]{0:T(256)S(1)} %bitcast.99), channel_id=1, source_target_pairs={{0,12},{1,13},{2,14},{3,15},{4,8},{5,9},{6,10},{7,11},{8,4},{9,5},... | collective-permute-start | bytes 3080 | tf_op jit(solution)/shard_map/ppermute | solution.py:33
  36.3 4.5 %collective-permute-start.13 = (f32[256]{0:T(256)S(1)}, f32[256]{0:T(256)S(1)}, u32[]{:S(2)}, u32[]{:S(2)}) collective-permute-start(f32[256]{0:T(256)S(1)} %bitcast.100), channel_id=1, source_target_pairs={{0,8},{1,9},{2,10},{3,11},{4,12},{5,13},{6,14},{7,15},{8,0},{9,1},... | collective-permute-start | bytes 3080 | tf_op jit(solution)/shard_map/ppermute | solution.py:33
  36.5 4.3 %collective-permute-start.12 = (f32[256]{0:T(256)S(1)}, f32[256]{0:T(256)S(1)}, u32[]{:S(2)}, u32[]{:S(2)}) collective-permute-start(f32[256]{0:T(256)S(1)} %bitcast.101), channel_id=1, source_target_pairs={{0,4},{1,5},{2,6},{3,7},{4,0},{5,1},{6,2},{7,3},{8,12},{9,13},{10,... | collective-permute-start | bytes 3080 | tf_op jit(solution)/shard_map/ppermute | solution.py:33
  42.0 4.3 %collective-permute-start.17 = (f32[16384]{0:T(1024)S(1)}, f32[16384]{0:T(1024)S(1)}, u32[]{:S(2)}, u32[]{:S(2)}) collective-permute-start(f32[16384]{0:T(1024)S(1)} %bitcast.58), channel_id=1, source_target_pairs={{0,2},{1,3},{2,0},{3,1},{4,6},{5,7},{6,4},{7,5},{8,10},{9,11},{10,... | collective-permute-start | bytes 196616 | tf_op jit(solution)/shard_map/ppermute | solution.py:33
  43.4 3.0 %collective-permute-start.16 = (f32[16384]{0:T(1024)S(1)}, f32[16384]{0:T(1024)S(1)}, u32[]{:S(2)}, u32[]{:S(2)}) collective-permute-start(f32[16384]{0:T(1024)S(1)} %bitcast.59), channel_id=1, source_target_pairs={{0,1},{1,0},{2,3},{3,2},{4,5},{5,4},{6,7},{7,6},{8,9},{9,8},{10,11... | collective-permute-start | bytes 196616 | tf_op jit(solution)/shard_map/ppermute | solution.py:33
  43.4 3.7 %collective-permute-start.15 = (f32[16384]{0:T(1024)S(1)}, f32[16384]{0:T(1024)S(1)}, u32[]{:S(2)}, u32[]{:S(2)}) collective-permute-start(f32[16384]{0:T(1024)S(1)} %bitcast.60), channel_id=1, source_target_pairs={{0,3},{1,2},{2,1},{3,0},{4,7},{5,6},{6,5},{7,4},{8,11},{9,10},{10,... | collective-permute-start | bytes 196616 | tf_op jit(solution)/shard_map/ppermute | solution.py:33
  48.4 5.4 %collective-permute-start.20 = (f32[256]{0:T(256)S(1)}, f32[256]{0:T(256)S(1)}, u32[]{:S(2)}, u32[]{:S(2)}) collective-permute-start(f32[256]{0:T(256)S(1)} %bitcast.102), channel_id=1, source_target_pairs={{0,12},{1,13},{2,14},{3,15},{4,8},{5,9},{6,10},{7,11},{8,4},{9,5},... | collective-permute-start | bytes 3080 | tf_op jit(solution)/shard_map/ppermute | solution.py:33
  50.6 4.5 %collective-permute-start.19 = (f32[256]{0:T(256)S(1)}, f32[256]{0:T(256)S(1)}, u32[]{:S(2)}, u32[]{:S(2)}) collective-permute-start(f32[256]{0:T(256)S(1)} %bitcast.103), channel_id=1, source_target_pairs={{0,8},{1,9},{2,10},{3,11},{4,12},{5,13},{6,14},{7,15},{8,0},{9,1},... | collective-permute-start | bytes 3080 | tf_op jit(solution)/shard_map/ppermute | solution.py:33
  51.5 3.6 %collective-permute-start.18 = (f32[256]{0:T(256)S(1)}, f32[256]{0:T(256)S(1)}, u32[]{:S(2)}, u32[]{:S(2)}) collective-permute-start(f32[256]{0:T(256)S(1)} %bitcast.104), channel_id=1, source_target_pairs={{0,4},{1,5},{2,6},{3,7},{4,0},{5,1},{6,2},{7,3},{8,12},{9,13},{10,... | collective-permute-start | bytes 3080 | tf_op jit(solution)/shard_map/ppermute | solution.py:33
  56.2 4.3 %collective-permute-start.23 = (f32[16384]{0:T(1024)S(1)}, f32[16384]{0:T(1024)S(1)}, u32[]{:S(2)}, u32[]{:S(2)}) collective-permute-start(f32[16384]{0:T(1024)S(1)} %bitcast.61), channel_id=1, source_target_pairs={{0,2},{1,3},{2,0},{3,1},{4,6},{5,7},{6,4},{7,5},{8,10},{9,11},{10,... | collective-permute-start | bytes 196616 | tf_op jit(solution)/shard_map/ppermute | solution.py:33
  57.7 2.9 %collective-permute-start.22 = (f32[16384]{0:T(1024)S(1)}, f32[16384]{0:T(1024)S(1)}, u32[]{:S(2)}, u32[]{:S(2)}) collective-permute-start(f32[16384]{0:T(1024)S(1)} %bitcast.62), channel_id=1, source_target_pairs={{0,1},{1,0},{2,3},{3,2},{4,5},{5,4},{6,7},{7,6},{8,9},{9,8},{10,11... | collective-permute-start | bytes 196616 | tf_op jit(solution)/shard_map/ppermute | solution.py:33
  57.7 3.7 %collective-permute-start.21 = (f32[16384]{0:T(1024)S(1)}, f32[16384]{0:T(1024)S(1)}, u32[]{:S(2)}, u32[]{:S(2)}) collective-permute-start(f32[16384]{0:T(1024)S(1)} %bitcast.63), channel_id=1, source_target_pairs={{0,3},{1,2},{2,1},{3,0},{4,7},{5,6},{6,5},{7,4},{8,11},{9,10},{10,... | collective-permute-start | bytes 196616 | tf_op jit(solution)/shard_map/ppermute | solution.py:33
  62.7 5.4 %collective-permute-start.26 = (f32[256]{0:T(256)S(1)}, f32[256]{0:T(256)S(1)}, u32[]{:S(2)}, u32[]{:S(2)}) collective-permute-start(f32[256]{0:T(256)S(1)} %bitcast.105), channel_id=1, source_target_pairs={{0,12},{1,13},{2,14},{3,15},{4,8},{5,9},{6,10},{7,11},{8,4},{9,5},... | collective-permute-start | bytes 3080 | tf_op jit(solution)/shard_map/ppermute | solution.py:33
  64.7 4.5 %collective-permute-start.25 = (f32[256]{0:T(256)S(1)}, f32[256]{0:T(256)S(1)}, u32[]{:S(2)}, u32[]{:S(2)}) collective-permute-start(f32[256]{0:T(256)S(1)} %bitcast.106), channel_id=1, source_target_pairs={{0,8},{1,9},{2,10},{3,11},{4,12},{5,13},{6,14},{7,15},{8,0},{9,1},... | collective-permute-start | bytes 3080 | tf_op jit(solution)/shard_map/ppermute | solution.py:33
  65.6 3.6 %collective-permute-start.24 = (f32[256]{0:T(256)S(1)}, f32[256]{0:T(256)S(1)}, u32[]{:S(2)}, u32[]{:S(2)}) collective-permute-start(f32[256]{0:T(256)S(1)} %bitcast.107), channel_id=1, source_target_pairs={{0,4},{1,5},{2,6},{3,7},{4,0},{5,1},{6,2},{7,3},{8,12},{9,13},{10,... | collective-permute-start | bytes 3080 | tf_op jit(solution)/shard_map/ppermute | solution.py:33
  70.4 4.3 %collective-permute-start.29 = (f32[16384]{0:T(1024)S(1)}, f32[16384]{0:T(1024)S(1)}, u32[]{:S(2)}, u32[]{:S(2)}) collective-permute-start(f32[16384]{0:T(1024)S(1)} %bitcast.64), channel_id=1, source_target_pairs={{0,2},{1,3},{2,0},{3,1},{4,6},{5,7},{6,4},{7,5},{8,10},{9,11},{10,... | collective-permute-start | bytes 196616 | tf_op jit(solution)/shard_map/ppermute | solution.py:33
  71.7 3.0 %collective-permute-start.28 = (f32[16384]{0:T(1024)S(1)}, f32[16384]{0:T(1024)S(1)}, u32[]{:S(2)}, u32[]{:S(2)}) collective-permute-start(f32[16384]{0:T(1024)S(1)} %bitcast.65), channel_id=1, source_target_pairs={{0,1},{1,0},{2,3},{3,2},{4,5},{5,4},{6,7},{7,6},{8,9},{9,8},{10,11... | collective-permute-start | bytes 196616 | tf_op jit(solution)/shard_map/ppermute | solution.py:33
  71.7 3.7 %collective-permute-start.27 = (f32[16384]{0:T(1024)S(1)}, f32[16384]{0:T(1024)S(1)}, u32[]{:S(2)}, u32[]{:S(2)}) collective-permute-start(f32[16384]{0:T(1024)S(1)} %bitcast.66), channel_id=1, source_target_pairs={{0,3},{1,2},{2,1},{3,0},{4,7},{5,6},{6,5},{7,4},{8,11},{9,10},{10,... | collective-permute-start | bytes 196616 | tf_op jit(solution)/shard_map/ppermute | solution.py:33
  76.7 5.4 %collective-permute-start.32 = (f32[256]{0:T(256)S(1)}, f32[256]{0:T(256)S(1)}, u32[]{:S(2)}, u32[]{:S(2)}) collective-permute-start(f32[256]{0:T(256)S(1)} %bitcast.108), channel_id=1, source_target_pairs={{0,12},{1,13},{2,14},{3,15},{4,8},{5,9},{6,10},{7,11},{8,4},{9,5},... | collective-permute-start | bytes 3080 | tf_op jit(solution)/shard_map/ppermute | solution.py:33
  78.9 4.5 %collective-permute-start.31 = (f32[256]{0:T(256)S(1)}, f32[256]{0:T(256)S(1)}, u32[]{:S(2)}, u32[]{:S(2)}) collective-permute-start(f32[256]{0:T(256)S(1)} %bitcast.109), channel_id=1, source_target_pairs={{0,8},{1,9},{2,10},{3,11},{4,12},{5,13},{6,14},{7,15},{8,0},{9,1},... | collective-permute-start | bytes 3080 | tf_op jit(solution)/shard_map/ppermute | solution.py:33
  79.8 3.6 %collective-permute-start.30 = (f32[256]{0:T(256)S(1)}, f32[256]{0:T(256)S(1)}, u32[]{:S(2)}, u32[]{:S(2)}) collective-permute-start(f32[256]{0:T(256)S(1)} %bitcast.110), channel_id=1, source_target_pairs={{0,4},{1,5},{2,6},{3,7},{4,0},{5,1},{6,2},{7,3},{8,12},{9,13},{10,... | collective-permute-start | bytes 3080 | tf_op jit(solution)/shard_map/ppermute | solution.py:33
  84.6 4.3 %collective-permute-start.35 = (f32[16384]{0:T(1024)S(1)}, f32[16384]{0:T(1024)S(1)}, u32[]{:S(2)}, u32[]{:S(2)}) collective-permute-start(f32[16384]{0:T(1024)S(1)} %bitcast.55), channel_id=1, source_target_pairs={{0,2},{1,3},{2,0},{3,1},{4,6},{5,7},{6,4},{7,5},{8,10},{9,11},{10,... | collective-permute-start | bytes 196616 | tf_op jit(solution)/shard_map/ppermute | solution.py:33
  86.0 2.9 %collective-permute-start.34 = (f32[16384]{0:T(1024)S(1)}, f32[16384]{0:T(1024)S(1)}, u32[]{:S(2)}, u32[]{:S(2)}) collective-permute-start(f32[16384]{0:T(1024)S(1)} %bitcast.56), channel_id=1, source_target_pairs={{0,1},{1,0},{2,3},{3,2},{4,5},{5,4},{6,7},{7,6},{8,9},{9,8},{10,11... | collective-permute-start | bytes 196616 | tf_op jit(solution)/shard_map/ppermute | solution.py:33
  86.0 3.7 %collective-permute-start.33 = (f32[16384]{0:T(1024)S(1)}, f32[16384]{0:T(1024)S(1)}, u32[]{:S(2)}, u32[]{:S(2)}) collective-permute-start(f32[16384]{0:T(1024)S(1)} %bitcast.57), channel_id=1, source_target_pairs={{0,3},{1,2},{2,1},{3,0},{4,7},{5,6},{6,5},{7,4},{8,11},{9,10},{10,... | collective-permute-start | bytes 196616 | tf_op jit(solution)/shard_map/ppermute | solution.py:33
  91.1 5.4 %collective-permute-start.38 = (f32[256]{0:T(256)S(1)}, f32[256]{0:T(256)S(1)}, u32[]{:S(2)}, u32[]{:S(2)}) collective-permute-start(f32[256]{0:T(256)S(1)} %bitcast.132), channel_id=1, source_target_pairs={{0,12},{1,13},{2,14},{3,15},{4,8},{5,9},{6,10},{7,11},{8,4},{9,5},... | collective-permute-start | bytes 3080 | tf_op jit(solution)/shard_map/ppermute | solution.py:33
  93.0 4.5 %collective-permute-start.37 = (f32[256]{0:T(256)S(1)}, f32[256]{0:T(256)S(1)}, u32[]{:S(2)}, u32[]{:S(2)}) collective-permute-start(f32[256]{0:T(256)S(1)} %bitcast.133), channel_id=1, source_target_pairs={{0,8},{1,9},{2,10},{3,11},{4,12},{5,13},{6,14},{7,15},{8,0},{9,1},... | collective-permute-start | bytes 3080 | tf_op jit(solution)/shard_map/ppermute | solution.py:33
  93.9 3.6 %collective-permute-start.36 = (f32[256]{0:T(256)S(1)}, f32[256]{0:T(256)S(1)}, u32[]{:S(2)}, u32[]{:S(2)}) collective-permute-start(f32[256]{0:T(256)S(1)} %bitcast.134), channel_id=1, source_target_pairs={{0,4},{1,5},{2,6},{3,7},{4,0},{5,1},{6,2},{7,3},{8,12},{9,13},{10,... | collective-permute-start | bytes 3080 | tf_op jit(solution)/shard_map/ppermute | solution.py:33
